TPU v7x, 32 devices: a whole 2x2x4 slice. The times are simulated.
32 devices in a mesh: phase: 2 (over core), space: 16 (over z, y, x).
Axes of the slice: x: 2, y: 2, z: 4, core: 2. Of those that a mesh axis runs over, the one named last changes fastest.
Arguments:
- features: bfloat16 [2, 8192, 256], P(None, 'space'), may hold values from -45 to 45
- weights: bfloat16 [2, 27, 256, 256], P('phase'), may hold values from -0.078125 to 0.078125
- conv_bias: float32 [2, 256], replicated, may hold values from -4 to 4
- rulebook: int32 [8192, 27], P('space'), may hold values from 0 to 576, as said below
- border: int32 [16, 64], P('space'), may hold values from 0 to 511, as said below
- pull_slots: int32 [16, 16, 4], P('space'), may hold values from 0 to 63
Outputs:
- section_outputs: bfloat16 [2, 2, 8192, 256], P('phase', None, 'space')
Inputs may be any that keep to these rules, and one draw needn't show every extreme that they name: `rulebook`: entries below 512 name a row of the voxel's own device, entries 512 + q * 4 + i name slot i pulled from device q, and the largest value means no neighbour; offset 27 // 2 always names the voxel itself. `border`: each device's entries are distinct rows of its own block.
All inputs are finite; a program needn't handle non-finite values.
Results may differ from a plain program's by a relative error of at most 0.0041.
Values may be sent and summed in bfloat16 or wider, within the bound.
No kernel may reach another device: no remote copies, remote signals or barrier semaphores. Data moves between devices by JAX's collectives and lax.ppermute only.
A program may use at most 64 MiB of HBM per device.

v0:
```python
import jax
import jax.numpy as jnp
from jax import lax
from jax.sharding import PartitionSpec as P


def passed_along(value, axis, steps):
    count = lax.axis_size(axis)
    initial, last = (max(0, -steps), min(count, count - steps))
    return lax.ppermute(value, axis, [(source, source + steps) for source in range(initial, last)])


def body(features, weights, conv_bias, rulebook, border, pull_slots):
    phase_index = lax.axis_index("phase")
    peer_count = lax.axis_size("space")
    rows_dev = rulebook.shape[0]
    channels = features.shape[2]
    micro = features.shape[0]
    own_border = border[0]
    wanted = pull_slots[0]
    offsets_first = rulebook.T
    kernel = weights[0]
    bias_row = jnp.take(conv_bias, phase_index, axis=0)
    received = jnp.zeros((rows_dev, channels), jnp.bfloat16)
    results = []
    for step_index in range(micro + 1):
        source = features[min(step_index, micro - 1)]
        inputs = jnp.where(phase_index == 0, source, received)
        values = inputs.astype(jnp.float32)
        mean_square = jnp.mean(values * values, axis=1, keepdims=True)
        normed = (values * lax.rsqrt(mean_square + 1e-06)).astype(jnp.bfloat16)
        border_rows = jnp.take(normed, own_border, axis=0)
        published = lax.all_gather(border_rows, "space", axis=0, tiled=True)
        positions = (
            jnp.arange(peer_count, dtype=jnp.int32)[:, None] * border_rows.shape[0] + wanted
        ).reshape(-1)
        halo_rows = jnp.take(published, positions, axis=0)
        lookup = jnp.concatenate(
            [normed, halo_rows, jnp.zeros((1, channels), jnp.bfloat16)], axis=0
        )
        picked = jnp.take(lookup, offsets_first, axis=0)
        convolved = jnp.einsum("krc,kcd->rd", picked, kernel, preferred_element_type=jnp.float32)
        result = (values + jax.nn.silu(convolved + bias_row)).astype(jnp.bfloat16)
        results.append(result)
        if step_index < micro:
            received = passed_along(result, "phase", 1)
    stacked = [
        jnp.where(phase_index == 0, results[batch_index], results[batch_index + 1])
        for batch_index in range(micro)
    ]
    return jnp.stack(stacked)[None]


def solution(mesh):
    return jax.shard_map(
        body,
        mesh=mesh,
        in_specs=(
            P(None, "space", None),
            P("phase", None, None, None),
            P(),
            P("space", None),
            P("space", None),
            P("space", None, None),
        ),
        out_specs=P("phase", None, "space", None),
        check_vma=False,
    )
```

profile of v0, /device:TPU:0, one launch (start us, length us, event | category | flops | bytes accessed | tf_op | source)
XLA Modules:
  0.0 303.4 jit_solution(663035064697330132)
XLA Ops:
  0.0 1.4 compare_and_fusion.2
  2.6 1.5 compare_and_fusion
  4.1 1.5 compare_select_fusion
  10.6 1.5 reshape.177
  12.1 1.4 pad_clamp_fusion
  13.5 1.8 fusion.52
  15.3 2.3 gather_fusion
  18.4 47.9 %all_gather.9 = bf16[1024,256]{1,0:T(8,128)(2,1)} all-gather(bf16[64,256]{1,0:T(8,128)(2,1)S(1)} %broadcast_select_fusion.5), channel_id=1, replica_groups=mesh['phase'=2,'space'=16] {'space'}, dimensions={0}, use_global_device_ids=true | all-gather | bytes 557056 | tf_op jit(solution)/shard_map/all_gather | solution.py:33
  67.6 2.5 gather_fusion.1
  71.0 1.8 maximum_maximum_fusion
  72.8 34.9 %gather_fusion.2 = bf16[13824,256]{1,0:T(8,128)(2,1)} fusion(bf16[577,256]{1,0:T(8,128)(2,1)} %maximum_maximum_fusion, s32[14336]{0:T(1024)} %pad_clamp_fusion), kind=kCustom, calls=%fused_computation.2.clone | custom fusion | bytes 14211072 | tf_op jit(solution)/shard_map/jit(_take)/gather | solution.py:41
  107.7 5.5 %fusion.53 = bf16[512,256]{1,0:T(8,128)(2,1)S(1)} fusion(bf16[1,27,256,256]{3,2,1,0:T(8,128)(2,1)S(1)} %copy-done, bf16[27,512,256]{2,1,0:T(8,128)(2,1)} %bitcast.82, pred[27,512]{1,0:T(8,128)(4,1)} %compare_and_fusion, f32[256]{0:T(256)} %bitcast.83, bf16[2,512,256]{2,1,0:T(8,128)(2,1)} %param.12, pred[]{:T(512)S(6)} %eq.2), kind=kOutput, calls=%fused_computation.47 | convolution fusion | flops 1816657920 | bytes 11155969 | tf_op jit(solution)/shard_map/krc,kcd->rd/dot_general | solution.py:42
  117.4 2.3 gather_fusion.3
  120.5 40.8 %all_gather.10 = bf16[1024,256]{1,0:T(8,128)(2,1)} all-gather(bf16[64,256]{1,0:T(8,128)(2,1)S(1)} %broadcast_select_fusion.4), channel_id=1, replica_groups=mesh['phase'=2,'space'=16] {'space'}, dimensions={0}, use_global_device_ids=true | all-gather | bytes 557056 | tf_op jit(solution)/shard_map/all_gather | solution.py:33
  161.2 2.5 gather_fusion.4
  164.6 1.8 maximum_maximum_fusion.1
  166.4 34.9 %gather_fusion.5 = bf16[13824,256]{1,0:T(8,128)(2,1)} fusion(bf16[577,256]{1,0:T(8,128)(2,1)} %maximum_maximum_fusion.1, s32[14336]{0:T(1024)} %pad_clamp_fusion), kind=kCustom, calls=%fused_computation.7.clone | custom fusion | bytes 14211072 | tf_op jit(solution)/shard_map/jit(_take)/gather | solution.py:41
  201.3 5.5 %fusion.47 = bf16[512,256]{1,0:T(8,128)(2,1)S(1)} fusion(bf16[512,256]{1,0:T(8,128)(2,1)} %copy-done.4, bf16[1,27,256,256]{3,2,1,0:T(8,128)(2,1)S(1)} %copy-done, bf16[27,512,256]{2,1,0:T(8,128)(2,1)} %bitcast.81, pred[27,512]{1,0:T(8,128)(4,1)} %compare_and_fusion, f32[256]{0:T(256)} %bitcast.84), kind=kOutput, calls=%fused_computation.41 | convolution fusion | flops 1816526848 | bytes 11155968 | tf_op jit(solution)/shard_map/krc,kcd->rd/dot_general | solution.py:42
  210.9 2.3 gather_fusion.6
  214.0 43.1 %all_gather.11 = bf16[1024,256]{1,0:T(8,128)(2,1)} all-gather(bf16[64,256]{1,0:T(8,128)(2,1)S(1)} %broadcast_select_fusion.3), channel_id=1, replica_groups=mesh['phase'=2,'space'=16] {'space'}, dimensions={0}, use_global_device_ids=true | all-gather | bytes 557056 | tf_op jit(solution)/shard_map/all_gather | solution.py:33
  257.1 2.5 gather_fusion.7
  260.4 1.8 maximum_maximum_fusion.2
  262.2 34.9 %gather_fusion.8 = bf16[13824,256]{1,0:T(8,128)(2,1)} fusion(bf16[577,256]{1,0:T(8,128)(2,1)} %maximum_maximum_fusion.2, s32[14336]{0:T(1024)} %pad_clamp_fusion), kind=kCustom, calls=%fused_computation.8.clone | custom fusion | bytes 14211072 | tf_op jit(solution)/shard_map/jit(_take)/gather | solution.py:41
  297.1 5.4 %fusion.63 = bf16[1,512,256]{2,1,0:T(8,128)(2,1)S(1)} fusion(bf16[512,256]{1,0:T(8,128)(2,1)} %copy-done.6, bf16[1,27,256,256]{3,2,1,0:T(8,128)(2,1)S(1)} %copy-done, bf16[27,512,256]{2,1,0:T(8,128)(2,1)} %bitcast.80, pred[27,512]{1,0:T(8,128)(4,1)S(1)} %copy-done.9, bf16[512,256]{1,0:T(8,128)(2,1)} %copy-done.3, f32[256]{0:T(256)} %bitcast.85, pred[]{:T(512)S(6)} %eq.2), kind=kOutput, calls=%fused_computation.50 | convolution fusion | flops 1816657920 | bytes 11418113 | tf_op jit(solution)/shard_map/krc,kcd->rd/dot_general | solution.py:42
  (53 shorter events, 21.6 us)
Async XLA Ops:
  0.0 107.7 %copy-start = (bf16[1,27,256,256]{3,2,1,0:T(8,128)(2,1)S(1)}, bf16[1,27,256,256]{3,2,1,0:T(8,128)(2,1)}, u32[]{:S(2)}) copy-start(bf16[1,27,256,256]{3,2,1,0:T(8,128)(2,1)} %param.13) | copy-start | bytes 10616836
  107.7 8.0 %copy-start.1 = (bf16[2,512,256]{2,1,0:T(8,128)(2,1)S(1)}, bf16[2,512,256]{2,1,0:T(8,128)(2,1)}, u32[]{:S(2)}) copy-start(bf16[2,512,256]{2,1,0:T(8,128)(2,1)} %param.12) | copy-start | bytes 1572868
  107.7 12.0 %copy-start.10 = (pred[64]{0:T(512)(128)(4,1)S(1)}, pred[64]{0:T(512)(128)(4,1)}, u32[]{:S(2)}) copy-start(pred[64]{0:T(512)(128)(4,1)} %compare_and_fusion.2) | copy-start | bytes 196
  113.2 2.6 copy-start.7
  113.2 2.4 collective-permute-start
  115.8 0.7 copy-start.4
  201.3 6.8 %copy-start.8 = (bf16[512,256]{1,0:T(8,128)(2,1)S(1)}, bf16[512,256]{1,0:T(8,128)(2,1)}, u32[]{:S(2)}) copy-start(bf16[512,256]{1,0:T(8,128)(2,1)} %copy-done.7) | copy-start | bytes 786436
  201.3 7.9 %copy-start.2 = (bf16[2,512,256]{2,1,0:T(8,128)(2,1)S(1)}, bf16[2,512,256]{2,1,0:T(8,128)(2,1)}, u32[]{:S(2)}) copy-start(bf16[2,512,256]{2,1,0:T(8,128)(2,1)} %param.12) | copy-start | bytes 1572868
  206.7 2.6 copy-start.6
  206.8 2.4 collective-permute-start.1
  209.4 0.7 copy-start.3
  262.2 34.9 %copy-start.9 = (pred[27,512]{1,0:T(8,128)(4,1)S(1)}, pred[27,512]{1,0:T(8,128)(4,1)}, u32[]{:S(2)}) copy-start(pred[27,512]{1,0:T(8,128)(4,1)} %compare_and_fusion) | copy-start | bytes 41476
  297.1 5.5 %copy-start.5 = (bf16[1,512,256]{2,1,0:T(8,128)(2,1)S(1)}, bf16[1,512,256]{2,1,0:T(8,128)(2,1)}, u32[]{:S(2)}) copy-start(bf16[1,512,256]{2,1,0:T(8,128)(2,1)} %select_bitcast_fusion) | copy-start | bytes 786436
where the time goes:
time: 308 us; the launch traced here: 303 us
  blocking collectives  132 us (43%)
  local copies, waits for them, and re-layouts  125 us (41%)
  other arithmetic  26.4 us (9%)
  matrix products  16.4 us (5%)
    all_gather x3, blocking collectives, body(): published = lax.all_gather(border_rows, 'space', axis=0, tiled=True)  132 us
    gather x3, local copies, waits for them, and re-layouts, body(): picked = jnp.take(lookup, offsets_first, axis=0)  105 us
    dot_general x3, matrix products, body(): jnp.einsum('krc,kcd->rd', picked, kernel, preferred_element_type=jnp.floa...  16.4 us
    gather x3, local copies, waits for them, and re-layouts, body(): halo_rows = jnp.take(published, positions, axis=0)  7.5 us
    gather x3, local copies, waits for them, and re-layouts, body(): border_rows = jnp.take(normed, own_border, axis=0)  6.75 us
  transfers between devices with their start and end apart: 2, of which 2 were waited for; matrix products, arithmetic and copies ran while one was open for 0% of the time, Pallas kernels for 0%

commit v1 on v0

v1 whole, which is shorter than its diff:
```python
import functools

import jax
import jax.numpy as jnp
from jax import lax
from jax.experimental import pallas as pl
from jax.experimental.pallas import tpu as pltpu
from jax.sharding import PartitionSpec as P

BF16 = jnp.bfloat16
F32 = jnp.float32
I32 = jnp.int32
AUX = 16
CHUNK = 3
VMEM_BYTES = 60 * 2**20


def iota(shape, dim):
    return lax.broadcasted_iota(I32, shape, dim)


def onehot(column, width):
    return (column == iota((column.shape[0], width), 1)).astype(BF16)


def dot(a, b):
    return jnp.dot(a, b, preferred_element_type=F32)


def normalise(values):
    mean_square = jnp.mean(values * values, axis=1, keepdims=True)
    return (values * lax.rsqrt(mean_square + 1e-06)).astype(BF16)


def row_to_column(row):
    n = row.shape[1]
    spread = jnp.where(iota((n, n), 0) == iota((n, n), 1), row.astype(F32), 0.0)
    return jnp.sum(spread, axis=1, keepdims=True).astype(I32)


def pick_lane(table, lane):
    kept = jnp.where(iota(table.shape, 1) == lane, table, 0.0)
    return jnp.sum(kept, axis=1, keepdims=True).astype(I32)


def slot_numbers(peers, cap):
    row = iota((peers * cap, 1), 0)
    peer = lax.div(row, cap)
    return peer, row - peer * cap


def prepare_kernel(phase_ref, features_ref, border_ref, wanted_ref, normed_ref, payload_ref, aux_ref):
    normed = normalise(features_ref[0].astype(F32))
    normed_ref[...] = normed
    peers, cap = wanted_ref.shape[1:]
    borders = border_ref.shape[1]
    stride = borders + AUX
    rows = dot(onehot(row_to_column(border_ref[...]), normed.shape[0]), normed).astype(BF16)
    aux_ref[...] = jnp.zeros_like(aux_ref)
    aux_ref[:, 0:cap] = wanted_ref[0].astype(F32)
    for peer in range(peers):
        payload_ref[peer * stride : peer * stride + borders, :] = rows
        own = jnp.broadcast_to(aux_ref[peer : peer + 1, :], (AUX, aux_ref.shape[1]))
        payload_ref[peer * stride + borders : (peer + 1) * stride, :] = own.astype(BF16)


def load_weights(section, phase_ref, own_ref, other_ref, held_ref, sems):
    offsets = held_ref.shape[0]
    chunks = [(c, min(CHUNK, offsets - c)) for c in range(0, offsets, CHUNK)]

    def copies(source):
        return [
            pltpu.make_async_copy(source.at[pl.ds(first, count)], held_ref.at[pl.ds(first, count)], sems.at[at])
            for at, (first, count) in enumerate(chunks)
        ]

    @pl.when(phase_ref[0] == section)
    def _():
        for copy in copies(own_ref):
            copy.start()

    @pl.when(phase_ref[0] != section)
    def _():
        for copy in copies(other_ref):
            copy.start()

    return chunks, [copy.wait for copy in copies(own_ref)]


def local_kernel(section, phase_ref, codes_ref, normed_ref, own_ref, other_ref, total_ref, held_ref, sems):
    chunks, waits = load_weights(section, phase_ref, own_ref, other_ref, held_ref, sems)
    rows, channels = normed_ref.shape
    normed = normed_ref[...]
    total = None
    for at, (first, count) in enumerate(chunks):
        picked = [
            dot(onehot(codes_ref[:, k : k + 1], rows), normed).astype(BF16) for k in range(first, first + count)
        ]
        waits[at]()
        matrix = held_ref[first : first + count].reshape(count * channels, channels)
        term = dot(jnp.concatenate(picked, axis=1), matrix)
        total = term if total is None else total + term
    total_ref[...] = total


def halo_term(chunks, waits, codes_ref, halo, held_ref, spread_ref):
    rows, offsets = codes_ref.shape
    channels = halo.shape[1]
    slots = halo.shape[0]
    pack = 128 // slots if slots < 128 else 1
    width = slots * pack
    groups = -(-offsets // pack)
    for k in range(offsets, groups * pack):
        spread_ref[k * slots : (k + 1) * slots, :] = jnp.zeros((slots, channels), BF16)
    lane = iota((rows, width), 1)
    pieces = []
    for group in range(groups):
        wanted = None
        for j in range(pack):
            k = group * pack + j
            code = codes_ref[:, k : k + 1] + (j * slots - rows) if k < offsets else jnp.full((rows, 1), -1, I32)
            code = jnp.broadcast_to(code, (rows, width))
            wanted = code if wanted is None else jnp.where(lane >= j * slots, code, wanted)
        pieces.append((wanted == lane).astype(BF16))
    for at, (first, count) in enumerate(chunks):
        waits[at]()
        for k in range(first, first + count):
            spread_ref[k * slots : (k + 1) * slots, :] = dot(halo, held_ref[k]).astype(BF16)
    return dot(jnp.concatenate(pieces, axis=1), spread_ref[...])


def residual(values, convolved):
    return (values + jax.nn.silu(convolved)).astype(BF16)


def encode_kernel(
    phase_ref, features_ref, total_ref, codes_ref, received_ref, border_ref, wanted_ref, bias_ref, own_ref, other_ref,
    latent_ref, normed_ref, send_ref, held_ref, spread_ref, aux_ref, sems,
):
    chunks, waits = load_weights(0, phase_ref, own_ref, other_ref, held_ref, sems)
    rows = codes_ref.shape[0]
    peers, cap = wanted_ref.shape[1:]
    borders = border_ref.shape[1]
    stride = borders + AUX
    peer, slot = slot_numbers(peers, cap)
    aux_ref[...] = jnp.zeros_like(aux_ref)
    aux_ref[:, 0:cap] = wanted_ref[0].astype(F32)
    mine = pick_lane(dot(onehot(peer, peers), aux_ref[...].astype(BF16)), slot)
    places = jnp.concatenate([peer * stride + mine, peer * stride + borders], axis=0)
    found = dot(onehot(places, peers * stride), received_ref[...])
    halo = found[: peers * cap].astype(BF16)
    theirs = pick_lane(found[peers * cap :, 0:128], slot)
    asked = pick_lane(jnp.broadcast_to(border_ref[...].astype(F32), (peers * cap, borders)), theirs)

    convolved = total_ref[...] + halo_term(chunks, waits, codes_ref, halo, held_ref, spread_ref) + bias_ref[0:1, :]
    latent = residual(features_ref[0].astype(F32), convolved)
    latent_ref[...] = latent
    normed = normalise(latent.astype(F32))
    normed_ref[...] = normed
    doubled = iota((2 * peers * cap, 1), 0)
    which = lax.div(doubled, 2)
    out = dot(onehot(asked, rows), normed).astype(BF16)
    half = out.shape[1] // 2
    pair = onehot(which, peers * cap)
    left = dot(pair, out[:, :half])
    right = dot(pair, out[:, half:])
    send_ref[...] = jnp.where(doubled - 2 * which == 0, left, right).astype(BF16)


def decode_kernel(
    phase_ref, latent_ref, total_ref, codes_ref, received_ref, bias_ref, own_ref, other_ref,
    out_ref, held_ref, spread_ref, sems,
):
    chunks, waits = load_weights(1, phase_ref, own_ref, other_ref, held_ref, sems)
    received = received_ref[...]
    slots = received.shape[0] // 2
    even = 2 * iota((slots, 1), 0)
    halves = [dot(onehot(even + j, 2 * slots), received).astype(BF16) for j in range(2)]
    halo = jnp.concatenate(halves, axis=1)
    convolved = total_ref[...] + halo_term(chunks, waits, codes_ref, halo, held_ref, spread_ref) + bias_ref[1:2, :]
    out_ref[...] = residual(latent_ref[...].astype(F32), convolved)


def body(features, weights, conv_bias, rulebook, border, pull_slots):
    phase = lax.axis_index("phase")
    micro, rows, channels = features.shape
    peers, cap = pull_slots.shape[1:]
    borders = border.shape[1]
    stride = borders + AUX
    offsets = rulebook.shape[1]
    slots = peers * cap
    pack = 128 // slots if slots < 128 else 1
    spread_rows = -(-offsets // pack) * pack * slots
    phase_row = phase.astype(I32).reshape(1)
    own = weights[0]
    swap = [(0, 1), (1, 0)]
    other = lax.ppermute(own, "phase", swap)

    whole = lambda *shape: pl.BlockSpec(shape, lambda i, p: (0,) * len(shape))
    mine = pl.BlockSpec((1, rows, channels), lambda i, p: (p[0], 0, 0))
    anywhere = pl.BlockSpec(memory_space=pl.ANY)
    block = jax.ShapeDtypeStruct((rows, channels), BF16)
    chunk_count = -(-offsets // CHUNK)
    held = [pltpu.VMEM((offsets, channels, channels), BF16)]
    spread = [pltpu.VMEM((spread_rows, channels), BF16)]
    aux = [pltpu.VMEM((peers, 128), F32)]
    sems = [pltpu.SemaphoreType.DMA((chunk_count,))]

    def call(kernel, name, in_specs, out_specs, out_shape, scratch, flops):
        return pl.pallas_call(
            kernel,
            grid_spec=pltpu.PrefetchScalarGridSpec(
                num_scalar_prefetch=1, grid=(1,), in_specs=in_specs, out_specs=out_specs, scratch_shapes=scratch
            ),
            out_shape=out_shape,
            compiler_params=pltpu.CompilerParams(vmem_limit_bytes=VMEM_BYTES),
            cost_estimate=pl.CostEstimate(flops=flops, bytes_accessed=offsets * channels * channels * 2, transcendentals=0),
            name=name,
        )

    normed, payload = call(
        prepare_kernel, "prepare",
        [mine, whole(1, borders), whole(1, peers, cap)],
        [whole(rows, channels), whole(peers * stride, channels)],
        [block, jax.ShapeDtypeStruct((peers * stride, channels), BF16)],
        [pltpu.VMEM((peers, channels), F32)], 10**8,
    )(phase_row, features, border, pull_slots)
    received = lax.all_to_all(payload, "space", 0, 0, tiled=True)

    def local(section, normed):
        return call(
            functools.partial(local_kernel, section), "local",
            [whole(rows, offsets), whole(rows, channels), anywhere, anywhere],
            whole(rows, channels), jax.ShapeDtypeStruct((rows, channels), F32),
            held + sems, 2 * offsets * rows * channels * (rows + channels),
        )(phase_row, rulebook, normed, own, other)

    total = local(0, normed)
    latent, normed, send = call(
        encode_kernel, "encode",
        [mine, whole(rows, channels), whole(rows, offsets), whole(peers * stride, channels), whole(1, borders),
         whole(1, peers, cap), whole(2, channels), anywhere, anywhere],
        [whole(rows, channels), whole(rows, channels), whole(2 * slots, channels // 2)],
        [block, block, jax.ShapeDtypeStruct((2 * slots, channels // 2), BF16)],
        held + spread + aux + sems, 10**9,
    )(phase_row, features, total, rulebook, received, border, pull_slots, conv_bias, own, other)
    received = lax.all_to_all(send, "space", 0, 0, tiled=True)
    total = local(1, normed)
    recon = call(
        decode_kernel, "decode",
        [whole(rows, channels), whole(rows, channels), whole(rows, offsets), whole(2 * slots, channels // 2),
         whole(2, channels), anywhere, anywhere],
        whole(rows, channels), block, held + spread + sems, 10**9,
    )(phase_row, latent, total, rulebook, received, conv_bias, own, other)

    latent_there = lax.ppermute(latent, "phase", [(1, 0)])
    recon_there = lax.ppermute(recon, "phase", [(0, 1)])
    return jnp.where(
        phase == 0, jnp.stack([latent, latent_there]), jnp.stack([recon_there, recon])
    )[None]


def solution(mesh):
    return jax.shard_map(
        body,
        mesh=mesh,
        in_specs=(
            P(None, "space", None),
            P("phase", None, None, None),
            P(),
            P("space", None),
            P("space", None),
            P("space", None, None),
        ),
        out_specs=P("phase", None, "space", None),
        check_vma=False,
    )
```

time: 308 us -> 67.6 us (0.22); the launches traced: 303 us -> 67 us
  blocking collectives: 132 us -> 0 us
  local copies, waits for them, and re-layouts: 125 us -> 5.38 us
  Pallas kernels: 0 us -> 36.8 us
  other arithmetic: 26.4 us -> 1.83 us
  matrix products: 16.4 us -> 0 us
  starting transfers between devices: 2.61 us -> 17.7 us
  waiting for transfers between devices: 1.51 us -> 5.27 us
    all_gather x3 -> x0, blocking collectives: 132 us -> none  [body(): published = lax.all_gather(border_rows, 'space', axis=0, tiled=True)]
    gather x9 -> x0, local copies, waits for them, and re-layouts: 119 us -> none  [the longest x3 105 us: body(): picked = jnp.take(lookup, offsets_first, axis=0)]
    pallas_call x0 -> x5, Pallas kernels: none -> 36.8 us  [the longest x2 20.9 us: local(): call(functools.partial(local_kernel, section), 'local', [whole(rows, offs...]
    dot_general x3 -> x0, matrix products: 16.4 us -> none  [body(): jnp.einsum('krc,kcd->rd', picked, kernel, preferred_element_type=jnp.floa...]
    all_to_all x0 -> x2, starting transfers between devices: none -> 12.7 us  [the longest x1 7.91 us: body(): received = lax.all_to_all(payload, 'space', 0, 0, tiled=True)]
    select_n x9 -> x1, other arithmetic: 8.36 us -> 1.83 us  [body(): jnp.where(phase == 0, jnp.stack([latent, latent_there]), jnp.stack([recon...]
    concatenate x3 -> x0, other arithmetic: 5.43 us -> none  [body(): jnp.concatenate([normed, halo_rows, jnp.zeros((1, channels), jnp.bfloat16...]
    all_to_all x0 -> x2, waiting for transfers between devices: none -> 3.94 us  [the longest x1 3.94 us: body(): received = lax.all_to_all(payload, 'space', 0, 0, tiled=True)]
  transfers between devices with their start and end apart: 2 -> 5, of which waited for: 2 -> 2; matrix products, arithmetic and copies ran while one was open for 0% -> 5% of each run, Pallas kernels for 0% -> 44%
where the time goes in v1:
time: 67.6 us; the launch traced here: 67 us
  Pallas kernels  36.8 us (54%)
  starting transfers between devices  17.7 us (26%)
  local copies, waits for them, and re-layouts  5.38 us (8%)
  waiting for transfers between devices  5.27 us (8%)
  other arithmetic  1.83 us (3%)
    pallas_call x2, Pallas kernels, local(): call(functools.partial(local_kernel, section), 'local', [whole(rows, offs...  20.9 us
    all_to_all x1, starting transfers between devices, body(): received = lax.all_to_all(payload, 'space', 0, 0, tiled=True)  7.91 us
    pallas_call x1, Pallas kernels, body(): call(encode_kernel, 'encode', [mine, whole(rows, channels), whole(rows, o...  7.29 us
    pallas_call x1, Pallas kernels, body(): call(decode_kernel, 'decode', [whole(rows, channels), whole(rows, channel...  6.44 us
    unnamed x8, local copies, waits for them, and re-layouts  5.38 us
    all_to_all x1, starting transfers between devices, body(): received = lax.all_to_all(send, 'space', 0, 0, tiled=True)  4.78 us
    all_to_all x1, waiting for transfers between devices, body(): received = lax.all_to_all(payload, 'space', 0, 0, tiled=True)  3.94 us
    ppermute x1, starting transfers between devices, body(): recon_there = lax.ppermute(recon, 'phase', [(0, 1)])  3.04 us
  transfers between devices with their start and end apart: 5, of which 2 were waited for; matrix products, arithmetic and copies ran while one was open for 5% of the time, Pallas kernels for 44%

profile of v1, /device:TPU:0, one launch (start us, length us, event | category | flops | bytes accessed | tf_op | source)
XLA Modules:
  0.0 67.0 jit_solution(15901812961641620359)
XLA Ops:
  0.0 0.5 collective-permute-start
  0.5 1.3 %copy.7.wanted_ref = s32[1,16,4]{2,1,0:T(8,128)} copy(s32[1,16,4]{1,2,0:T(4,128)} %param.11) | data formatting | bytes 512 | tf_op args[5]
  1.8 2.1 %prepare.1 = (bf16[512,256]{1,0:T(8,128)(2,1)}, bf16[1280,256]{1,0:T(8,128)(2,1)}) custom-call(s32[1]{0:T(128)} %bitcast.phase_ref, bf16[2,512,256]{2,1,0:T(8,128)(2,1)} %features_ref.3, s32[1,64]{1,0:T(1,128)} %border_ref.3, s32[1,16,4]{2,1,0:T(8,128)} %copy.7.wanted_ref), custom_call_target="tpu_custom_call" | custom-call | flops 100000000 | bytes 3538944 | tf_op jit(solution)/shard_map/prepare/pallas_call | solution.py:221
  3.9 7.9 %all-to-all-start = ((bf16[16,80,256]{2,1,0:T(8,128)(2,1)}), bf16[16,80,256]{2,1,0:T(8,128)(2,1)}, u32[]{:S(2)}, u32[]{:S(2)}) async-start(bf16[16,80,256]{2,1,0:T(8,128)(2,1)} %bitcast.17), calls=%async_computation | async-start | bytes 1310720 | tf_op jit(solution)/shard_map/all_to_all | solution.py:228
  11.8 1.7 %copy.8.codes_ref = s32[512,27]{1,0:T(8,128)} copy(s32[512,27]{0,1:T(8,128)} %param.9) | data formatting | bytes 110592 | tf_op args[3]
  13.5 0.0 collective-permute-done.other_ref
  13.5 0.0 copy-start
  13.5 1.7 %copy-done = bf16[27,256,256]{2,1,0:T(8,128)(2,1)} copy-done((bf16[27,256,256]{2,1,0:T(8,128)(2,1)}, bf16[27,256,256]{2,1,0:T(8,128)(2,1)S(1)}, u32[]{:S(2)}) %copy-start) | copy-done | bytes 3538968
  15.3 10.5 %local.2.total_ref = f32[512,256]{1,0:T(8,128)} custom-call(s32[1]{0:T(128)} %bitcast.phase_ref, s32[512,27]{1,0:T(8,128)} %copy.8.codes_ref, bf16[512,256]{1,0:T(8,128)(2,1)} %get-tuple-element.10.normed_ref, bf16[27,256,256]{2,1,0:T(8,128)(2,1)} %bitcast.11, bf16[27,256,256]{2,1,0:T(8,128)(2,1)} %copy-done), custom_call_target="tpu_custom_call" | custom-call | flops 5435817984 | bytes 3538944 | tf_op jit(solution)/shard_map/local/pallas_call | solution.py:231
  25.8 3.9 %all-to-all-done = bf16[16,80,256]{2,1,0:T(8,128)(2,1)} async-done(((bf16[16,80,256]{2,1,0:T(8,128)(2,1)}), bf16[16,80,256]{2,1,0:T(8,128)(2,1)}, u32[]{:S(2)}, u32[]{:S(2)}) %all-to-all-start) | async-done | bytes 655392 | tf_op jit(solution)/shard_map/all_to_all | solution.py:228
  29.7 7.3 %encode.1 = (bf16[512,256]{1,0:T(8,128)(2,1)}, bf16[512,256]{1,0:T(8,128)(2,1)}, bf16[128,128]{1,0:T(8,128)(2,1)}) custom-call(s32[1]{0:T(128)} %bitcast.phase_ref, bf16[2,512,256]{2,1,0:T(8,128)(2,1)} %features_ref.3, f32[512,256]{1,0:T(8,128)} %local.2.total_ref, s32[512,27]{1,0:T(8,128)} %copy.8.codes_ref, bf16[1280,256]{1,0:T(8,128)(2,1)} %bitcast.3.received_ref, ...), custom_call_target="tpu_custom_call" | custom-call | flops 1000000000 | bytes 3538944 | tf_op jit(solution)/shard_map/encode/pallas_call | solution.py:239
  37.0 4.8 %all-to-all-start.1 = ((bf16[16,8,128]{2,1,0:T(8,128)(2,1)}), bf16[16,8,128]{2,1,0:T(8,128)(2,1)S(1)}, u32[]{:S(2)}, u32[]{:S(2)}) async-start(bf16[16,8,128]{2,1,0:T(8,128)(2,1)} %bitcast.21), calls=%async_computation.1 | async-start | bytes 65536 | tf_op jit(solution)/shard_map/all_to_all | solution.py:247
  41.8 1.5 %collective-permute-start.1 = (bf16[512,256]{1,0:T(8,128)(2,1)}, bf16[512,256]{1,0:T(8,128)(2,1)S(1)}, u32[]{:S(2)}, u32[]{:S(2)}) collective-permute-start(bf16[512,256]{1,0:T(8,128)(2,1)} %get-tuple-element.12.latent_ref), channel_id=1, source_target_pairs={{16,0},{17,1},{18,2},{19,3},{20,4},{21,5},{22,6},{23,7},{24,8},{25... | collective-permute-start | bytes 786440 | tf_op jit(solution)/shard_map/ppermute | solution.py:256
  43.3 10.5 %local.3.total_ref = f32[512,256]{1,0:T(8,128)} custom-call(s32[1]{0:T(128)} %bitcast.phase_ref, s32[512,27]{1,0:T(8,128)} %copy.8.codes_ref, bf16[512,256]{1,0:T(8,128)(2,1)} %get-tuple-element.13.normed_ref, bf16[27,256,256]{2,1,0:T(8,128)(2,1)} %bitcast.13, bf16[27,256,256]{2,1,0:T(8,128)(2,1)} %copy-done), custom_call_target="tpu_custom_call" | custom-call | flops 5435817984 | bytes 3538944 | tf_op jit(solution)/shard_map/local/pallas_call | solution.py:231
  53.7 0.0 all-to-all-done.1
  53.8 0.0 copy-start.2
  53.8 0.6 copy-done.2
  54.4 0.0 copy-start.1
  54.4 6.4 %decode.1 = bf16[512,256]{1,0:T(8,128)(2,1)} custom-call(s32[1]{0:T(128)} %bitcast.phase_ref, bf16[512,256]{1,0:T(8,128)(2,1)} %get-tuple-element.12.latent_ref, f32[512,256]{1,0:T(8,128)} %local.3.total_ref, s32[512,27]{1,0:T(8,128)} %copy.8.codes_ref, bf16[128,128]{1,0:T(8,128)(2,1)} %bitcast.20, f32[2,256]{1,0:T(2,128)} %bias_ref.3, ...), custom_call_target="tpu_custom_call" | custom-call | flops 1000000000 | bytes 3538944 | tf_op jit(solution)/shard_map/decode/pallas_call | solution.py:249
  60.8 3.0 %collective-permute-start.2 = (bf16[512,256]{1,0:T(8,128)(2,1)}, bf16[512,256]{1,0:T(8,128)(2,1)S(1)}, u32[]{:S(2)}, u32[]{:S(2)}) collective-permute-start(bf16[512,256]{1,0:T(8,128)(2,1)} %decode.1), channel_id=1, source_target_pairs={{0,16},{1,17},{2,18},{3,19},{4,20},{5,21},{6,22},{7,23},{8,24},{9,... | collective-permute-start | bytes 786440 | tf_op jit(solution)/shard_map/ppermute | solution.py:257
  63.9 0.0 collective-permute-done.1
  63.9 1.3 %collective-permute-done.2 = bf16[512,256]{1,0:T(8,128)(2,1)S(1)} collective-permute-done((bf16[512,256]{1,0:T(8,128)(2,1)}, bf16[512,256]{1,0:T(8,128)(2,1)S(1)}, u32[]{:S(2)}, u32[]{:S(2)}) %collective-permute-start.2) | collective-permute-done | bytes 262176 | tf_op jit(solution)/shard_map/ppermute | solution.py:257
  65.2 0.0 copy-done.1
  65.2 1.8 %maximum_select_fusion = bf16[1,2,512,256]{3,2,1,0:T(8,128)(2,1)} fusion(bf16[1,1,512,256]{3,2,1,0:T(8,128)(2,1)S(1)} %bitcast.18, bf16[1,1,512,256]{3,2,1,0:T(8,128)(2,1)S(1)} %bitcast.15, bf16[1,1,512,256]{3,2,1,0:T(8,128)(2,1)} %bitcast.16, bf16[1,1,512,256]{3,2,1,0:T(8,128)(2,1)S(1)} %bitcast.19, pred[]{:T(512)S(6)} %eq.3), kind=kLoop, calls=%fused_computation | loop fusion | flops 786432 | bytes 1572865 | tf_op jit(solution)/shard_map/jit(_where)/select_n | solution.py:258
Async XLA Ops:
  0.0 13.5 %collective-permute-start = (bf16[27,256,256]{2,1,0:T(8,128)(2,1)}, bf16[27,256,256]{2,1,0:T(8,128)(2,1)S(1)}, u32[]{:S(2)}, u32[]{:S(2)}) collective-permute-start(bf16[27,256,256]{2,1,0:T(8,128)(2,1)} %bitcast.10), channel_id=1, source_target_pairs={{0,16},{16,0},{1,17},{17,1},{2,18},{18,2},{3,19},{19,3},{4,20},{20... | collective-permute-start | bytes 10616840 | tf_op jit(solution)/shard_map/ppermute | solution.py:197
  3.9 25.8 %all-to-all-start = ((bf16[16,80,256]{2,1,0:T(8,128)(2,1)}), bf16[16,80,256]{2,1,0:T(8,128)(2,1)}, u32[]{:S(2)}, u32[]{:S(2)}) async-start(bf16[16,80,256]{2,1,0:T(8,128)(2,1)} %bitcast.17), calls=%async_computation | async-start | bytes 1310720 | tf_op jit(solution)/shard_map/all_to_all | solution.py:228
  13.5 1.7 %copy-start = (bf16[27,256,256]{2,1,0:T(8,128)(2,1)}, bf16[27,256,256]{2,1,0:T(8,128)(2,1)S(1)}, u32[]{:S(2)}) copy-start(bf16[27,256,256]{2,1,0:T(8,128)(2,1)S(1)} %collective-permute-done.other_ref) | copy-start | bytes 10616836
  37.0 16.8 %all-to-all-start.1 = ((bf16[16,8,128]{2,1,0:T(8,128)(2,1)}), bf16[16,8,128]{2,1,0:T(8,128)(2,1)S(1)}, u32[]{:S(2)}, u32[]{:S(2)}) async-start(bf16[16,8,128]{2,1,0:T(8,128)(2,1)} %bitcast.21), calls=%async_computation.1 | async-start | bytes 65536 | tf_op jit(solution)/shard_map/all_to_all | solution.py:247
  41.8 22.1 %collective-permute-start.1 = (bf16[512,256]{1,0:T(8,128)(2,1)}, bf16[512,256]{1,0:T(8,128)(2,1)S(1)}, u32[]{:S(2)}, u32[]{:S(2)}) collective-permute-start(bf16[512,256]{1,0:T(8,128)(2,1)} %get-tuple-element.12.latent_ref), channel_id=1, source_target_pairs={{16,0},{17,1},{18,2},{19,3},{20,4},{21,5},{22,6},{23,7},{24,8},{25... | collective-permute-start | bytes 786440 | tf_op jit(solution)/shard_map/ppermute | solution.py:256
  53.8 0.6 copy-start.2
  54.4 10.8 %copy-start.1 = (bf16[512,256]{1,0:T(8,128)(2,1)S(1)}, bf16[512,256]{1,0:T(8,128)(2,1)}, u32[]{:S(2)}) copy-start(bf16[512,256]{1,0:T(8,128)(2,1)} %get-tuple-element.12.latent_ref) | copy-start | bytes 786436
  60.8 4.4 %collective-permute-start.2 = (bf16[512,256]{1,0:T(8,128)(2,1)}, bf16[512,256]{1,0:T(8,128)(2,1)S(1)}, u32[]{:S(2)}, u32[]{:S(2)}) collective-permute-start(bf16[512,256]{1,0:T(8,128)(2,1)} %decode.1), channel_id=1, source_target_pairs={{0,16},{1,17},{2,18},{3,19},{4,20},{5,21},{6,22},{7,23},{8,24},{9,... | collective-permute-start | bytes 786440 | tf_op jit(solution)/shard_map/ppermute | solution.py:257

commit v2 on v0

v2 whole, which is shorter than its diff:
```python
import functools

import jax
import jax.numpy as jnp
from jax import lax
from jax.experimental import pallas as pl
from jax.experimental.pallas import tpu as pltpu
from jax.sharding import PartitionSpec as P

BF16 = jnp.bfloat16
F32 = jnp.float32
I32 = jnp.int32
TILE = 8
CHUNK = 3
VMEM_BYTES = 24 * 2**20


def iota(shape, dim):
    return lax.broadcasted_iota(I32, shape, dim)


def onehot(column, width):
    return (column == iota((column.shape[0], width), 1)).astype(BF16)


def dot(a, b):
    return jnp.dot(a, b, preferred_element_type=F32)


def normalise(values):
    mean_square = jnp.mean(values * values, axis=1, keepdims=True)
    return (values * lax.rsqrt(mean_square + 1e-06)).astype(BF16)


def packing(slots, offsets):
    pack = 128 // slots if slots < 128 else 1
    return pack, -(-offsets // pack)


def ask_kernel(wanted_ref, ask_ref):
    cap, peers = wanted_ref.shape
    for peer in range(peers):
        column = jnp.broadcast_to(wanted_ref[:, peer : peer + 1], (cap, 128))
        for at in range(0, TILE, cap):
            ask_ref[peer * TILE + at : peer * TILE + at + cap, :] = column


def build_halo_onehot(codes_ref, halo_onehot_ref, slots):
    rows, offsets = codes_ref.shape
    pack, groups = packing(slots, offsets)
    width = slots * pack
    lane = iota((rows, width), 1)
    for group in range(groups):
        named = None
        for j in range(pack):
            k = group * pack + j
            code = codes_ref[:, k : k + 1] + (j * slots - rows) if k < offsets else jnp.full((rows, 1), -1, I32)
            code = jnp.broadcast_to(code, (rows, width))
            named = code if named is None else jnp.where(lane >= j * slots, code, named)
        halo_onehot_ref[:, group * width : (group + 1) * width] = (named == lane).astype(BF16)


def send_kernel(normed_ref, asked_ref, border_ref, send_ref):
    send_ref[...] = wanted_rows(normed_ref[...], asked_ref, border_ref)


def wanted_rows(normed, asked_ref, border_ref):
    requests, borders = asked_ref.shape[0], border_ref.shape[1]
    named = asked_ref[:, 0:1] == iota((requests, borders), 1)
    places = jnp.where(named, jnp.broadcast_to(border_ref[...].astype(F32), (requests, borders)), 0.0)
    place = jnp.sum(places, axis=1, keepdims=True).astype(I32)
    return dot(onehot(place, normed.shape[0]), normed).astype(BF16)


def local_kernel(section, phase_ref, codes_ref, normed_ref, own_ref, other_ref, total_ref):
    rows, channels = normed_ref.shape
    offsets = codes_ref.shape[1]

    def convolve(weights_ref):
        normed = normed_ref[...]
        total = None
        for first in range(0, offsets, CHUNK):
            count = min(CHUNK, offsets - first)
            picked = [
                dot(onehot(codes_ref[:, k : k + 1], rows), normed).astype(BF16) for k in range(first, first + count)
            ]
            matrix = weights_ref[first : first + count].reshape(count * channels, channels)
            term = dot(jnp.concatenate(picked, axis=1), matrix)
            total = term if total is None else total + term
        total_ref[...] = total

    pl.when(phase_ref[0] == section)(lambda: convolve(own_ref))
    pl.when(phase_ref[0] != section)(lambda: convolve(other_ref))


def halo_term(section, phase_ref, received_ref, cap, halo_onehot_ref, own_ref, other_ref, spread_ref):
    offsets, channels = own_ref.shape[:2]
    requests = received_ref.shape[0]
    slots = requests // TILE * cap
    pack, groups = packing(slots, offsets)
    row = iota((slots, 1), 0)
    peer = lax.div(row, cap)
    halo = dot(onehot(peer * TILE + row - peer * cap, requests), received_ref[...]).astype(BF16)
    for k in range(offsets, groups * pack):
        spread_ref[k * slots : (k + 1) * slots, :] = jnp.zeros((slots, channels), BF16)

    def spread(weights_ref):
        for k in range(offsets):
            spread_ref[k * slots : (k + 1) * slots, :] = dot(halo, weights_ref[k]).astype(BF16)

    pl.when(phase_ref[0] == section)(lambda: spread(own_ref))
    pl.when(phase_ref[0] != section)(lambda: spread(other_ref))
    whole = groups * pack * slots
    step = 2048 if whole > 2048 else whole
    total = None
    for first in range(0, whole, step):
        last = min(first + step, whole)
        term = dot(halo_onehot_ref[:, first:last], spread_ref[first:last, :])
        total = term if total is None else total + term
    return total


def residual(values, convolved):
    return (values + jax.nn.silu(convolved)).astype(BF16)


def encode_kernel(
    cap, phase_ref, features_ref, total_ref, received_ref, halo_onehot_ref, asked_ref, border_ref, bias_ref,
    own_ref, other_ref, latent_ref, normed_ref, send_ref, spread_ref,
):
    term = halo_term(0, phase_ref, received_ref, cap, halo_onehot_ref, own_ref, other_ref, spread_ref)
    latent = residual(features_ref[phase_ref[0]].astype(F32), total_ref[...] + term + bias_ref[0:1, :])
    latent_ref[...] = latent
    normed = normalise(latent.astype(F32))
    normed_ref[...] = normed
    send_ref[...] = wanted_rows(normed, asked_ref, border_ref)


def decode_kernel(
    cap, phase_ref, latent_ref, total_ref, received_ref, halo_onehot_ref, bias_ref, own_ref, other_ref,
    kept_ref, passed_ref, spread_ref,
):
    term = halo_term(1, phase_ref, received_ref, cap, halo_onehot_ref, own_ref, other_ref, spread_ref)
    latent = latent_ref[...]
    recon = residual(latent.astype(F32), total_ref[...] + term + bias_ref[1:2, :])
    first = phase_ref[0] == 0
    kept_ref[phase_ref[0]] = jnp.where(first, latent, recon)
    passed_ref[...] = jnp.where(first, recon, latent)


def body(features, weights, conv_bias, rulebook, border, pull_slots):
    phase = lax.axis_index("phase").astype(I32)
    micro, rows, channels = features.shape
    peers, cap = pull_slots.shape[1:]
    offsets = rulebook.shape[1]
    slots = peers * cap
    pack, groups = packing(slots, offsets)
    spread_rows = groups * pack * slots
    phase_row = phase.reshape(1)
    own = weights[0]
    swap = [(0, 1), (1, 0)]
    other = lax.ppermute(own, "phase", swap)

    vmem = pl.BlockSpec(memory_space=pltpu.VMEM)
    smem = pl.BlockSpec(memory_space=pltpu.SMEM)
    block = jax.ShapeDtypeStruct((rows, channels), BF16)
    sent = jax.ShapeDtypeStruct((peers * TILE, channels), BF16)
    spread = [pltpu.VMEM((spread_rows, channels), BF16)]

    def call(kernel, name, in_specs, out_shape, flops, scratch=()):
        single = isinstance(out_shape, jax.ShapeDtypeStruct)
        return pl.pallas_call(
            kernel,
            in_specs=in_specs,
            out_specs=vmem if single else [vmem] * len(out_shape),
            out_shape=out_shape,
            scratch_shapes=list(scratch),
            compiler_params=pltpu.CompilerParams(vmem_limit_bytes=VMEM_BYTES),
            cost_estimate=pl.CostEstimate(flops=flops, bytes_accessed=10**6, transcendentals=0),
            name=name,
        )

    def exchange(value):
        return lax.all_to_all(value, "space", 0, 0, tiled=True)

    ask = call(ask_kernel, "ask", [vmem], jax.ShapeDtypeStruct((peers * TILE, 128), I32), 10**6)(pull_slots[0].T)
    asked = exchange(ask)

    def prepare(phase_ref, features_ref, codes_ref, normed_ref, halo_onehot_ref):
        normed_ref[...] = normalise(features_ref[phase_ref[0]].astype(F32))
        build_halo_onehot(codes_ref, halo_onehot_ref, slots)

    normed, halo_onehot = call(
        prepare, "prepare", [smem, vmem, vmem],
        [block, jax.ShapeDtypeStruct((rows, spread_rows), BF16)], 10**9,
    )(phase_row, features, rulebook)
    send = call(send_kernel, "send", [vmem] * 3, sent, 10**8)(normed, asked, border)
    received = exchange(send)

    def local(section, normed):
        return call(
            functools.partial(local_kernel, section), "local", [smem] + [vmem] * 4,
            jax.ShapeDtypeStruct((rows, channels), F32), 2 * offsets * rows * channels * (rows + channels),
        )(phase_row, rulebook, normed, own, other)

    total = local(0, normed)
    latent, normed, send = call(
        functools.partial(encode_kernel, cap), "encode", [smem] + [vmem] * 9, [block, block, sent], 10**9, spread
    )(phase_row, features, total, received, halo_onehot, asked, border, conv_bias, own, other)
    received = exchange(send)
    total = local(1, normed)
    kept, passed = call(
        functools.partial(decode_kernel, cap), "decode", [smem] + [vmem] * 7,
        [jax.ShapeDtypeStruct((2, rows, channels), BF16), block], 10**9, spread,
    )(phase_row, latent, total, received, halo_onehot, conv_bias, own, other)
    got = lax.ppermute(passed, "phase", swap)
    return lax.dynamic_update_slice(kept, got[None], (1 - phase, 0, 0))[None]


def solution(mesh):
    return jax.shard_map(
        body,
        mesh=mesh,
        in_specs=(
            P(None, "space", None),
            P("phase", None, None, None),
            P(),
            P("space", None),
            P("space", None),
            P("space", None, None),
        ),
        out_specs=P("phase", None, "space", None),
        check_vma=False,
    )
```

time: 308 us -> 77.4 us (0.25); the launches traced: 303 us -> 76.5 us
  blocking collectives: 132 us -> 0 us
  local copies, waits for them, and re-layouts: 125 us -> 23.9 us
  Pallas kernels: 0 us -> 28.5 us
  other arithmetic: 26.4 us -> 0 us
  starting transfers between devices: 2.61 us -> 22.1 us
  matrix products: 16.4 us -> 0 us
    all_gather x3 -> x0, blocking collectives: 132 us -> none  [body(): published = lax.all_gather(border_rows, 'space', axis=0, tiled=True)]
    gather x9 -> x0, local copies, waits for them, and re-layouts: 119 us -> none  [the longest x3 105 us: body(): picked = jnp.take(lookup, offsets_first, axis=0)]
    pallas_call x0 -> x7, Pallas kernels: none -> 28.5 us  [the longest x2 16.8 us: local(): call(functools.partial(local_kernel, section), 'local', [smem] + [vmem] *...]
    all_to_all x0 -> x3, starting transfers between devices: none -> 21.6 us  [exchange(): return lax.all_to_all(value, 'space', 0, 0, tiled=True)]
    unnamed x23 -> x53, local copies, waits for them, and re-layouts: 2.13 us -> 23.2 us
    dot_general x3 -> x0, matrix products: 16.4 us -> none  [body(): jnp.einsum('krc,kcd->rd', picked, kernel, preferred_element_type=jnp.floa...]
    select_n x9 -> x0, other arithmetic: 8.36 us -> none  [the longest x4 3.16 us: body(): border_rows = jnp.take(normed, own_border, axis=0)]
    concatenate x3 -> x0, other arithmetic: 5.43 us -> none  [body(): jnp.concatenate([normed, halo_rows, jnp.zeros((1, channels), jnp.bfloat16...]
  transfers between devices with their start and end apart: 2 -> 5, of which waited for: 2 -> 1; matrix products, arithmetic and copies ran while one was open for 0% -> 2% of each run, Pallas kernels for 0% -> 25%
where the time goes in v2:
time: 77.4 us; the launch traced here: 76.5 us
  Pallas kernels  28.5 us (37%)
  local copies, waits for them, and re-layouts  23.9 us (31%)
  starting transfers between devices  22.1 us (29%)
  waiting for transfers between devices  1.75 us (2%)
    unnamed x53, local copies, waits for them, and re-layouts  23.2 us
    all_to_all x3, starting transfers between devices, exchange(): return lax.all_to_all(value, 'space', 0, 0, tiled=True)  21.6 us
    pallas_call x2, Pallas kernels, local(): call(functools.partial(local_kernel, section), 'local', [smem] + [vmem] *...  16.8 us
    pallas_call x1, Pallas kernels, body(): call(functools.partial(decode_kernel, cap), 'decode', [smem] + [vmem] * 7...  4.49 us
    pallas_call x1, Pallas kernels, body(): call(functools.partial(encode_kernel, cap), 'encode', [smem] + [vmem] * 9...  3.95 us
    pallas_call x1, Pallas kernels, body(): call(prepare, 'prepare', [smem, vmem, vmem], [block, jax.ShapeDtypeStruct...  2.04 us
    ppermute x1, waiting for transfers between devices, body(): got = lax.ppermute(passed, 'phase', swap)  1.74 us
  transfers between devices with their start and end apart: 5, of which 1 were waited for; matrix products, arithmetic and copies ran while one was open for 2% of the time, Pallas kernels for 25%

profile of v2, /device:TPU:0, one launch (start us, length us, event | category | flops | bytes accessed | tf_op | source)
XLA Modules:
  0.0 76.5 jit_solution(3948342929673962121)
XLA Ops:
  2.1 7.8 %all-to-all-start = ((s32[16,8,128]{2,1,0:T(8,128)}), s32[16,8,128]{2,1,0:T(8,128)}, u32[]{:S(2)}, u32[]{:S(2)}) async-start(s32[16,8,128]{2,1,0:T(8,128)} %bitcast.19), calls=%async_computation | async-start | bytes 131072 | tf_op jit(solution)/shard_map/all_to_all | solution.py:184
  9.9 1.7 %copy.8.codes_ref = s32[512,27]{1,0:T(8,128)} copy(s32[512,27]{0,1:T(8,128)} %param.9) | data formatting | bytes 110592 | tf_op args[3]
  11.6 1.0 %copy-done.4 = bf16[2,512,256]{2,1,0:T(8,128)(2,1)S(1)} copy-done((bf16[2,512,256]{2,1,0:T(8,128)(2,1)S(1)}, bf16[2,512,256]{2,1,0:T(8,128)(2,1)}, u32[]{:S(2)}) %copy-start.4) | copy-done | bytes 524312
  12.7 0.9 %copy-done.12 = s32[512,27]{1,0:T(8,128)S(1)} copy-done((s32[512,27]{1,0:T(8,128)S(1)}, s32[512,27]{1,0:T(8,128)}, u32[]{:S(2)}) %copy-start.12) | copy-done | bytes 55320
  13.6 2.0 %prepare.1 = (bf16[512,256]{1,0:T(8,128)(2,1)S(1)}, bf16[512,1792]{1,0:T(8,128)(2,1)S(1)}) custom-call(s32[1]{0:T(128)} %bitcast.phase_ref, bf16[2,512,256]{2,1,0:T(8,128)(2,1)S(1)} %copy-done.4, s32[512,27]{1,0:T(8,128)S(1)} %copy-done.12), custom_call_target="tpu_custom_call" | custom-call | flops 1000000000 | bytes 1000000 | tf_op jit(solution)/shard_map/prepare/pallas_call | solution.py:193
  15.7 1.2 %copy-done.1 = bf16[512,1792]{1,0:T(8,128)(2,1)} copy-done((bf16[512,1792]{1,0:T(8,128)(2,1)}, bf16[512,1792]{1,0:T(8,128)(2,1)S(1)}, u32[]{:S(2)}) %copy-start.1) | copy-done | bytes 1835032
  17.6 0.9 %copy-done.16 = bf16[512,256]{1,0:T(8,128)(2,1)S(1)} copy-done((bf16[512,256]{1,0:T(8,128)(2,1)S(1)}, bf16[512,256]{1,0:T(8,128)(2,1)}, u32[]{:S(2)}) %copy-start.16) | copy-done | bytes 262168
  18.6 1.1 %send.1 = bf16[128,256]{1,0:T(8,128)(2,1)S(1)} custom-call(bf16[512,256]{1,0:T(8,128)(2,1)S(1)} %copy-done.16, s32[128,128]{1,0:T(8,128)} %bitcast.5.asked_ref, s32[1,64]{1,0:T(1,128)S(1)} %copy-done.22), custom_call_target="tpu_custom_call" | custom-call | flops 100000000 | bytes 1000000 | tf_op jit(solution)/shard_map/send/pallas_call | solution.py:197
  20.4 6.9 %all-to-all-start.1 = ((bf16[16,8,256]{2,1,0:T(8,128)(2,1)}), bf16[16,8,256]{2,1,0:T(8,128)(2,1)}, u32[]{:S(2)}, u32[]{:S(2)}) async-start(bf16[16,8,256]{2,1,0:T(8,128)(2,1)} %bitcast.20), calls=%async_computation.1 | async-start | bytes 131072 | tf_op jit(solution)/shard_map/all_to_all | solution.py:184
  27.3 0.9 %copy-done.13 = s32[512,27]{1,0:T(8,128)S(1)} copy-done((s32[512,27]{1,0:T(8,128)S(1)}, s32[512,27]{1,0:T(8,128)}, u32[]{:S(2)}) %copy-start.13) | copy-done | bytes 55320
  28.2 0.9 %copy-done.17 = bf16[512,256]{1,0:T(8,128)(2,1)S(1)} copy-done((bf16[512,256]{1,0:T(8,128)(2,1)S(1)}, bf16[512,256]{1,0:T(8,128)(2,1)}, u32[]{:S(2)}) %copy-start.17) | copy-done | bytes 262168
  29.2 8.5 %local.2.total_ref = f32[512,256]{1,0:T(8,128)S(1)} custom-call(s32[1]{0:T(128)} %bitcast.phase_ref, s32[512,27]{1,0:T(8,128)S(1)} %copy-done.13, bf16[512,256]{1,0:T(8,128)(2,1)S(1)} %copy-done.17, bf16[27,256,256]{2,1,0:T(8,128)(2,1)S(1)} %bitcast.15, bf16[27,256,256]{2,1,0:T(8,128)(2,1)} %collective-permute-done.other_ref), custom_call_target="tpu_custom_call" | custom-call | flops 5435817984 | bytes 1000000 | tf_op jit(solution)/shard_map/local/pallas_call | solution.py:201
  38.5 1.5 %copy-done.2 = bf16[512,1792]{1,0:T(8,128)(2,1)S(1)} copy-done((bf16[512,1792]{1,0:T(8,128)(2,1)S(1)}, bf16[512,1792]{1,0:T(8,128)(2,1)}, u32[]{:S(2)}) %copy-start.2) | copy-done | bytes 1835032
  40.0 1.0 %copy-done.5 = bf16[2,512,256]{2,1,0:T(8,128)(2,1)S(1)} copy-done((bf16[2,512,256]{2,1,0:T(8,128)(2,1)S(1)}, bf16[2,512,256]{2,1,0:T(8,128)(2,1)}, u32[]{:S(2)}) %copy-start.5) | copy-done | bytes 524312
  41.1 1.0 %copy-done.9 = f32[512,256]{1,0:T(8,128)S(1)} copy-done((f32[512,256]{1,0:T(8,128)S(1)}, f32[512,256]{1,0:T(8,128)}, u32[]{:S(2)}) %copy-start.9) | copy-done | bytes 524312
  42.1 4.0 %encode.1 = (bf16[512,256]{1,0:T(8,128)(2,1)S(1)}, bf16[512,256]{1,0:T(8,128)(2,1)S(1)}, bf16[128,256]{1,0:T(8,128)(2,1)S(1)}) custom-call(s32[1]{0:T(128)} %bitcast.phase_ref, bf16[2,512,256]{2,1,0:T(8,128)(2,1)S(1)} %copy-done.5, f32[512,256]{1,0:T(8,128)S(1)} %copy-done.9, bf16[128,256]{1,0:T(8,128)(2,1)} %bitcast.7.received_ref, ...), custom_call_target="tpu_custom_call" | custom-call | flops 1000000000 | bytes 1000000 | tf_op jit(solution)/shard_map/encode/pallas_call | solution.py:207
  48.1 6.9 %all-to-all-start.2 = ((bf16[16,8,256]{2,1,0:T(8,128)(2,1)}), bf16[16,8,256]{2,1,0:T(8,128)(2,1)}, u32[]{:S(2)}, u32[]{:S(2)}) async-start(bf16[16,8,256]{2,1,0:T(8,128)(2,1)} %bitcast.21), calls=%async_computation.2 | async-start | bytes 131072 | tf_op jit(solution)/shard_map/all_to_all | solution.py:184
  55.9 0.9 %copy-done.25 = bf16[512,256]{1,0:T(8,128)(2,1)S(1)} copy-done((bf16[512,256]{1,0:T(8,128)(2,1)S(1)}, bf16[512,256]{1,0:T(8,128)(2,1)}, u32[]{:S(2)}) %copy-start.25) | copy-done | bytes 262168
  56.9 8.3 %local.3.total_ref = f32[512,256]{1,0:T(8,128)S(1)} custom-call(s32[1]{0:T(128)} %bitcast.phase_ref, s32[512,27]{1,0:T(8,128)S(1)} %copy-done.14, bf16[512,256]{1,0:T(8,128)(2,1)S(1)} %copy-done.25, bf16[27,256,256]{2,1,0:T(8,128)(2,1)S(1)} %bitcast.17, bf16[27,256,256]{2,1,0:T(8,128)(2,1)} %collective-permute-done.other_ref), custom_call_target="tpu_custom_call" | custom-call | flops 5435817984 | bytes 1000000 | tf_op jit(solution)/shard_map/local/pallas_call | solution.py:201
  66.0 1.5 %copy-done.3 = bf16[512,1792]{1,0:T(8,128)(2,1)S(1)} copy-done((bf16[512,1792]{1,0:T(8,128)(2,1)S(1)}, bf16[512,1792]{1,0:T(8,128)(2,1)}, u32[]{:S(2)}) %copy-start.3) | copy-done | bytes 1835032
  67.5 1.0 %copy-done.7 = f32[512,256]{1,0:T(8,128)S(1)} copy-done((f32[512,256]{1,0:T(8,128)S(1)}, f32[512,256]{1,0:T(8,128)}, u32[]{:S(2)}) %copy-start.7) | copy-done | bytes 524312
  68.5 0.9 %copy-done.11 = bf16[512,256]{1,0:T(8,128)(2,1)S(1)} copy-done((bf16[512,256]{1,0:T(8,128)(2,1)S(1)}, bf16[512,256]{1,0:T(8,128)(2,1)}, u32[]{:S(2)}) %copy-start.11) | copy-done | bytes 262168
  69.5 4.5 %decode.1 = (bf16[2,512,256]{2,1,0:T(8,128)(2,1)}, bf16[512,256]{1,0:T(8,128)(2,1)}) custom-call(s32[1]{0:T(128)} %bitcast.phase_ref, bf16[512,256]{1,0:T(8,128)(2,1)S(1)} %copy-done.11, f32[512,256]{1,0:T(8,128)S(1)} %copy-done.7, bf16[128,256]{1,0:T(8,128)(2,1)} %bitcast.9.received_ref, bf16[512,1792]{1,0:T(8,128)(2,1)S(1)} %copy-done.3, ...), custom_call_target="tpu_custom_call" | custom-call | flops 1000000000 | bytes 1000000 | tf_op jit(solution)/shard_map/decode/pallas_call | solution.py:212
  74.0 1.7 %collective-permute-done.1 = bf16[512,256]{1,0:T(8,128)(2,1)S(1)} collective-permute-done((bf16[512,256]{1,0:T(8,128)(2,1)}, bf16[512,256]{1,0:T(8,128)(2,1)S(1)}, u32[]{:S(2)}, u32[]{:S(2)}) %collective-permute-start.1) | collective-permute-done | bytes 262176 | tf_op jit(solution)/shard_map/ppermute | solution.py:216
  (47 shorter events, 8.7 us)
Async XLA Ops:
  0.0 27.3 %copy-start = (bf16[1,27,256,256]{3,2,1,0:T(8,128)(2,1)S(1)}, bf16[1,27,256,256]{3,2,1,0:T(8,128)(2,1)}, u32[]{:S(2)}) copy-start(bf16[1,27,256,256]{3,2,1,0:T(8,128)(2,1)} %param.7) | copy-start | bytes 10616836
  0.0 27.3 %collective-permute-start = (bf16[27,256,256]{2,1,0:T(8,128)(2,1)}, bf16[27,256,256]{2,1,0:T(8,128)(2,1)}, u32[]{:S(2)}, u32[]{:S(2)}) collective-permute-start(bf16[27,256,256]{2,1,0:T(8,128)(2,1)} %bitcast.14), channel_id=1, source_target_pairs={{0,16},{16,0},{1,17},{17,1},{2,18},{18,2},{3,19},{19,3},{4,20},{20... | collective-permute-start | bytes 10616840 | tf_op jit(solution)/shard_map/ppermute | solution.py:162
  0.5 0.9 %copy-start.23 = (s32[1,16,4]{1,2,0:T(4,128)S(1)}, s32[1,16,4]{1,2,0:T(4,128)}, u32[]{:S(2)}) copy-start(s32[1,16,4]{1,2,0:T(4,128)} %param.11) | copy-start | bytes 772
  2.1 15.5 %all-to-all-start = ((s32[16,8,128]{2,1,0:T(8,128)}), s32[16,8,128]{2,1,0:T(8,128)}, u32[]{:S(2)}, u32[]{:S(2)}) async-start(s32[16,8,128]{2,1,0:T(8,128)} %bitcast.19), calls=%async_computation | async-start | bytes 131072 | tf_op jit(solution)/shard_map/all_to_all | solution.py:184
  11.6 1.0 %copy-start.4 = (bf16[2,512,256]{2,1,0:T(8,128)(2,1)S(1)}, bf16[2,512,256]{2,1,0:T(8,128)(2,1)}, u32[]{:S(2)}) copy-start(bf16[2,512,256]{2,1,0:T(8,128)(2,1)} %features_ref.3) | copy-start | bytes 1572868
  12.7 0.9 %copy-start.12 = (s32[512,27]{1,0:T(8,128)S(1)}, s32[512,27]{1,0:T(8,128)}, u32[]{:S(2)}) copy-start(s32[512,27]{1,0:T(8,128)} %copy.8.codes_ref) | copy-start | bytes 165892
  13.6 4.0 %copy-start.22 = (s32[1,64]{1,0:T(1,128)S(1)}, s32[1,64]{1,0:T(1,128)}, u32[]{:S(2)}) copy-start(s32[1,64]{1,0:T(1,128)} %border_ref.3) | copy-start | bytes 772
  15.7 1.2 %copy-start.1 = (bf16[512,1792]{1,0:T(8,128)(2,1)}, bf16[512,1792]{1,0:T(8,128)(2,1)S(1)}, u32[]{:S(2)}) copy-start(bf16[512,1792]{1,0:T(8,128)(2,1)S(1)} %get-tuple-element.13.halo_onehot_ref) | copy-start | bytes 5505028
  17.6 1.0 %copy-start.16 = (bf16[512,256]{1,0:T(8,128)(2,1)S(1)}, bf16[512,256]{1,0:T(8,128)(2,1)}, u32[]{:S(2)}) copy-start(bf16[512,256]{1,0:T(8,128)(2,1)} %copy-done.15) | copy-start | bytes 786436
  20.4 18.2 %all-to-all-start.1 = ((bf16[16,8,256]{2,1,0:T(8,128)(2,1)}), bf16[16,8,256]{2,1,0:T(8,128)(2,1)}, u32[]{:S(2)}, u32[]{:S(2)}) async-start(bf16[16,8,256]{2,1,0:T(8,128)(2,1)} %bitcast.20), calls=%async_computation.1 | async-start | bytes 131072 | tf_op jit(solution)/shard_map/all_to_all | solution.py:184
  27.3 1.0 %copy-start.13 = (s32[512,27]{1,0:T(8,128)S(1)}, s32[512,27]{1,0:T(8,128)}, u32[]{:S(2)}) copy-start(s32[512,27]{1,0:T(8,128)} %copy.8.codes_ref) | copy-start | bytes 165892
  28.2 0.9 %copy-start.17 = (bf16[512,256]{1,0:T(8,128)(2,1)S(1)}, bf16[512,256]{1,0:T(8,128)(2,1)}, u32[]{:S(2)}) copy-start(bf16[512,256]{1,0:T(8,128)(2,1)} %copy-done.15) | copy-start | bytes 786436
  29.2 9.3 %copy-start.21 = (f32[2,256]{1,0:T(2,128)S(1)}, f32[2,256]{1,0:T(2,128)}, u32[]{:S(2)}) copy-start(f32[2,256]{1,0:T(2,128)} %bias_ref.3) | copy-start | bytes 6148
  37.7 0.8 %copy-start.8 = (f32[512,256]{1,0:T(8,128)}, f32[512,256]{1,0:T(8,128)S(1)}, u32[]{:S(2)}) copy-start(f32[512,256]{1,0:T(8,128)S(1)} %local.2.total_ref) | copy-start | bytes 1572868
  38.5 1.5 %copy-start.2 = (bf16[512,1792]{1,0:T(8,128)(2,1)S(1)}, bf16[512,1792]{1,0:T(8,128)(2,1)}, u32[]{:S(2)}) copy-start(bf16[512,1792]{1,0:T(8,128)(2,1)} %copy-done.1) | copy-start | bytes 5505028
  40.0 1.0 %copy-start.5 = (bf16[2,512,256]{2,1,0:T(8,128)(2,1)S(1)}, bf16[2,512,256]{2,1,0:T(8,128)(2,1)}, u32[]{:S(2)}) copy-start(bf16[2,512,256]{2,1,0:T(8,128)(2,1)} %features_ref.3) | copy-start | bytes 1572868
  41.1 1.0 %copy-start.9 = (f32[512,256]{1,0:T(8,128)S(1)}, f32[512,256]{1,0:T(8,128)}, u32[]{:S(2)}) copy-start(f32[512,256]{1,0:T(8,128)} %copy-done.8) | copy-start | bytes 1572868
  48.1 17.9 %all-to-all-start.2 = ((bf16[16,8,256]{2,1,0:T(8,128)(2,1)}), bf16[16,8,256]{2,1,0:T(8,128)(2,1)}, u32[]{:S(2)}, u32[]{:S(2)}) async-start(bf16[16,8,256]{2,1,0:T(8,128)(2,1)} %bitcast.21), calls=%async_computation.2 | async-start | bytes 131072 | tf_op jit(solution)/shard_map/all_to_all | solution.py:184
  55.0 1.0 %copy-start.14 = (s32[512,27]{1,0:T(8,128)S(1)}, s32[512,27]{1,0:T(8,128)}, u32[]{:S(2)}) copy-start(s32[512,27]{1,0:T(8,128)} %copy.8.codes_ref) | copy-start | bytes 165892
  55.9 0.9 %copy-start.25 = (bf16[512,256]{1,0:T(8,128)(2,1)S(1)}, bf16[512,256]{1,0:T(8,128)(2,1)}, u32[]{:S(2)}) copy-start(bf16[512,256]{1,0:T(8,128)(2,1)} %copy-done.24) | copy-start | bytes 786436
  66.0 1.5 %copy-start.3 = (bf16[512,1792]{1,0:T(8,128)(2,1)S(1)}, bf16[512,1792]{1,0:T(8,128)(2,1)}, u32[]{:S(2)}) copy-start(bf16[512,1792]{1,0:T(8,128)(2,1)} %copy-done.1) | copy-start | bytes 5505028
  67.5 1.0 %copy-start.7 = (f32[512,256]{1,0:T(8,128)S(1)}, f32[512,256]{1,0:T(8,128)}, u32[]{:S(2)}) copy-start(f32[512,256]{1,0:T(8,128)} %copy-done.6) | copy-start | bytes 1572868
  68.5 0.9 %copy-start.11 = (bf16[512,256]{1,0:T(8,128)(2,1)S(1)}, bf16[512,256]{1,0:T(8,128)(2,1)}, u32[]{:S(2)}) copy-start(bf16[512,256]{1,0:T(8,128)(2,1)} %copy-done.10) | copy-start | bytes 786436
  74.0 1.7 %collective-permute-start.1 = (bf16[512,256]{1,0:T(8,128)(2,1)}, bf16[512,256]{1,0:T(8,128)(2,1)S(1)}, u32[]{:S(2)}, u32[]{:S(2)}) collective-permute-start(bf16[512,256]{1,0:T(8,128)(2,1)} %get-tuple-element.18), channel_id=1, source_target_pairs={{0,16},{16,0},{1,17},{17,1},{2,18},{18,2},{3,19},{19,3},{4,20},{20... | collective-permute-start | bytes 786440 | tf_op jit(solution)/shard_map/ppermute | solution.py:216
  (7 other events, 4.8 us)

commit v3 on v0

v3 whole, which is shorter than its diff:
```python
import functools

import jax
import jax.numpy as jnp
from jax import lax
from jax.experimental import pallas as pl
from jax.experimental.pallas import tpu as pltpu
from jax.sharding import PartitionSpec as P

BF16 = jnp.bfloat16
F32 = jnp.float32
I32 = jnp.int32
TILE = 8
CHUNK = 9
VMEM_BYTES = 60 * 2**20


def iota(shape, dim):
    return lax.broadcasted_iota(I32, shape, dim)


def onehot(column, width):
    return (column == iota((column.shape[0], width), 1)).astype(BF16)


def dot(a, b):
    return jnp.dot(a, b, preferred_element_type=F32)


def normalise(values):
    mean_square = jnp.mean(values * values, axis=1, keepdims=True)
    return (values * lax.rsqrt(mean_square + 1e-06)).astype(BF16)


def packing(slots, offsets):
    pack = 128 // slots if slots < 128 else 1
    return pack, -(-offsets // pack)


def lookup(column, row):
    shape = (column.shape[0], row.shape[1])
    named = jnp.where(column == iota(shape, 1), jnp.broadcast_to(row.astype(F32), shape), 0.0)
    return jnp.sum(named, axis=1, keepdims=True).astype(I32)


class Copies:
    def __init__(self, sems):
        self.sems = sems
        self.used = 0

    def start(self, source, target):
        copy = pltpu.make_async_copy(source, target, self.sems.at[self.used])
        self.used += 1
        copy.start()
        return copy

    def weights(self, section, phase, own_ref, other_ref, held_ref):
        offsets = held_ref.shape[0]
        spans = [(first, min(CHUNK, offsets - first)) for first in range(0, offsets, CHUNK)]
        base = self.used
        self.used += len(spans)

        def copies(source):
            return [
                pltpu.make_async_copy(source.at[pl.ds(first, n)], held_ref.at[pl.ds(first, n)], self.sems.at[base + i])
                for i, (first, n) in enumerate(spans)
            ]

        pl.when(phase == section)(lambda: [copy.start() for copy in copies(own_ref)] and None)
        pl.when(phase != section)(lambda: [copy.start() for copy in copies(other_ref)] and None)
        return [(first, n, copy) for (first, n), copy in zip(spans, copies(own_ref))]


def publish_kernel(features_ref, border_ref, wanted_ref, payload_ref, block_ref, border_v, wanted_v, payload_v, sems):
    copies = Copies(sems)
    loads = [
        copies.start(features_ref.at[lax.axis_index("phase")], block_ref),
        copies.start(border_ref, border_v),
        copies.start(wanted_ref, wanted_v),
    ]
    for load in loads:
        load.wait()
    borders = border_v.shape[1]
    cap, peers = wanted_v.shape
    rows, channels = block_ref.shape
    place = lookup(iota((borders, 1), 0), border_v[...])
    picked = dot(onehot(place, rows), block_ref[...])
    shown = normalise(picked).astype(F32)
    stride = borders + TILE
    pad = jnp.zeros((TILE - cap, channels), F32)
    wanted = wanted_v[...].astype(F32)
    for peer in range(0, peers, 2):
        parts = []
        for each in (peer, peer + 1):
            parts += [shown, jnp.concatenate([jnp.broadcast_to(wanted[:, each : each + 1], (cap, channels)), pad], axis=0)]
        payload_v[peer * stride : (peer + 2) * stride, :] = jnp.concatenate(parts, axis=0).astype(BF16)
    copies.start(payload_v, payload_ref).wait()


def convolve(codes_ref, normed, held_ref, chunks):
    rows, channels = normed.shape
    total = None
    for first, count, copy in chunks:
        picked = [dot(onehot(codes_ref[:, k : k + 1], rows), normed).astype(BF16) for k in range(first, first + count)]
        copy.wait()
        matrix = held_ref[first : first + count].reshape(count * channels, channels)
        term = dot(jnp.concatenate(picked, axis=1), matrix)
        total = term if total is None else total + term
    return total


def slot_numbers(rows, per_peer, cap):
    row = iota((rows, 1), 0)
    peer = lax.div(row, per_peer)
    return peer, lax.rem(row - peer * per_peer, cap)


def build_halo_onehot(codes_ref, slots, halo_onehot_v):
    rows, offsets = codes_ref.shape
    pack, groups = packing(slots, offsets)
    width = slots * pack
    lane = iota((rows, width), 1)
    for group in range(groups):
        named = None
        for j in range(pack):
            k = group * pack + j
            code = codes_ref[:, k : k + 1] + (j * slots - rows) if k < offsets else jnp.full((rows, 1), -1, I32)
            code = jnp.broadcast_to(code, (rows, width))
            named = code if named is None else jnp.where(lane >= j * slots, code, named)
        halo_onehot_v[:, group * width : (group + 1) * width] = (named == lane).astype(BF16)


def published_places(wanted, borders):
    cap, peers = wanted.shape
    stride = borders + TILE
    peer, slot = slot_numbers(peers * cap, cap, cap)
    mine = lax.dot_general(
        onehot(peer, peers), wanted.astype(BF16), (((1,), (1,)), ((), ())), preferred_element_type=F32
    )
    mine = jnp.sum(jnp.where(iota(mine.shape, 1) == slot, mine, 0.0), axis=1, keepdims=True).astype(I32)
    asker, place = slot_numbers(peers * TILE, TILE, cap)
    return jnp.concatenate([peer * stride + mine, asker * stride + borders + place], axis=0)


def first_local_kernel(
    borders, features_ref, codes_ref, wanted_ref, own_ref, other_ref, total_ref, halo_onehot_ref, places_ref,
    block_ref, codes_v, wanted_v, held_ref, total_v, halo_onehot_v, places_v, sems,
):
    phase = lax.axis_index("phase")
    copies = Copies(sems)
    loads = [
        copies.start(codes_ref, codes_v),
        copies.start(features_ref.at[phase], block_ref),
        copies.start(wanted_ref, wanted_v),
    ]
    chunks = copies.weights(0, phase, own_ref, other_ref, held_ref)
    for load in loads:
        load.wait()
    cap, peers = wanted_v.shape
    places_v[...] = jnp.broadcast_to(published_places(wanted_v[...], borders), places_v.shape)
    build_halo_onehot(codes_v, peers * cap, halo_onehot_v)
    stores = [copies.start(places_v, places_ref), copies.start(halo_onehot_v, halo_onehot_ref)]
    total_v[...] = convolve(codes_v, normalise(block_ref[...].astype(F32)), held_ref, chunks)
    stores.append(copies.start(total_v, total_ref))
    for store in stores:
        store.wait()


def second_local_kernel(normed_ref, codes_ref, own_ref, other_ref, total_ref, block_ref, codes_v, held_ref, total_v, sems):
    phase = lax.axis_index("phase")
    copies = Copies(sems)
    loads = [copies.start(codes_ref, codes_v), copies.start(normed_ref, block_ref)]
    chunks = copies.weights(1, phase, own_ref, other_ref, held_ref)
    for load in loads:
        load.wait()
    total_v[...] = convolve(codes_v, block_ref[...], held_ref, chunks)
    copies.start(total_v, total_ref).wait()


def pick_rows(places, source_ref):
    rows = source_ref.shape[0]
    step = next(n for n in range(min(rows, 1536) // 16 * 16, 0, -16) if rows % n == 0)
    found = None
    for first in range(0, rows, step):
        term = dot(onehot(places - first, step), source_ref[first : first + step, :])
        found = term if found is None else found + term
    return found


def halo_term(halo, offsets, chunks, held_ref, spread_ref, halo_onehot_v, onehot_load):
    slots, channels = halo.shape
    pack, groups = packing(slots, offsets)
    whole = groups * pack * slots
    if whole > offsets * slots:
        spread_ref[offsets * slots : whole, :] = jnp.zeros((whole - offsets * slots, channels), BF16)
    for first, count, copy in chunks:
        copy.wait()
        for k in range(first, first + count):
            spread_ref[k * slots : (k + 1) * slots, :] = dot(halo, held_ref[k]).astype(BF16)
    onehot_load.wait()
    total = None
    for first in range(0, whole, 2048):
        last = min(first + 2048, whole)
        term = dot(halo_onehot_v[:, first:last], spread_ref[first:last, :])
        total = term if total is None else total + term
    return total


def residual(values, convolved):
    return (values + jax.nn.silu(convolved)).astype(BF16)


def encode_kernel(
    features_ref, total_ref, received_ref, halo_onehot_ref, places_ref, border_ref, bias_ref, own_ref, other_ref,
    latent_ref, normed_ref, send_ref,
    block_ref, total_v, received_v, halo_onehot_v, places_v, border_v, bias_v, held_ref, spread_ref,
    latent_v, normed_v, send_v, sems,
):
    phase = lax.axis_index("phase")
    copies = Copies(sems)
    early = [
        copies.start(received_ref, received_v),
        copies.start(places_ref, places_v),
        copies.start(border_ref, border_v),
    ]
    chunks = copies.weights(0, phase, own_ref, other_ref, held_ref)
    onehot_load = copies.start(halo_onehot_ref, halo_onehot_v)
    late = [
        copies.start(total_ref, total_v),
        copies.start(features_ref.at[phase], block_ref),
        copies.start(bias_ref, bias_v),
    ]
    for load in early:
        load.wait()
    requests = send_v.shape[0]
    slots = places_v.shape[0] - requests
    found = pick_rows(places_v[:, 0:1], received_v)
    asked = lookup(found[slots:, 0:1].astype(I32), border_v[...])
    term = halo_term(found[:slots].astype(BF16), held_ref.shape[0], chunks, held_ref, spread_ref, halo_onehot_v, onehot_load)
    for load in late:
        load.wait()
    latent = residual(block_ref[...].astype(F32), total_v[...] + term + bias_v[0:1, :])
    latent_v[...] = latent
    stores = [copies.start(latent_v, latent_ref)]
    normed = normalise(latent.astype(F32))
    normed_v[...] = normed
    stores.append(copies.start(normed_v, normed_ref))
    send_v[...] = dot(onehot(asked, normed.shape[0]), normed).astype(BF16)
    stores.append(copies.start(send_v, send_ref))
    for store in stores:
        store.wait()


def decode_kernel(
    cap, latent_ref, total_ref, received_ref, halo_onehot_ref, bias_ref, own_ref, other_ref,
    kept_ref, passed_ref,
    latent_v, total_v, received_v, halo_onehot_v, bias_v, held_ref, spread_ref, recon_v, sems,
):
    phase = lax.axis_index("phase")
    copies = Copies(sems)
    received_load = copies.start(received_ref, received_v)
    chunks = copies.weights(1, phase, own_ref, other_ref, held_ref)
    onehot_load = copies.start(halo_onehot_ref, halo_onehot_v)
    late = [
        copies.start(total_ref, total_v),
        copies.start(latent_ref, latent_v),
        copies.start(bias_ref, bias_v),
    ]
    received_load.wait()
    requests = received_v.shape[0]
    peer, slot = slot_numbers(requests // TILE * cap, cap, cap)
    halo = pick_rows(peer * TILE + slot, received_v).astype(BF16)
    term = halo_term(halo, held_ref.shape[0], chunks, held_ref, spread_ref, halo_onehot_v, onehot_load)
    for load in late:
        load.wait()
    recon_v[...] = residual(latent_v[...].astype(F32), total_v[...] + term + bias_v[1:2, :])
    stores = [(latent_v, kept_ref.at[0], recon_v, passed_ref), (recon_v, kept_ref.at[1], latent_v, passed_ref)]
    used = copies.used

    def put(kept, place, passed, target):
        return [
            pltpu.make_async_copy(kept, place, sems.at[used]),
            pltpu.make_async_copy(passed, target, sems.at[used + 1]),
        ]

    pl.when(phase == 0)(lambda: [copy.start() for copy in put(*stores[0])] and None)
    pl.when(phase != 0)(lambda: [copy.start() for copy in put(*stores[1])] and None)
    for copy in put(*stores[0]):
        copy.wait()


def body(features, weights, conv_bias, rulebook, border, pull_slots):
    micro, rows, channels = features.shape
    peers, cap = pull_slots.shape[1:]
    borders = border.shape[1]
    offsets = rulebook.shape[1]
    slots = peers * cap
    pack, groups = packing(slots, offsets)
    published = peers * (borders + TILE)
    phase = lax.axis_index("phase")
    wanted = pull_slots[0].T
    own = weights[0]
    swap = [(0, 1), (1, 0)]
    other = lax.ppermute(own, "phase", swap)

    anywhere = pl.BlockSpec(memory_space=pl.ANY)
    array = jax.ShapeDtypeStruct
    block = array((rows, channels), BF16)
    total_like = array((rows, channels), F32)
    published_like = array((published, channels), BF16)
    sent_like = array((peers * TILE, channels), BF16)
    onehot_like = array((rows, groups * pack * slots), BF16)
    places_like = array((slots + peers * TILE, 128), I32)
    weights_like = array(own.shape, BF16)
    spread_like = array((groups * pack * slots, channels), BF16)

    def call(kernel, name, args, out_shapes, scratch, flops):
        return pl.pallas_call(
            kernel,
            in_specs=[anywhere] * len(args),
            out_specs=[anywhere] * len(out_shapes),
            out_shape=out_shapes,
            scratch_shapes=[pltpu.VMEM(s.shape, s.dtype) for s in scratch] + [pltpu.SemaphoreType.DMA((20,))],
            compiler_params=pltpu.CompilerParams(vmem_limit_bytes=VMEM_BYTES),
            cost_estimate=pl.CostEstimate(flops=flops, bytes_accessed=10**6, transcendentals=0),
            name=name,
        )(*args)

    def exchange(value):
        return lax.all_to_all(value, "space", 0, 0, tiled=True)

    local_flops = 2 * offsets * rows * channels * (rows + channels)
    payload, = call(
        publish_kernel, "publish", (features, border, wanted), [published_like],
        [block, border, wanted, published_like], 10**8,
    )
    received = exchange(payload)
    total, halo_onehot, places = call(
        functools.partial(first_local_kernel, borders), "first_local", (features, rulebook, wanted, own, other),
        [total_like, onehot_like, places_like],
        [block, rulebook, wanted, weights_like, total_like, onehot_like, places_like], local_flops,
    )
    latent, normed, send = call(
        encode_kernel, "encode", (features, total, received, halo_onehot, places, border, conv_bias, own, other),
        [block, block, sent_like],
        [block, total_like, published_like, onehot_like, places_like, border, conv_bias, weights_like, spread_like,
         block, block, sent_like], 10**9,
    )
    received = exchange(send)
    total, = call(
        second_local_kernel, "second_local", (normed, rulebook, own, other), [total_like],
        [block, rulebook, weights_like, total_like], local_flops,
    )
    kept, passed = call(
        functools.partial(decode_kernel, cap), "decode", (latent, total, received, halo_onehot, conv_bias, own, other),
        [array((2, rows, channels), BF16), block],
        [block, total_like, sent_like, onehot_like, conv_bias, weights_like, spread_like, block], 10**9,
    )
    got = lax.ppermute(passed, "phase", swap)
    return lax.dynamic_update_slice(kept, got[None], (1 - phase, 0, 0))[None]


def solution(mesh):
    return jax.shard_map(
        body,
        mesh=mesh,
        in_specs=(
            P(None, "space", None),
            P("phase", None, None, None),
            P(),
            P("space", None),
            P("space", None),
            P("space", None, None),
        ),
        out_specs=P("phase", None, "space", None),
        check_vma=False,
    )
```

time: 308 us -> 54.5 us (0.18); the launches traced: 303 us -> 54.1 us
  blocking collectives: 132 us -> 0 us
  local copies, waits for them, and re-layouts: 125 us -> 4.8 us
  Pallas kernels: 0 us -> 32.2 us
  other arithmetic: 26.4 us -> 0 us
  matrix products: 16.4 us -> 0 us
  starting transfers between devices: 2.61 us -> 13.4 us
    all_gather x3 -> x0, blocking collectives: 132 us -> none  [body(): published = lax.all_gather(border_rows, 'space', axis=0, tiled=True)]
    gather x9 -> x0, local copies, waits for them, and re-layouts: 119 us -> none  [the longest x3 105 us: body(): picked = jnp.take(lookup, offsets_first, axis=0)]
    pallas_call x0 -> x5, Pallas kernels: none -> 32.2 us  [call(): pl.pallas_call(kernel, in_specs=[anywhere] * len(args), out_specs=[anywhe...]
    dot_general x3 -> x0, matrix products: 16.4 us -> none  [body(): jnp.einsum('krc,kcd->rd', picked, kernel, preferred_element_type=jnp.floa...]
    all_to_all x0 -> x2, starting transfers between devices: none -> 12.9 us  [exchange(): return lax.all_to_all(value, 'space', 0, 0, tiled=True)]
    select_n x9 -> x0, other arithmetic: 8.36 us -> none  [the longest x4 3.16 us: body(): border_rows = jnp.take(normed, own_border, axis=0)]
    concatenate x3 -> x0, other arithmetic: 5.43 us -> none  [body(): jnp.concatenate([normed, halo_rows, jnp.zeros((1, channels), jnp.bfloat16...]
    and x3 -> x0, other arithmetic: 3.5 us -> none  [the longest x1 1.46 us: body(): picked = jnp.take(lookup, offsets_first, axis=0)]
  transfers between devices with their start and end apart: 2 -> 4, of which waited for: 2 -> 2; matrix products, arithmetic and copies ran while one was open for 0% -> 3% of each run, Pallas kernels for 0% -> 43%
where the time goes in v3:
time: 54.5 us; the launch traced here: 54.1 us
  Pallas kernels  32.2 us (59%)
  starting transfers between devices  13.4 us (25%)
  local copies, waits for them, and re-layouts  4.8 us (9%)
  waiting for transfers between devices  3.68 us (7%)
    pallas_call x5, Pallas kernels, call(): pl.pallas_call(kernel, in_specs=[anywhere] * len(args), out_specs=[anywhe...  32.2 us
    all_to_all x2, starting transfers between devices, exchange(): return lax.all_to_all(value, 'space', 0, 0, tiled=True)  12.9 us
    unnamed x5, local copies, waits for them, and re-layouts  4.08 us
    all_to_all x2, waiting for transfers between devices, exchange(): return lax.all_to_all(value, 'space', 0, 0, tiled=True)  1.95 us
    ppermute x1, waiting for transfers between devices, body(): got = lax.ppermute(passed, 'phase', swap)  1.73 us
  transfers between devices with their start and end apart: 4, of which 2 were waited for; matrix products, arithmetic and copies ran while one was open for 3% of the time, Pallas kernels for 43%

profile of v3, /device:TPU:0, one launch (start us, length us, event | category | flops | bytes accessed | tf_op | source)
XLA Modules:
  0.0 54.1 jit_solution(18218395012012179925)
XLA Ops:
  0.0 0.5 collective-permute-start
  0.5 2.3 %publish.1 = bf16[1152,256]{1,0:T(8,128)(2,1)} custom-call(bf16[2,512,256]{2,1,0:T(8,128)(2,1)} %features_ref.5, s32[1,64]{1,0:T(1,128)} %border_ref.3, s32[4,16]{1,0:T(4,128)} %bitcast.19), custom_call_target="tpu_custom_call" | custom-call | flops 100000000 | bytes 1000000 | tf_op jit(solution)/shard_map/publish/pallas_call | solution.py:318
  2.8 7.9 %all-to-all-start = ((bf16[16,72,256]{2,1,0:T(8,128)(2,1)}), bf16[16,72,256]{2,1,0:T(8,128)(2,1)}, u32[]{:S(2)}, u32[]{:S(2)}) async-start(bf16[16,72,256]{2,1,0:T(8,128)(2,1)} %bitcast.16), calls=%async_computation | async-start | bytes 1179648 | tf_op jit(solution)/shard_map/all_to_all | solution.py:330
  10.7 1.7 %copy.7.codes_ref = s32[512,27]{1,0:T(8,128)} copy(s32[512,27]{0,1:T(8,128)} %param.9) | data formatting | bytes 110592 | tf_op args[3]
  12.4 0.0 collective-permute-done.other_ref
  12.4 0.0 copy-start
  12.4 1.7 %copy-done = bf16[27,256,256]{2,1,0:T(8,128)(2,1)} copy-done((bf16[27,256,256]{2,1,0:T(8,128)(2,1)}, bf16[27,256,256]{2,1,0:T(8,128)(2,1)S(1)}, u32[]{:S(2)}) %copy-start) | copy-done | bytes 3538968
  14.1 11.3 %first_local.1 = (f32[512,256]{1,0:T(8,128)}, bf16[512,1792]{1,0:T(8,128)(2,1)}, s32[192,128]{1,0:T(8,128)}) custom-call(bf16[2,512,256]{2,1,0:T(8,128)(2,1)} %features_ref.5, s32[512,27]{1,0:T(8,128)} %copy.7.codes_ref, s32[4,16]{1,0:T(4,128)} %bitcast.20, bf16[27,256,256]{2,1,0:T(8,128)(2,1)} %bitcast.12, bf16[27,256,256]{2,1,0:T(8,128)(2,1)} %copy-done), custom_call_target="tpu_custom_call" | custom-call | flops 5435817984 | bytes 1000000 | tf_op jit(solution)/shard_map/first_local/pallas_call | solution.py:318
  25.4 1.9 %all-to-all-done = bf16[16,72,256]{2,1,0:T(8,128)(2,1)} async-done(((bf16[16,72,256]{2,1,0:T(8,128)(2,1)}), bf16[16,72,256]{2,1,0:T(8,128)(2,1)}, u32[]{:S(2)}, u32[]{:S(2)}) %all-to-all-start) | async-done | bytes 589856 | tf_op jit(solution)/shard_map/all_to_all | solution.py:330
  27.4 4.7 %encode.1 = (bf16[512,256]{1,0:T(8,128)(2,1)}, bf16[512,256]{1,0:T(8,128)(2,1)}, bf16[128,256]{1,0:T(8,128)(2,1)}) custom-call(bf16[2,512,256]{2,1,0:T(8,128)(2,1)} %features_ref.5, f32[512,256]{1,0:T(8,128)} %get-tuple-element.13.total_ref, bf16[1152,256]{1,0:T(8,128)(2,1)} %bitcast.5.received_ref, bf16[512,1792]{1,0:T(8,128)(2,1)} %get-tuple-element.14.halo_onehot_ref, ...), custom_call_target="tpu_custom_call" | custom-call | flops 1000000000 | bytes 1000000 | tf_op jit(solution)/shard_map/encode/pallas_call | solution.py:318
  32.1 5.0 %all-to-all-start.1 = ((bf16[16,8,256]{2,1,0:T(8,128)(2,1)}), bf16[16,8,256]{2,1,0:T(8,128)(2,1)S(1)}, u32[]{:S(2)}, u32[]{:S(2)}) async-start(bf16[16,8,256]{2,1,0:T(8,128)(2,1)} %bitcast.18), calls=%async_computation.1 | async-start | bytes 131072 | tf_op jit(solution)/shard_map/all_to_all | solution.py:330
  37.1 9.6 %second_local.1.total_ref = f32[512,256]{1,0:T(8,128)} custom-call(bf16[512,256]{1,0:T(8,128)(2,1)} %get-tuple-element.17.normed_ref, s32[512,27]{1,0:T(8,128)} %copy.7.codes_ref, bf16[27,256,256]{2,1,0:T(8,128)(2,1)} %bitcast.14, bf16[27,256,256]{2,1,0:T(8,128)(2,1)} %copy-done), custom_call_target="tpu_custom_call" | custom-call | flops 5435817984 | bytes 1000000 | tf_op jit(solution)/shard_map/second_local/pallas_call | solution.py:318
  46.7 0.0 all-to-all-done.1
  46.7 0.0 copy-start.1
  46.7 0.6 %copy-done.1 = bf16[16,8,256]{2,1,0:T(8,128)(2,1)} copy-done((bf16[16,8,256]{2,1,0:T(8,128)(2,1)}, bf16[16,8,256]{2,1,0:T(8,128)(2,1)S(1)}, u32[]{:S(2)}) %copy-start.1) | copy-done | bytes 65560
  47.3 4.3 %decode.1 = (bf16[2,512,256]{2,1,0:T(8,128)(2,1)}, bf16[512,256]{1,0:T(8,128)(2,1)}) custom-call(bf16[512,256]{1,0:T(8,128)(2,1)} %get-tuple-element.16.latent_ref, f32[512,256]{1,0:T(8,128)} %second_local.1.total_ref, bf16[128,256]{1,0:T(8,128)(2,1)} %bitcast.17, bf16[512,1792]{1,0:T(8,128)(2,1)} %get-tuple-element.14.halo_onehot_ref, f32[2,256]{1,0:T(2,128)} %bias_ref.3, ...), custom_call_target="tpu_custom_call" | custom-call | flops 1000000000 | bytes 1000000 | tf_op jit(solution)/shard_map/decode/pallas_call | solution.py:318
  51.6 0.1 collective-permute-start.1
  51.7 1.7 %collective-permute-done.1 = bf16[512,256]{1,0:T(8,128)(2,1)S(1)} collective-permute-done((bf16[512,256]{1,0:T(8,128)(2,1)}, bf16[512,256]{1,0:T(8,128)(2,1)S(1)}, u32[]{:S(2)}, u32[]{:S(2)}) %collective-permute-start.1) | collective-permute-done | bytes 262176 | tf_op jit(solution)/shard_map/ppermute | solution.py:359
  53.4 0.7 %bitcast_dynamic-update-slice_fusion = bf16[1,2,512,256]{3,2,1,0:T(8,128)(2,1)} fusion(bf16[1,2,512,256]{3,2,1,0:T(8,128)(2,1)} %bitcast.21, s32[]{:T(128)S(6)} %select_n.3, bf16[512,256]{1,0:T(8,128)(2,1)S(1)} %collective-permute-done.1), kind=kLoop, calls=%fused_computation | loop fusion | bytes 524292 | tf_op jit(solution)/shard_map/dynamic_update_slice | solution.py:360
Async XLA Ops:
  0.0 12.4 %collective-permute-start = (bf16[27,256,256]{2,1,0:T(8,128)(2,1)}, bf16[27,256,256]{2,1,0:T(8,128)(2,1)S(1)}, u32[]{:S(2)}, u32[]{:S(2)}) collective-permute-start(bf16[27,256,256]{2,1,0:T(8,128)(2,1)} %bitcast.11), channel_id=1, source_target_pairs={{0,16},{16,0},{1,17},{17,1},{2,18},{18,2},{3,19},{19,3},{4,20},{20... | collective-permute-start | bytes 10616840 | tf_op jit(solution)/shard_map/ppermute | solution.py:304
  2.8 24.6 %all-to-all-start = ((bf16[16,72,256]{2,1,0:T(8,128)(2,1)}), bf16[16,72,256]{2,1,0:T(8,128)(2,1)}, u32[]{:S(2)}, u32[]{:S(2)}) async-start(bf16[16,72,256]{2,1,0:T(8,128)(2,1)} %bitcast.16), calls=%async_computation | async-start | bytes 1179648 | tf_op jit(solution)/shard_map/all_to_all | solution.py:330
  12.4 1.8 %copy-start = (bf16[27,256,256]{2,1,0:T(8,128)(2,1)}, bf16[27,256,256]{2,1,0:T(8,128)(2,1)S(1)}, u32[]{:S(2)}) copy-start(bf16[27,256,256]{2,1,0:T(8,128)(2,1)S(1)} %collective-permute-done.other_ref) | copy-start | bytes 10616836
  32.1 14.5 %all-to-all-start.1 = ((bf16[16,8,256]{2,1,0:T(8,128)(2,1)}), bf16[16,8,256]{2,1,0:T(8,128)(2,1)S(1)}, u32[]{:S(2)}, u32[]{:S(2)}) async-start(bf16[16,8,256]{2,1,0:T(8,128)(2,1)} %bitcast.18), calls=%async_computation.1 | async-start | bytes 131072 | tf_op jit(solution)/shard_map/all_to_all | solution.py:330
  46.7 0.6 %copy-start.1 = (bf16[16,8,256]{2,1,0:T(8,128)(2,1)}, bf16[16,8,256]{2,1,0:T(8,128)(2,1)S(1)}, u32[]{:S(2)}) copy-start(bf16[16,8,256]{2,1,0:T(8,128)(2,1)S(1)} %all-to-all-done.1) | copy-start | bytes 196612
  51.6 1.8 %collective-permute-start.1 = (bf16[512,256]{1,0:T(8,128)(2,1)}, bf16[512,256]{1,0:T(8,128)(2,1)S(1)}, u32[]{:S(2)}, u32[]{:S(2)}) collective-permute-start(bf16[512,256]{1,0:T(8,128)(2,1)} %get-tuple-element.20), channel_id=1, source_target_pairs={{0,16},{16,0},{1,17},{17,1},{2,18},{18,2},{3,19},{19,3},{4,20},{20... | collective-permute-start | bytes 786440 | tf_op jit(solution)/shard_map/ppermute | solution.py:359

commit v4 on v3

v4 whole, which is shorter than its diff:
```python
import functools

import jax
import jax.numpy as jnp
from jax import lax
from jax.experimental import pallas as pl
from jax.experimental.pallas import tpu as pltpu
from jax.sharding import PartitionSpec as P

BF16 = jnp.bfloat16
F32 = jnp.float32
I32 = jnp.int32
TILE = 8
BLOCK = 128
VMEM_BYTES = 60 * 2**20


def iota(shape, dim):
    return lax.broadcasted_iota(I32, shape, dim)


def onehot(column, width):
    return (column == iota((column.shape[0], width), 1)).astype(BF16)


def dot(a, b):
    return jnp.dot(a, b, preferred_element_type=F32)


def normalise(values):
    mean_square = jnp.mean(values * values, axis=1, keepdims=True)
    return (values * lax.rsqrt(mean_square + 1e-06)).astype(BF16)


def packing(slots, offsets):
    pack = 128 // slots if slots < 128 else 1
    return pack, -(-offsets // pack)


def lookup(column, row):
    shape = (column.shape[0], row.shape[1])
    named = jnp.where(column == iota(shape, 1), jnp.broadcast_to(row.astype(F32), shape), 0.0)
    return jnp.sum(named, axis=1, keepdims=True).astype(I32)


class Copies:
    def __init__(self, sems):
        self.sems = sems
        self.used = 0

    def start(self, source, target):
        copy = pltpu.make_async_copy(source, target, self.sems.at[self.used])
        self.used += 1
        copy.start()
        return copy

    def start_either(self, chosen, copy, other):
        sem = self.sems.at[self.used]
        self.used += 1
        copy, other = (pltpu.make_async_copy(source, target, sem) for source, target in (copy, other))
        pl.when(chosen)(copy.start)
        pl.when(jnp.logical_not(chosen))(other.start)
        return copy


def publish_kernel(features_ref, border_ref, wanted_ref, payload_ref, block_ref, border_v, wanted_v, payload_v, sems):
    copies = Copies(sems)
    loads = [
        copies.start(features_ref.at[lax.axis_index("phase")], block_ref),
        copies.start(border_ref, border_v),
        copies.start(wanted_ref, wanted_v),
    ]
    for load in loads:
        load.wait()
    borders = border_v.shape[1]
    cap, peers = wanted_v.shape
    rows, channels = block_ref.shape
    place = lookup(iota((borders, 1), 0), border_v[...])
    picked = dot(onehot(place, rows), block_ref[...])
    shown = normalise(picked).astype(F32)
    stride = borders + TILE
    pad = jnp.zeros((TILE - cap, channels), F32)
    wanted = wanted_v[...].astype(F32)
    for peer in range(0, peers, 2):
        parts = []
        for each in (peer, peer + 1):
            parts += [shown, jnp.concatenate([jnp.broadcast_to(wanted[:, each : each + 1], (cap, channels)), pad], axis=0)]
        payload_v[peer * stride : (peer + 2) * stride, :] = jnp.concatenate(parts, axis=0).astype(BF16)
    copies.start(payload_v, payload_ref).wait()


def gather(codes, normed, picked_v, beside=lambda k: None):
    rows, channels = normed.shape
    for k in range(codes.shape[1]):
        picked_v[:, k * channels : (k + 1) * channels] = dot(onehot(codes[:, k : k + 1], rows), normed).astype(BF16)
        beside(k)


def convolved_blocks(picked_v, held_ref):
    rows = picked_v.shape[0]
    matrix = held_ref[...].reshape(picked_v.shape[1], held_ref.shape[2])
    for first in range(0, rows, BLOCK):
        span = pl.ds(first, BLOCK)
        yield span, dot(picked_v[span, :], matrix)


def slot_numbers(rows, per_peer, cap):
    row = iota((rows, 1), 0)
    peer = lax.div(row, per_peer)
    return peer, lax.rem(row - peer * per_peer, cap)


def halo_onehot_group(codes, slots, group, halo_onehot_v):
    rows, offsets = codes.shape
    pack, groups = packing(slots, offsets)
    width = slots * pack
    lane = iota((rows, width), 1)
    named = None
    for j in range(pack):
        k = group * pack + j
        code = codes[:, k : k + 1] + (j * slots - rows) if k < offsets else jnp.full((rows, 1), -1, I32)
        code = jnp.broadcast_to(code, (rows, width))
        named = code if named is None else jnp.where(lane >= j * slots, code, named)
    halo_onehot_v[:, group * width : (group + 1) * width] = (named == lane).astype(BF16)


def published_places(wanted, borders):
    cap, peers = wanted.shape
    stride = borders + TILE
    peer, slot = slot_numbers(peers * cap, cap, cap)
    mine = lax.dot_general(
        onehot(peer, peers), wanted.astype(BF16), (((1,), (1,)), ((), ())), preferred_element_type=F32
    )
    mine = jnp.sum(jnp.where(iota(mine.shape, 1) == slot, mine, 0.0), axis=1, keepdims=True).astype(I32)
    asker, place = slot_numbers(peers * TILE, TILE, cap)
    return jnp.concatenate([peer * stride + mine, asker * stride + borders + place], axis=0)


def first_local_kernel(
    borders, features_ref, codes_ref, wanted_ref, own_ref, other_ref,
    total_ref, halo_onehot_ref, places_ref,
    block_ref, codes_v, wanted_v, held_ref, picked_v, total_v, halo_onehot_v, places_v, sems,
):
    phase = lax.axis_index("phase")
    copies = Copies(sems)
    loads = [
        copies.start(codes_ref, codes_v),
        copies.start(features_ref.at[phase], block_ref),
        copies.start(wanted_ref, wanted_v),
    ]
    weights_load = copies.start_either(phase == 0, (own_ref, held_ref), (other_ref, held_ref))
    for load in loads:
        load.wait()
    codes = codes_v[...].T
    cap, peers = wanted_v.shape
    slots = peers * cap
    pack, groups = packing(slots, codes.shape[1])
    places_v[...] = jnp.broadcast_to(published_places(wanted_v[...], borders), places_v.shape)

    def beside(k):
        if k % pack == 0:
            halo_onehot_group(codes, slots, k // pack, halo_onehot_v)

    gather(codes, normalise(block_ref[...].astype(F32)), picked_v, beside)
    stores = [copies.start(places_v, places_ref), copies.start(halo_onehot_v, halo_onehot_ref)]
    weights_load.wait()
    for span, term in convolved_blocks(picked_v, held_ref):
        total_v[span, :] = term
        stores.append(copies.start(total_v.at[span], total_ref.at[span]))
    for store in stores:
        store.wait()


def pick_rows(places, source_ref):
    rows = source_ref.shape[0]
    step = next(n for n in range(min(rows, 1536) // 16 * 16, 0, -16) if rows % n == 0)
    found = None
    for first in range(0, rows, step):
        term = dot(onehot(places - first, step), source_ref[first : first + step, :])
        found = term if found is None else found + term
    return found


def spread_halo(halo, held_ref, spread_ref):
    slots, channels = halo.shape
    offsets = held_ref.shape[0]
    whole = spread_ref.shape[0]
    if whole > offsets * slots:
        spread_ref[offsets * slots : whole, :] = jnp.zeros((whole - offsets * slots, channels), BF16)
    for k in range(offsets):
        spread_ref[k * slots : (k + 1) * slots, :] = dot(halo, held_ref[k]).astype(BF16)


def halo_term(halo_onehot_v, span, spread_ref):
    total = None
    for first in range(0, spread_ref.shape[0], 2048):
        lanes = pl.ds(first, min(2048, spread_ref.shape[0] - first))
        term = dot(halo_onehot_v[span, lanes], spread_ref[lanes, :])
        total = term if total is None else total + term
    return total


def residual(values, convolved):
    return (values + jax.nn.silu(convolved)).astype(BF16)


def encode_kernel(
    features_ref, total_ref, received_ref, halo_onehot_ref, places_ref, border_ref, bias_ref, own_ref, other_ref,
    latent_ref, normed_ref, send_ref,
    block_ref, total_v, received_v, halo_onehot_v, places_v, border_v, bias_v, held_ref, spread_ref,
    latent_v, normed_v, send_v, sems,
):
    phase = lax.axis_index("phase")
    copies = Copies(sems)
    early = [
        copies.start(received_ref, received_v),
        copies.start(places_ref, places_v),
        copies.start(border_ref, border_v),
    ]
    weights_load = copies.start_either(phase == 0, (own_ref, held_ref), (other_ref, held_ref))
    late = [
        copies.start(halo_onehot_ref, halo_onehot_v),
        copies.start(total_ref, total_v),
        copies.start(features_ref.at[phase], block_ref),
        copies.start(bias_ref, bias_v),
    ]
    for load in early:
        load.wait()
    slots = places_v.shape[0] - send_v.shape[0]
    found = pick_rows(places_v[:, 0:1], received_v)
    asked = lookup(found[slots:, 0:1].astype(I32), border_v[...])
    weights_load.wait()
    spread_halo(found[:slots].astype(BF16), held_ref, spread_ref)
    for load in late:
        load.wait()
    term = halo_term(halo_onehot_v, pl.ds(0, block_ref.shape[0]), spread_ref)
    latent = residual(block_ref[...].astype(F32), total_v[...] + term + bias_v[0:1, :])
    latent_v[...] = latent
    stores = [copies.start(latent_v, latent_ref)]
    normed = normalise(latent.astype(F32))
    normed_v[...] = normed
    stores.append(copies.start(normed_v, normed_ref))
    send_v[...] = dot(onehot(asked, normed.shape[0]), normed).astype(BF16)
    stores.append(copies.start(send_v, send_ref))
    for store in stores:
        store.wait()


def second_local_kernel(
    normed_ref, codes_ref, own_ref, other_ref, total_ref, normed_v, codes_v, held_ref, picked_v, total_v, sems
):
    phase = lax.axis_index("phase")
    copies = Copies(sems)
    early = [copies.start(codes_ref, codes_v), copies.start(normed_ref, normed_v)]
    weights_load = copies.start_either(phase == 1, (own_ref, held_ref), (other_ref, held_ref))
    for load in early:
        load.wait()
    gather(codes_v[...].T, normed_v[...], picked_v)
    weights_load.wait()
    stores = []
    for span, term in convolved_blocks(picked_v, held_ref):
        total_v[span, :] = term
        stores.append(copies.start(total_v.at[span], total_ref.at[span]))
    for store in stores:
        store.wait()


def decode_kernel(
    cap, latent_ref, total_ref, received_ref, halo_onehot_ref, bias_ref, own_ref, other_ref, kept_ref, passed_ref,
    latent_v, total_v, received_v, halo_onehot_v, bias_v, held_ref, spread_ref, recon_v, sems,
):
    first = lax.axis_index("phase") == 0
    copies = Copies(sems)
    received_load = copies.start(received_ref, received_v)
    weights_load = copies.start_either(first, (other_ref, held_ref), (own_ref, held_ref))
    late = [
        copies.start(halo_onehot_ref, halo_onehot_v),
        copies.start(total_ref, total_v),
        copies.start(latent_ref, latent_v),
        copies.start(bias_ref, bias_v),
    ]
    received_load.wait()
    peer, slot = slot_numbers(received_v.shape[0] // TILE * cap, cap, cap)
    halo = pick_rows(peer * TILE + slot, received_v).astype(BF16)
    weights_load.wait()
    spread_halo(halo, held_ref, spread_ref)
    for load in late:
        load.wait()
    stores = [copies.start_either(first, (latent_v, kept_ref.at[0]), (latent_v, passed_ref))]
    term = halo_term(halo_onehot_v, pl.ds(0, latent_v.shape[0]), spread_ref)
    recon_v[...] = residual(latent_v[...].astype(F32), total_v[...] + term + bias_v[1:2, :])
    stores.append(copies.start_either(first, (recon_v, passed_ref), (recon_v, kept_ref.at[1])))
    for store in stores:
        store.wait()


def body(features, weights, conv_bias, rulebook, border, pull_slots):
    micro, rows, channels = features.shape
    peers, cap = pull_slots.shape[1:]
    borders = border.shape[1]
    offsets = rulebook.shape[1]
    slots = peers * cap
    pack, groups = packing(slots, offsets)
    published = peers * (borders + TILE)
    phase = lax.axis_index("phase")
    wanted = pull_slots[0].T
    codes = rulebook.T
    own = weights[0]
    swap = [(0, 1), (1, 0)]
    other = lax.ppermute(own, "phase", swap)

    anywhere = pl.BlockSpec(memory_space=pl.ANY)
    array = jax.ShapeDtypeStruct
    block = array((rows, channels), BF16)
    total_like = array((rows, channels), F32)
    published_like = array((published, channels), BF16)
    sent_like = array((peers * TILE, channels), BF16)
    onehot_like = array((rows, groups * pack * slots), BF16)
    places_like = array((slots + peers * TILE, 128), I32)
    weights_like = array(own.shape, BF16)
    picked_like = array((rows, offsets * channels), BF16)
    spread_like = array((groups * pack * slots, channels), BF16)

    def call(kernel, name, args, out_shapes, scratch, flops):
        return pl.pallas_call(
            kernel,
            in_specs=[anywhere] * len(args),
            out_specs=[anywhere] * len(out_shapes),
            out_shape=out_shapes,
            scratch_shapes=[pltpu.VMEM(s.shape, s.dtype) for s in scratch] + [pltpu.SemaphoreType.DMA((12,))],
            compiler_params=pltpu.CompilerParams(vmem_limit_bytes=VMEM_BYTES),
            cost_estimate=pl.CostEstimate(flops=flops, bytes_accessed=10**6, transcendentals=0),
            name=name,
        )(*args)

    def exchange(value):
        return lax.all_to_all(value, "space", 0, 0, tiled=True)

    local_flops = 2 * offsets * rows * channels * (rows + channels)
    payload, = call(
        publish_kernel, "publish", (features, border, wanted), [published_like],
        [block, border, wanted, published_like], 10**8,
    )
    received = exchange(payload)
    total, halo_onehot, places = call(
        functools.partial(first_local_kernel, borders), "first_local", (features, codes, wanted, own, other),
        [total_like, onehot_like, places_like],
        [block, codes, wanted, weights_like, picked_like, total_like, onehot_like, places_like], local_flops,
    )
    latent, normed, send = call(
        encode_kernel, "encode",
        (features, total, received, halo_onehot, places, border, conv_bias, own, other), [block, block, sent_like],
        [block, total_like, published_like, onehot_like, places_like, border, conv_bias, weights_like, spread_like,
         block, block, sent_like], 10**9,
    )
    received = exchange(send)
    total, = call(
        second_local_kernel, "second_local", (normed, codes, own, other), [total_like],
        [block, codes, weights_like, picked_like, total_like], local_flops,
    )
    kept, passed = call(
        functools.partial(decode_kernel, cap), "decode",
        (latent, total, received, halo_onehot, conv_bias, own, other), [array((2, rows, channels), BF16), block],
        [block, total_like, sent_like, onehot_like, conv_bias, weights_like, spread_like, block], 10**9,
    )
    got = lax.ppermute(passed, "phase", swap)
    return lax.dynamic_update_slice(kept, got[None], (1 - phase, 0, 0))[None]


def solution(mesh):
    return jax.shard_map(
        body,
        mesh=mesh,
        in_specs=(
            P(None, "space", None),
            P("phase", None, None, None),
            P(),
            P("space", None),
            P("space", None),
            P("space", None, None),
        ),
        out_specs=P("phase", None, "space", None),
        check_vma=False,
    )
```

time: 54.5 us -> 52.4 us (0.961)
  waiting for transfers between devices: 3.68 us -> 8.4 us
  Pallas kernels: 32.2 us -> 27.6 us
  local copies, waits for them, and re-layouts: 4.8 us -> 3.1 us
    all_to_all x2, waiting for transfers between devices: 1.95 us -> 6.67 us  [exchange(): return lax.all_to_all(value, 'space', 0, 0, tiled=True)]
    pallas_call x5, Pallas kernels: 32.2 us -> 27.6 us  [call(): pl.pallas_call(kernel, in_specs=[anywhere] * len(args), out_specs=[anywhe...]
    unnamed x5 -> x4, local copies, waits for them, and re-layouts: 4.08 us -> 2.38 us
  transfers between devices with their start and end apart: 4 -> 4, of which waited for: 2 -> 2; matrix products, arithmetic and copies ran while one was open for 3% -> 0% of each run, Pallas kernels for 43% -> 35%
where the time goes in v4:
time: 52.4 us; the launch traced here: 52.2 us
  Pallas kernels  27.6 us (53%)
  starting transfers between devices  13 us (25%)
  waiting for transfers between devices  8.4 us (16%)
  local copies, waits for them, and re-layouts  3.1 us (6%)
    pallas_call x5, Pallas kernels, call(): pl.pallas_call(kernel, in_specs=[anywhere] * len(args), out_specs=[anywhe...  27.6 us
    all_to_all x2, starting transfers between devices, exchange(): return lax.all_to_all(value, 'space', 0, 0, tiled=True)  12.5 us
    all_to_all x2, waiting for transfers between devices, exchange(): return lax.all_to_all(value, 'space', 0, 0, tiled=True)  6.67 us
    unnamed x4, local copies, waits for them, and re-layouts  2.38 us
    ppermute x1, waiting for transfers between devices, body(): got = lax.ppermute(passed, 'phase', swap)  1.73 us
  transfers between devices with their start and end apart: 4, of which 2 were waited for; matrix products, arithmetic and copies ran while one was open for 0% of the time, Pallas kernels for 35%

profile of v4, /device:TPU:0, one launch (start us, length us, event | category | flops | bytes accessed | tf_op | source)
XLA Modules:
  0.0 52.2 jit_solution(3458932786577653290)
XLA Ops:
  0.0 0.5 collective-permute-start
  0.5 2.2 %publish.1 = bf16[1152,256]{1,0:T(8,128)(2,1)} custom-call(bf16[2,512,256]{2,1,0:T(8,128)(2,1)} %features_ref.5, s32[1,64]{1,0:T(1,128)} %border_ref.3, s32[4,16]{1,0:T(4,128)} %bitcast.20), custom_call_target="tpu_custom_call" | custom-call | flops 100000000 | bytes 1000000 | tf_op jit(solution)/shard_map/publish/pallas_call | solution.py:325
  2.7 7.9 %all-to-all-start = ((bf16[16,72,256]{2,1,0:T(8,128)(2,1)}), bf16[16,72,256]{2,1,0:T(8,128)(2,1)}, u32[]{:S(2)}, u32[]{:S(2)}) async-start(bf16[16,72,256]{2,1,0:T(8,128)(2,1)} %bitcast.17), calls=%async_computation | async-start | bytes 1179648 | tf_op jit(solution)/shard_map/all_to_all | solution.py:337
  10.6 0.0 collective-permute-done.other_ref
  10.6 0.0 copy-start
  10.7 1.7 %copy-done = bf16[27,256,256]{2,1,0:T(8,128)(2,1)} copy-done((bf16[27,256,256]{2,1,0:T(8,128)(2,1)}, bf16[27,256,256]{2,1,0:T(8,128)(2,1)S(1)}, u32[]{:S(2)}) %copy-start) | copy-done | bytes 3538968
  12.4 8.2 %first_local.1 = (f32[512,256]{1,0:T(8,128)}, bf16[512,1792]{1,0:T(8,128)(2,1)}, s32[192,128]{1,0:T(8,128)}) custom-call(bf16[2,512,256]{2,1,0:T(8,128)(2,1)} %features_ref.5, s32[27,512]{1,0:T(8,128)} %bitcast.23, s32[4,16]{1,0:T(4,128)} %bitcast.21, bf16[27,256,256]{2,1,0:T(8,128)(2,1)} %bitcast.13, bf16[27,256,256]{2,1,0:T(8,128)(2,1)} %copy-done), custom_call_target="tpu_custom_call" | custom-call | flops 5435817984 | bytes 1000000 | tf_op jit(solution)/shard_map/first_local/pallas_call | solution.py:325
  20.6 6.7 %all-to-all-done = bf16[16,72,256]{2,1,0:T(8,128)(2,1)} async-done(((bf16[16,72,256]{2,1,0:T(8,128)(2,1)}), bf16[16,72,256]{2,1,0:T(8,128)(2,1)}, u32[]{:S(2)}, u32[]{:S(2)}) %all-to-all-start) | async-done | bytes 589856 | tf_op jit(solution)/shard_map/all_to_all | solution.py:337
  27.3 4.8 %encode.1 = (bf16[512,256]{1,0:T(8,128)(2,1)}, bf16[512,256]{1,0:T(8,128)(2,1)}, bf16[128,256]{1,0:T(8,128)(2,1)}) custom-call(bf16[2,512,256]{2,1,0:T(8,128)(2,1)} %features_ref.5, f32[512,256]{1,0:T(8,128)} %get-tuple-element.13.total_ref, bf16[1152,256]{1,0:T(8,128)(2,1)} %bitcast.6.received_ref, bf16[512,1792]{1,0:T(8,128)(2,1)} %get-tuple-element.14.halo_onehot_ref, ...), custom_call_target="tpu_custom_call" | custom-call | flops 1000000000 | bytes 1000000 | tf_op jit(solution)/shard_map/encode/pallas_call | solution.py:325
  32.1 4.5 %all-to-all-start.1 = ((bf16[16,8,256]{2,1,0:T(8,128)(2,1)}), bf16[16,8,256]{2,1,0:T(8,128)(2,1)S(1)}, u32[]{:S(2)}, u32[]{:S(2)}) async-start(bf16[16,8,256]{2,1,0:T(8,128)(2,1)} %bitcast.19), calls=%async_computation.1 | async-start | bytes 131072 | tf_op jit(solution)/shard_map/all_to_all | solution.py:337
  36.6 8.1 %second_local.1.total_ref = f32[512,256]{1,0:T(8,128)} custom-call(bf16[512,256]{1,0:T(8,128)(2,1)} %get-tuple-element.17.normed_ref, s32[27,512]{1,0:T(8,128)} %bitcast.24, bf16[27,256,256]{2,1,0:T(8,128)(2,1)} %bitcast.15, bf16[27,256,256]{2,1,0:T(8,128)(2,1)} %copy-done), custom_call_target="tpu_custom_call" | custom-call | flops 5435817984 | bytes 1000000 | tf_op jit(solution)/shard_map/second_local/pallas_call | solution.py:325
  44.7 0.0 all-to-all-done.1
  44.7 0.0 copy-start.1
  44.7 0.6 %copy-done.1 = bf16[16,8,256]{2,1,0:T(8,128)(2,1)} copy-done((bf16[16,8,256]{2,1,0:T(8,128)(2,1)}, bf16[16,8,256]{2,1,0:T(8,128)(2,1)S(1)}, u32[]{:S(2)}) %copy-start.1) | copy-done | bytes 65560
  45.4 4.3 %decode.1 = (bf16[2,512,256]{2,1,0:T(8,128)(2,1)}, bf16[512,256]{1,0:T(8,128)(2,1)}) custom-call(bf16[512,256]{1,0:T(8,128)(2,1)} %get-tuple-element.16.latent_ref, f32[512,256]{1,0:T(8,128)} %second_local.1.total_ref, bf16[128,256]{1,0:T(8,128)(2,1)} %bitcast.18, bf16[512,1792]{1,0:T(8,128)(2,1)} %get-tuple-element.14.halo_onehot_ref, f32[2,256]{1,0:T(2,128)} %bias_ref.3, ...), custom_call_target="tpu_custom_call" | custom-call | flops 1000000000 | bytes 1000000 | tf_op jit(solution)/shard_map/decode/pallas_call | solution.py:325
  49.6 0.1 collective-permute-start.1
  49.7 1.7 %collective-permute-done.1 = bf16[512,256]{1,0:T(8,128)(2,1)S(1)} collective-permute-done((bf16[512,256]{1,0:T(8,128)(2,1)}, bf16[512,256]{1,0:T(8,128)(2,1)S(1)}, u32[]{:S(2)}, u32[]{:S(2)}) %collective-permute-start.1) | collective-permute-done | bytes 262176 | tf_op jit(solution)/shard_map/ppermute | solution.py:366
  51.4 0.7 %bitcast_dynamic-update-slice_fusion = bf16[1,2,512,256]{3,2,1,0:T(8,128)(2,1)} fusion(bf16[1,2,512,256]{3,2,1,0:T(8,128)(2,1)} %bitcast.22, s32[]{:T(128)S(6)} %select_n.3, bf16[512,256]{1,0:T(8,128)(2,1)S(1)} %collective-permute-done.1), kind=kLoop, calls=%fused_computation | loop fusion | bytes 524292 | tf_op jit(solution)/shard_map/dynamic_update_slice | solution.py:367
Async XLA Ops:
  0.0 10.6 %collective-permute-start = (bf16[27,256,256]{2,1,0:T(8,128)(2,1)}, bf16[27,256,256]{2,1,0:T(8,128)(2,1)S(1)}, u32[]{:S(2)}, u32[]{:S(2)}) collective-permute-start(bf16[27,256,256]{2,1,0:T(8,128)(2,1)} %bitcast.12), channel_id=1, source_target_pairs={{0,16},{16,0},{1,17},{17,1},{2,18},{18,2},{3,19},{19,3},{4,20},{20... | collective-permute-start | bytes 10616840 | tf_op jit(solution)/shard_map/ppermute | solution.py:310
  2.7 24.6 %all-to-all-start = ((bf16[16,72,256]{2,1,0:T(8,128)(2,1)}), bf16[16,72,256]{2,1,0:T(8,128)(2,1)}, u32[]{:S(2)}, u32[]{:S(2)}) async-start(bf16[16,72,256]{2,1,0:T(8,128)(2,1)} %bitcast.17), calls=%async_computation | async-start | bytes 1179648 | tf_op jit(solution)/shard_map/all_to_all | solution.py:337
  10.6 1.8 %copy-start = (bf16[27,256,256]{2,1,0:T(8,128)(2,1)}, bf16[27,256,256]{2,1,0:T(8,128)(2,1)S(1)}, u32[]{:S(2)}) copy-start(bf16[27,256,256]{2,1,0:T(8,128)(2,1)S(1)} %collective-permute-done.other_ref) | copy-start | bytes 10616836
  32.1 12.6 %all-to-all-start.1 = ((bf16[16,8,256]{2,1,0:T(8,128)(2,1)}), bf16[16,8,256]{2,1,0:T(8,128)(2,1)S(1)}, u32[]{:S(2)}, u32[]{:S(2)}) async-start(bf16[16,8,256]{2,1,0:T(8,128)(2,1)} %bitcast.19), calls=%async_computation.1 | async-start | bytes 131072 | tf_op jit(solution)/shard_map/all_to_all | solution.py:337
  44.7 0.6 %copy-start.1 = (bf16[16,8,256]{2,1,0:T(8,128)(2,1)}, bf16[16,8,256]{2,1,0:T(8,128)(2,1)S(1)}, u32[]{:S(2)}) copy-start(bf16[16,8,256]{2,1,0:T(8,128)(2,1)S(1)} %all-to-all-done.1) | copy-start | bytes 196612
  49.6 1.8 %collective-permute-start.1 = (bf16[512,256]{1,0:T(8,128)(2,1)}, bf16[512,256]{1,0:T(8,128)(2,1)S(1)}, u32[]{:S(2)}, u32[]{:S(2)}) collective-permute-start(bf16[512,256]{1,0:T(8,128)(2,1)} %get-tuple-element.20), channel_id=1, source_target_pairs={{0,16},{16,0},{1,17},{17,1},{2,18},{18,2},{3,19},{19,3},{4,20},{20... | collective-permute-start | bytes 786440 | tf_op jit(solution)/shard_map/ppermute | solution.py:366

commit v5 on v4

--- a/solution.py
+++ b/solution.py
@@ -63,7 +63,9 @@
         return copy
 
 
-def publish_kernel(features_ref, border_ref, wanted_ref, payload_ref, block_ref, border_v, wanted_v, payload_v, sems):
+def publish_kernel(
+    features_ref, border_ref, wanted_ref, shown_ref, payload_ref, block_ref, border_v, wanted_v, aux_ref, shown_v, sems
+):
     copies = Copies(sems)
     loads = [
         copies.start(features_ref.at[lax.axis_index("phase")], block_ref),
@@ -72,21 +74,17 @@
     ]
     for load in loads:
         load.wait()
-    borders = border_v.shape[1]
     cap, peers = wanted_v.shape
-    rows, channels = block_ref.shape
-    place = lookup(iota((borders, 1), 0), border_v[...])
-    picked = dot(onehot(place, rows), block_ref[...])
-    shown = normalise(picked).astype(F32)
-    stride = borders + TILE
-    pad = jnp.zeros((TILE - cap, channels), F32)
-    wanted = wanted_v[...].astype(F32)
-    for peer in range(0, peers, 2):
-        parts = []
-        for each in (peer, peer + 1):
-            parts += [shown, jnp.concatenate([jnp.broadcast_to(wanted[:, each : each + 1], (cap, channels)), pad], axis=0)]
-        payload_v[peer * stride : (peer + 2) * stride, :] = jnp.concatenate(parts, axis=0).astype(BF16)
-    copies.start(payload_v, payload_ref).wait()
+    place = lookup(iota((border_v.shape[1], 1), 0), border_v[...])
+    picked = dot(onehot(place, block_ref.shape[0]), block_ref[...])
+    aux_ref[...] = jnp.zeros_like(aux_ref)
+    aux_ref[0:cap, 0:peers] = wanted_v[...].astype(F32)
+    shown_v[...] = jnp.concatenate([normalise(picked).astype(F32), aux_ref[...]], axis=0).astype(BF16)
+    stores = [copies.start(shown_v, shown_ref)]
+    for member in range(payload_ref.shape[0]):
+        stores.append(copies.start(shown_v, payload_ref.at[member, 0]))
+    for store in stores:
+        store.wait()
 
 
 def gather(codes, normed, picked_v, beside=lambda k: None):
@@ -126,14 +124,21 @@
 
 def published_places(wanted, borders):
     cap, peers = wanted.shape
-    stride = borders + TILE
+    half = peers // 2
+    upper_here = (lax.axis_index("space") >= half).astype(I32)
+
+    def block_start(peer):
+        upper = (peer >= half).astype(I32)
+        across = (upper != upper_here).astype(I32)
+        return ((peer - half * upper) * 2 + across) * (borders + TILE)
+
     peer, slot = slot_numbers(peers * cap, cap, cap)
     mine = lax.dot_general(
         onehot(peer, peers), wanted.astype(BF16), (((1,), (1,)), ((), ())), preferred_element_type=F32
     )
     mine = jnp.sum(jnp.where(iota(mine.shape, 1) == slot, mine, 0.0), axis=1, keepdims=True).astype(I32)
     asker, place = slot_numbers(peers * TILE, TILE, cap)
-    return jnp.concatenate([peer * stride + mine, asker * stride + borders + place], axis=0)
+    return jnp.concatenate([block_start(peer) + mine, block_start(asker) + borders + place], axis=0)
 
 
 def first_local_kernel(
@@ -228,7 +233,8 @@
         load.wait()
     slots = places_v.shape[0] - send_v.shape[0]
     found = pick_rows(places_v[:, 0:1], received_v)
-    asked = lookup(found[slots:, 0:1].astype(I32), border_v[...])
+    theirs = jnp.where(iota((send_v.shape[0], found.shape[1]), 1) == lax.axis_index("space"), found[slots:], 0.0)
+    asked = lookup(jnp.sum(theirs, axis=1, keepdims=True).astype(I32), border_v[...])
     weights_load.wait()
     spread_halo(found[:slots].astype(BF16), held_ref, spread_ref)
     for load in late:
@@ -300,6 +306,7 @@
     borders = border.shape[1]
     offsets = rulebook.shape[1]
     slots = peers * cap
+    half = peers // 2
     pack, groups = packing(slots, offsets)
     published = peers * (borders + TILE)
     phase = lax.axis_index("phase")
@@ -314,6 +321,7 @@
     block = array((rows, channels), BF16)
     total_like = array((rows, channels), F32)
     published_like = array((published, channels), BF16)
+    shown_like = array((borders + TILE, channels), BF16)
     sent_like = array((peers * TILE, channels), BF16)
     onehot_like = array((rows, groups * pack * slots), BF16)
     places_like = array((slots + peers * TILE, 128), I32)
@@ -327,21 +335,26 @@
             in_specs=[anywhere] * len(args),
             out_specs=[anywhere] * len(out_shapes),
             out_shape=out_shapes,
-            scratch_shapes=[pltpu.VMEM(s.shape, s.dtype) for s in scratch] + [pltpu.SemaphoreType.DMA((12,))],
+            scratch_shapes=[pltpu.VMEM(s.shape, s.dtype) for s in scratch] + [pltpu.SemaphoreType.DMA((max(12, half + 4),))],
             compiler_params=pltpu.CompilerParams(vmem_limit_bytes=VMEM_BYTES),
             cost_estimate=pl.CostEstimate(flops=flops, bytes_accessed=10**6, transcendentals=0),
             name=name,
         )(*args)
 
-    def exchange(value):
-        return lax.all_to_all(value, "space", 0, 0, tiled=True)
+    def exchange(value, groups=None):
+        return lax.all_to_all(value, "space", 0, 0, tiled=True, axis_index_groups=groups)
 
     local_flops = 2 * offsets * rows * channels * (rows + channels)
-    payload, = call(
-        publish_kernel, "publish", (features, border, wanted), [published_like],
-        [block, border, wanted, published_like], 10**8,
-    )
-    received = exchange(payload)
+    shown, payload = call(
+        publish_kernel, "publish", (features, border, wanted), [shown_like, array((half, 2, *shown_like.shape), BF16)],
+        [block, border, wanted, array((TILE, channels), F32), shown_like], 10**8,
+    )
+    across = lax.ppermute(shown, "space", [(place, (place + half) % peers) for place in range(peers)])
+    payload = lax.dynamic_update_slice(
+        payload, jnp.broadcast_to(across, (half, 1, *across.shape)), (0, 1, 0, 0)
+    ).reshape(published, channels)
+    payload, other = lax.optimization_barrier((payload, other))
+    received = exchange(payload, [list(range(half)), list(range(half, peers))])
     total, halo_onehot, places = call(
         functools.partial(first_local_kernel, borders), "first_local", (features, codes, wanted, own, other),
         [total_like, onehot_like, places_like],

time: 52.4 us -> 50.8 us (0.969)
  waiting for transfers between devices: 8.4 us -> 5.68 us
  starting transfers between devices: 13 us -> 15.3 us
  local copies, waits for them, and re-layouts: 3.1 us -> 2.1 us
    all_to_all x2, waiting for transfers between devices: 6.67 us -> 1.59 us  [exchange(): lax.all_to_all(value, 'space', 0, 0, tiled=True, axis_index_groups=groups)]
    ppermute x0 -> x1, starting transfers between devices: none -> 3.65 us  [body(): lax.ppermute(shown, 'space', [(place, (place + half) % peers) for place i...]
    ppermute x0 -> x1, waiting for transfers between devices: none -> 2.36 us  [body(): lax.ppermute(shown, 'space', [(place, (place + half) % peers) for place i...]
    unnamed x4, local copies, waits for them, and re-layouts: 2.38 us -> 0.63 us
    all_to_all x2, starting transfers between devices: 12.5 us -> 11.1 us  [exchange(): lax.all_to_all(value, 'space', 0, 0, tiled=True, axis_index_groups=groups)]
    dynamic_update_slice x0 -> x1, local copies, waits for them, and re-layouts: none -> 0.75 us  [body(): lax.dynamic_update_slice(payload, jnp.broadcast_to(across, (half, 1, *acr...]
  transfers between devices with their start and end apart: 4 -> 5, of which waited for: 2 -> 3; matrix products, arithmetic and copies ran while one was open for 0% -> 1% of each run, Pallas kernels for 35% -> 36%
where the time goes in v5:
time: 50.8 us; the launch traced here: 50.6 us
  Pallas kernels  27.4 us (54%)
  starting transfers between devices  15.3 us (30%)
  waiting for transfers between devices  5.68 us (11%)
  local copies, waits for them, and re-layouts  2.1 us (4%)
    pallas_call x5, Pallas kernels, call(): pl.pallas_call(kernel, in_specs=[anywhere] * len(args), out_specs=[anywhe...  27.4 us
    all_to_all x2, starting transfers between devices, exchange(): lax.all_to_all(value, 'space', 0, 0, tiled=True, axis_index_groups=groups)  11.1 us
    ppermute x1, starting transfers between devices, body(): lax.ppermute(shown, 'space', [(place, (place + half) % peers) for place i...  3.65 us
    ppermute x1, waiting for transfers between devices, body(): lax.ppermute(shown, 'space', [(place, (place + half) % peers) for place i...  2.36 us
    ppermute x1, waiting for transfers between devices, body(): got = lax.ppermute(passed, 'phase', swap)  1.73 us
    all_to_all x2, waiting for transfers between devices, exchange(): lax.all_to_all(value, 'space', 0, 0, tiled=True, axis_index_groups=groups)  1.59 us
  transfers between devices with their start and end apart: 5, of which 3 were waited for; matrix products, arithmetic and copies ran while one was open for 1% of the time, Pallas kernels for 36%

profile of v5, /device:TPU:0, one launch (start us, length us, event | category | flops | bytes accessed | tf_op | source)
XLA Modules:
  0.0 50.6 jit_solution(565619861950974598)
XLA Ops:
  0.0 0.5 collective-permute-start.1
  0.5 2.1 %publish.1 = (bf16[72,256]{1,0:T(8,128)(2,1)}, bf16[8,2,72,256]{3,2,1,0:T(8,128)(2,1)}) custom-call(bf16[2,512,256]{2,1,0:T(8,128)(2,1)} %features_ref.5, s32[1,64]{1,0:T(1,128)} %border_ref.3, s32[4,16]{1,0:T(4,128)} %bitcast.21), custom_call_target="tpu_custom_call" | custom-call | flops 100000000 | bytes 1000000 | tf_op jit(solution)/shard_map/publish/pallas_call | solution.py:333
  2.5 3.7 %collective-permute-start = (bf16[72,256]{1,0:T(8,128)(2,1)}, bf16[72,256]{1,0:T(8,128)(2,1)S(1)}, u32[]{:S(2)}, u32[]{:S(2)}) collective-permute-start(bf16[72,256]{1,0:T(8,128)(2,1)} %get-tuple-element.18), channel_id=1, source_target_pairs={{0,8},{1,9},{2,10},{3,11},{4,12},{5,13},{6,14},{7,15},{8,0},{9,1},... | collective-permute-start | bytes 110600 | tf_op jit(solution)/shard_map/ppermute | solution.py:352
  6.2 2.4 %collective-permute-done = bf16[72,256]{1,0:T(8,128)(2,1)S(1)} collective-permute-done((bf16[72,256]{1,0:T(8,128)(2,1)}, bf16[72,256]{1,0:T(8,128)(2,1)S(1)}, u32[]{:S(2)}, u32[]{:S(2)}) %collective-permute-start) | collective-permute-done | bytes 36896 | tf_op jit(solution)/shard_map/ppermute | solution.py:352
  8.6 0.7 %broadcast_dynamic-update-slice_fusion = bf16[8,2,72,256]{3,2,1,0:T(8,128)(2,1)} fusion(bf16[8,2,72,256]{3,2,1,0:T(8,128)(2,1)} %get-tuple-element.17, bf16[72,256]{1,0:T(8,128)(2,1)S(1)} %collective-permute-done), kind=kLoop, calls=%fused_computation.1 | loop fusion | bytes 331776 | tf_op jit(solution)/shard_map/dynamic_update_slice | solution.py:353
  9.3 0.0 collective-permute-done.1.other_ref
  9.3 0.0 copy-start
  9.3 4.9 %all-to-all-start = ((bf16[8,144,256]{2,1,0:T(8,128)(2,1)}), bf16[8,144,256]{2,1,0:T(8,128)(2,1)}, u32[]{:S(2)}, u32[]{:S(2)}) async-start(bf16[8,144,256]{2,1,0:T(8,128)(2,1)} %bitcast.18), calls=%async_computation | async-start | bytes 1179648 | tf_op jit(solution)/shard_map/all_to_all | solution.py:345
  14.2 0.0 copy-done
  14.2 8.2 %first_local.1 = (f32[512,256]{1,0:T(8,128)}, bf16[512,1792]{1,0:T(8,128)(2,1)}, s32[192,128]{1,0:T(8,128)}) custom-call(bf16[2,512,256]{2,1,0:T(8,128)(2,1)} %features_ref.5, s32[27,512]{1,0:T(8,128)} %bitcast.24, s32[4,16]{1,0:T(4,128)} %bitcast.22, bf16[27,256,256]{2,1,0:T(8,128)(2,1)} %bitcast.14, bf16[27,256,256]{2,1,0:T(8,128)(2,1)} %copy-done), custom_call_target="tpu_custom_call" | custom-call | flops 5435817984 | bytes 1000000 | tf_op jit(solution)/shard_map/first_local/pallas_call | solution.py:333
  22.4 1.6 %all-to-all-done = bf16[8,144,256]{2,1,0:T(8,128)(2,1)} async-done(((bf16[8,144,256]{2,1,0:T(8,128)(2,1)}), bf16[8,144,256]{2,1,0:T(8,128)(2,1)}, u32[]{:S(2)}, u32[]{:S(2)}) %all-to-all-start) | async-done | bytes 589856 | tf_op jit(solution)/shard_map/all_to_all | solution.py:345
  24.0 4.8 %encode.1 = (bf16[512,256]{1,0:T(8,128)(2,1)}, bf16[512,256]{1,0:T(8,128)(2,1)}, bf16[128,256]{1,0:T(8,128)(2,1)}) custom-call(bf16[2,512,256]{2,1,0:T(8,128)(2,1)} %features_ref.5, f32[512,256]{1,0:T(8,128)} %get-tuple-element.20.total_ref, bf16[1152,256]{1,0:T(8,128)(2,1)} %bitcast.7.received_ref, bf16[512,1792]{1,0:T(8,128)(2,1)} %get-tuple-element.22.halo_onehot_ref, ...), custom_call_target="tpu_custom_call" | custom-call | flops 1000000000 | bytes 1000000 | tf_op jit(solution)/shard_map/encode/pallas_call | solution.py:333
  28.8 6.3 %all-to-all-start.1 = ((bf16[16,8,256]{2,1,0:T(8,128)(2,1)}), bf16[16,8,256]{2,1,0:T(8,128)(2,1)S(1)}, u32[]{:S(2)}, u32[]{:S(2)}) async-start(bf16[16,8,256]{2,1,0:T(8,128)(2,1)} %bitcast.20), calls=%async_computation.1 | async-start | bytes 131072 | tf_op jit(solution)/shard_map/all_to_all | solution.py:345
  35.1 8.0 %second_local.1.total_ref = f32[512,256]{1,0:T(8,128)} custom-call(bf16[512,256]{1,0:T(8,128)(2,1)} %get-tuple-element.25.normed_ref, s32[27,512]{1,0:T(8,128)} %bitcast.25, bf16[27,256,256]{2,1,0:T(8,128)(2,1)} %bitcast.16, bf16[27,256,256]{2,1,0:T(8,128)(2,1)} %copy-done), custom_call_target="tpu_custom_call" | custom-call | flops 5435817984 | bytes 1000000 | tf_op jit(solution)/shard_map/second_local/pallas_call | solution.py:333
  43.1 0.0 all-to-all-done.1
  43.1 0.0 copy-start.1
  43.1 0.6 %copy-done.1 = bf16[16,8,256]{2,1,0:T(8,128)(2,1)} copy-done((bf16[16,8,256]{2,1,0:T(8,128)(2,1)}, bf16[16,8,256]{2,1,0:T(8,128)(2,1)S(1)}, u32[]{:S(2)}) %copy-start.1) | copy-done | bytes 65560
  43.8 4.3 %decode.1 = (bf16[2,512,256]{2,1,0:T(8,128)(2,1)}, bf16[512,256]{1,0:T(8,128)(2,1)}) custom-call(bf16[512,256]{1,0:T(8,128)(2,1)} %get-tuple-element.24.latent_ref, f32[512,256]{1,0:T(8,128)} %second_local.1.total_ref, bf16[128,256]{1,0:T(8,128)(2,1)} %bitcast.19, bf16[512,1792]{1,0:T(8,128)(2,1)} %get-tuple-element.22.halo_onehot_ref, f32[2,256]{1,0:T(2,128)} %bias_ref.3, ...), custom_call_target="tpu_custom_call" | custom-call | flops 1000000000 | bytes 1000000 | tf_op jit(solution)/shard_map/decode/pallas_call | solution.py:333
  48.0 0.1 collective-permute-start.2
  48.1 1.7 %collective-permute-done.2 = bf16[512,256]{1,0:T(8,128)(2,1)S(1)} collective-permute-done((bf16[512,256]{1,0:T(8,128)(2,1)}, bf16[512,256]{1,0:T(8,128)(2,1)S(1)}, u32[]{:S(2)}, u32[]{:S(2)}) %collective-permute-start.2) | collective-permute-done | bytes 262176 | tf_op jit(solution)/shard_map/ppermute | solution.py:379
  49.8 0.7 %bitcast_dynamic-update-slice_fusion = bf16[1,2,512,256]{3,2,1,0:T(8,128)(2,1)} fusion(bf16[1,2,512,256]{3,2,1,0:T(8,128)(2,1)} %bitcast.23, s32[]{:T(128)S(6)} %select_n.3, bf16[512,256]{1,0:T(8,128)(2,1)S(1)} %collective-permute-done.2), kind=kLoop, calls=%fused_computation | loop fusion | bytes 524292 | tf_op jit(solution)/shard_map/dynamic_update_slice | solution.py:380
Async XLA Ops:
  0.0 9.3 %collective-permute-start.1 = (bf16[27,256,256]{2,1,0:T(8,128)(2,1)}, bf16[27,256,256]{2,1,0:T(8,128)(2,1)S(1)}, u32[]{:S(2)}, u32[]{:S(2)}) collective-permute-start(bf16[27,256,256]{2,1,0:T(8,128)(2,1)} %bitcast.13), channel_id=1, source_target_pairs={{0,16},{16,0},{1,17},{17,1},{2,18},{18,2},{3,19},{19,3},{4,20},{20... | collective-permute-start | bytes 10616840 | tf_op jit(solution)/shard_map/ppermute | solution.py:317
  2.5 6.0 %collective-permute-start = (bf16[72,256]{1,0:T(8,128)(2,1)}, bf16[72,256]{1,0:T(8,128)(2,1)S(1)}, u32[]{:S(2)}, u32[]{:S(2)}) collective-permute-start(bf16[72,256]{1,0:T(8,128)(2,1)} %get-tuple-element.18), channel_id=1, source_target_pairs={{0,8},{1,9},{2,10},{3,11},{4,12},{5,13},{6,14},{7,15},{8,0},{9,1},... | collective-permute-start | bytes 110600 | tf_op jit(solution)/shard_map/ppermute | solution.py:352
  9.3 4.9 %copy-start = (bf16[27,256,256]{2,1,0:T(8,128)(2,1)}, bf16[27,256,256]{2,1,0:T(8,128)(2,1)S(1)}, u32[]{:S(2)}) copy-start(bf16[27,256,256]{2,1,0:T(8,128)(2,1)S(1)} %collective-permute-done.1.other_ref) | copy-start | bytes 10616836
  9.3 14.7 %all-to-all-start = ((bf16[8,144,256]{2,1,0:T(8,128)(2,1)}), bf16[8,144,256]{2,1,0:T(8,128)(2,1)}, u32[]{:S(2)}, u32[]{:S(2)}) async-start(bf16[8,144,256]{2,1,0:T(8,128)(2,1)} %bitcast.18), calls=%async_computation | async-start | bytes 1179648 | tf_op jit(solution)/shard_map/all_to_all | solution.py:345
  28.8 14.3 %all-to-all-start.1 = ((bf16[16,8,256]{2,1,0:T(8,128)(2,1)}), bf16[16,8,256]{2,1,0:T(8,128)(2,1)S(1)}, u32[]{:S(2)}, u32[]{:S(2)}) async-start(bf16[16,8,256]{2,1,0:T(8,128)(2,1)} %bitcast.20), calls=%async_computation.1 | async-start | bytes 131072 | tf_op jit(solution)/shard_map/all_to_all | solution.py:345
  43.1 0.6 %copy-start.1 = (bf16[16,8,256]{2,1,0:T(8,128)(2,1)}, bf16[16,8,256]{2,1,0:T(8,128)(2,1)S(1)}, u32[]{:S(2)}) copy-start(bf16[16,8,256]{2,1,0:T(8,128)(2,1)S(1)} %all-to-all-done.1) | copy-start | bytes 196612
  48.0 1.8 %collective-permute-start.2 = (bf16[512,256]{1,0:T(8,128)(2,1)}, bf16[512,256]{1,0:T(8,128)(2,1)S(1)}, u32[]{:S(2)}, u32[]{:S(2)}) collective-permute-start(bf16[512,256]{1,0:T(8,128)(2,1)} %get-tuple-element.28), channel_id=1, source_target_pairs={{0,16},{16,0},{1,17},{17,1},{2,18},{18,2},{3,19},{19,3},{4,20},{20... | collective-permute-start | bytes 786440 | tf_op jit(solution)/shard_map/ppermute | solution.py:379

commit v6 on v5

--- a/solution.py
+++ b/solution.py
@@ -13,6 +13,8 @@
 TILE = 8
 BLOCK = 128
 VMEM_BYTES = 60 * 2**20
+DECODE_BYTES = 50 * 2**20
+PADDED_ROWS = 15 * 1024
 
 
 def iota(shape, dim):
@@ -89,8 +91,12 @@
 
 def gather(codes, normed, picked_v, beside=lambda k: None):
     rows, channels = normed.shape
-    for k in range(codes.shape[1]):
-        picked_v[:, k * channels : (k + 1) * channels] = dot(onehot(codes[:, k : k + 1], rows), normed).astype(BF16)
+    offsets = codes.shape[1]
+    for k in range(offsets):
+        if k == offsets // 2:
+            picked_v[:, k * channels : (k + 1) * channels] = normed
+        else:
+            picked_v[:, k * channels : (k + 1) * channels] = dot(onehot(codes[:, k : k + 1], rows), normed).astype(BF16)
         beside(k)
 
 
@@ -143,8 +149,8 @@
 
 def first_local_kernel(
     borders, features_ref, codes_ref, wanted_ref, own_ref, other_ref,
-    total_ref, halo_onehot_ref, places_ref,
-    block_ref, codes_v, wanted_v, held_ref, picked_v, total_v, halo_onehot_v, places_v, sems,
+    total_ref, halo_onehot_ref, places_ref, columns_ref,
+    block_ref, codes_v, wanted_v, held_ref, picked_v, total_v, halo_onehot_v, places_v, columns_v, sems,
 ):
     phase = lax.axis_index("phase")
     copies = Copies(sems)
@@ -157,6 +163,7 @@
     for load in loads:
         load.wait()
     codes = codes_v[...].T
+    columns_v[:, 0 : codes.shape[1]] = codes
     cap, peers = wanted_v.shape
     slots = peers * cap
     pack, groups = packing(slots, codes.shape[1])
@@ -167,7 +174,7 @@
             halo_onehot_group(codes, slots, k // pack, halo_onehot_v)
 
     gather(codes, normalise(block_ref[...].astype(F32)), picked_v, beside)
-    stores = [copies.start(places_v, places_ref), copies.start(halo_onehot_v, halo_onehot_ref)]
+    stores = [copies.start(places_v, places_ref), copies.start(columns_v, columns_ref), copies.start(halo_onehot_v, halo_onehot_ref)]
     weights_load.wait()
     for span, term in convolved_blocks(picked_v, held_ref):
         total_v[span, :] = term
@@ -261,7 +268,7 @@
     weights_load = copies.start_either(phase == 1, (own_ref, held_ref), (other_ref, held_ref))
     for load in early:
         load.wait()
-    gather(codes_v[...].T, normed_v[...], picked_v)
+    gather(codes_v[:, 0 : picked_v.shape[1] // normed_v.shape[1]], normed_v[...], picked_v)
     weights_load.wait()
     stores = []
     for span, term in convolved_blocks(picked_v, held_ref):
@@ -281,7 +288,7 @@
     weights_load = copies.start_either(first, (other_ref, held_ref), (own_ref, held_ref))
     late = [
         copies.start(halo_onehot_ref, halo_onehot_v),
-        copies.start(total_ref, total_v),
+        copies.start(total_ref.at[pl.ds(0, total_v.shape[0])], total_v),
         copies.start(latent_ref, latent_v),
         copies.start(bias_ref, bias_v),
     ]
@@ -325,18 +332,19 @@
     sent_like = array((peers * TILE, channels), BF16)
     onehot_like = array((rows, groups * pack * slots), BF16)
     places_like = array((slots + peers * TILE, 128), I32)
+    columns_like = array((rows, -(-offsets // 128) * 128), I32)
     weights_like = array(own.shape, BF16)
     picked_like = array((rows, offsets * channels), BF16)
     spread_like = array((groups * pack * slots, channels), BF16)
 
-    def call(kernel, name, args, out_shapes, scratch, flops):
+    def call(kernel, name, args, out_shapes, scratch, flops, limit=VMEM_BYTES):
         return pl.pallas_call(
             kernel,
             in_specs=[anywhere] * len(args),
             out_specs=[anywhere] * len(out_shapes),
             out_shape=out_shapes,
             scratch_shapes=[pltpu.VMEM(s.shape, s.dtype) for s in scratch] + [pltpu.SemaphoreType.DMA((max(12, half + 4),))],
-            compiler_params=pltpu.CompilerParams(vmem_limit_bytes=VMEM_BYTES),
+            compiler_params=pltpu.CompilerParams(vmem_limit_bytes=limit),
             cost_estimate=pl.CostEstimate(flops=flops, bytes_accessed=10**6, transcendentals=0),
             name=name,
         )(*args)
@@ -355,10 +363,10 @@
     ).reshape(published, channels)
     payload, other = lax.optimization_barrier((payload, other))
     received = exchange(payload, [list(range(half)), list(range(half, peers))])
-    total, halo_onehot, places = call(
+    total, halo_onehot, places, columns = call(
         functools.partial(first_local_kernel, borders), "first_local", (features, codes, wanted, own, other),
-        [total_like, onehot_like, places_like],
-        [block, codes, wanted, weights_like, picked_like, total_like, onehot_like, places_like], local_flops,
+        [total_like, onehot_like, places_like, columns_like],
+        [block, codes, wanted, weights_like, picked_like, total_like, onehot_like, places_like, columns_like], local_flops,
     )
     latent, normed, send = call(
         encode_kernel, "encode",
@@ -368,13 +376,13 @@
     )
     received = exchange(send)
     total, = call(
-        second_local_kernel, "second_local", (normed, codes, own, other), [total_like],
-        [block, codes, weights_like, picked_like, total_like], local_flops,
+        second_local_kernel, "second_local", (normed, columns, own, other), [array((max(rows, PADDED_ROWS), channels), F32)],
+        [block, columns_like, weights_like, picked_like, total_like], local_flops,
     )
     kept, passed = call(
         functools.partial(decode_kernel, cap), "decode",
         (latent, total, received, halo_onehot, conv_bias, own, other), [array((2, rows, channels), BF16), block],
-        [block, total_like, sent_like, onehot_like, conv_bias, weights_like, spread_like, block], 10**9,
+        [block, total_like, sent_like, onehot_like, conv_bias, weights_like, spread_like, block], 10**9, DECODE_BYTES,
     )
     got = lax.ppermute(passed, "phase", swap)
     return lax.dynamic_update_slice(kept, got[None], (1 - phase, 0, 0))[None]

time: 50.8 us -> 49.2 us (0.969)
  Pallas kernels: 27.4 us -> 26.5 us
  local copies, waits for them, and re-layouts: 2.1 us -> 1.51 us
    pallas_call x5, Pallas kernels: 27.4 us -> 26.5 us  [call(): pl.pallas_call(kernel, in_specs=[anywhere] * len(args), out_specs=[anywhe...]
    unnamed x4 -> x8, local copies, waits for them, and re-layouts: 0.63 us -> 0.02 us
  transfers between devices with their start and end apart: 5 -> 5, of which waited for: 3 -> 3; matrix products, arithmetic and copies ran while one was open for 1% -> 2% of each run, Pallas kernels for 36% -> 37%
where the time goes in v6:
time: 49.2 us; the launch traced here: 48.9 us
  Pallas kernels  26.5 us (54%)
  starting transfers between devices  15.2 us (31%)
  waiting for transfers between devices  5.57 us (11%)
  local copies, waits for them, and re-layouts  1.51 us (3%)
    pallas_call x5, Pallas kernels, call(): pl.pallas_call(kernel, in_specs=[anywhere] * len(args), out_specs=[anywhe...  26.5 us
    all_to_all x2, starting transfers between devices, exchange(): lax.all_to_all(value, 'space', 0, 0, tiled=True, axis_index_groups=groups)  11 us
    ppermute x1, starting transfers between devices, body(): lax.ppermute(shown, 'space', [(place, (place + half) % peers) for place i...  3.65 us
    ppermute x1, waiting for transfers between devices, body(): lax.ppermute(shown, 'space', [(place, (place + half) % peers) for place i...  2.36 us
    all_to_all x2, waiting for transfers between devices, exchange(): lax.all_to_all(value, 'space', 0, 0, tiled=True, axis_index_groups=groups)  1.69 us
    ppermute x1, waiting for transfers between devices, body(): got = lax.ppermute(passed, 'phase', swap)  1.52 us
  transfers between devices with their start and end apart: 5, of which 3 were waited for; matrix products, arithmetic and copies ran while one was open for 2% of the time, Pallas kernels for 37%

profile of v6, /device:TPU:0, one launch (start us, length us, event | category | flops | bytes accessed | tf_op | source)
XLA Modules:
  0.0 48.9 jit_solution(1580202620822444705)
XLA Ops:
  0.0 0.5 collective-permute-start.1
  0.5 2.1 %publish.1 = (bf16[72,256]{1,0:T(8,128)(2,1)}, bf16[8,2,72,256]{3,2,1,0:T(8,128)(2,1)}) custom-call(bf16[2,512,256]{2,1,0:T(8,128)(2,1)} %features_ref.5, s32[1,64]{1,0:T(1,128)} %border_ref.3, s32[4,16]{1,0:T(4,128)} %bitcast.21), custom_call_target="tpu_custom_call" | custom-call | flops 100000000 | bytes 1000000 | tf_op jit(solution)/shard_map/publish/pallas_call | solution.py:341
  2.5 3.7 %collective-permute-start = (bf16[72,256]{1,0:T(8,128)(2,1)}, bf16[72,256]{1,0:T(8,128)(2,1)S(1)}, u32[]{:S(2)}, u32[]{:S(2)}) collective-permute-start(bf16[72,256]{1,0:T(8,128)(2,1)} %get-tuple-element.19), channel_id=1, source_target_pairs={{0,8},{1,9},{2,10},{3,11},{4,12},{5,13},{6,14},{7,15},{8,0},{9,1},... | collective-permute-start | bytes 110600 | tf_op jit(solution)/shard_map/ppermute | solution.py:360
  6.2 2.4 %collective-permute-done = bf16[72,256]{1,0:T(8,128)(2,1)S(1)} collective-permute-done((bf16[72,256]{1,0:T(8,128)(2,1)}, bf16[72,256]{1,0:T(8,128)(2,1)S(1)}, u32[]{:S(2)}, u32[]{:S(2)}) %collective-permute-start) | collective-permute-done | bytes 36896 | tf_op jit(solution)/shard_map/ppermute | solution.py:360
  8.5 0.8 %broadcast_dynamic-update-slice_fusion = bf16[8,2,72,256]{3,2,1,0:T(8,128)(2,1)} fusion(bf16[8,2,72,256]{3,2,1,0:T(8,128)(2,1)} %get-tuple-element.18, bf16[72,256]{1,0:T(8,128)(2,1)S(1)} %collective-permute-done), kind=kLoop, calls=%fused_computation.1 | loop fusion | bytes 331776 | tf_op jit(solution)/shard_map/dynamic_update_slice | solution.py:361
  9.3 0.0 collective-permute-done.1.other_ref
  9.3 4.9 %all-to-all-start = ((bf16[8,144,256]{2,1,0:T(8,128)(2,1)}), bf16[8,144,256]{2,1,0:T(8,128)(2,1)}, u32[]{:S(2)}, u32[]{:S(2)}) async-start(bf16[8,144,256]{2,1,0:T(8,128)(2,1)} %bitcast.19), calls=%async_computation | async-start | bytes 1179648 | tf_op jit(solution)/shard_map/all_to_all | solution.py:353
  14.2 0.0 copy-done.3
  14.2 8.1 %first_local.1 = (f32[512,256]{1,0:T(8,128)}, bf16[512,1792]{1,0:T(8,128)(2,1)}, s32[192,128]{1,0:T(8,128)}, s32[512,128]{1,0:T(8,128)}) custom-call(bf16[2,512,256]{2,1,0:T(8,128)(2,1)} %features_ref.5, s32[27,512]{1,0:T(8,128)} %bitcast.24, s32[4,16]{1,0:T(4,128)} %bitcast.22, bf16[27,256,256]{2,1,0:T(8,128)(2,1)} %bitcast.15, bf16[27,256,256]{2,1,0:T(8,128)(2,1)} %copy-done.3), custom_call_target="tpu_custom_call" | custom-call | flops 5435817984 | bytes 1000000 | tf_op jit(solution)/shard_map/first_local/pallas_call | solution.py:341
  22.3 1.7 %all-to-all-done = bf16[8,144,256]{2,1,0:T(8,128)(2,1)} async-done(((bf16[8,144,256]{2,1,0:T(8,128)(2,1)}), bf16[8,144,256]{2,1,0:T(8,128)(2,1)}, u32[]{:S(2)}, u32[]{:S(2)}) %all-to-all-start) | async-done | bytes 589856 | tf_op jit(solution)/shard_map/all_to_all | solution.py:353
  24.0 4.8 %encode.1 = (bf16[512,256]{1,0:T(8,128)(2,1)}, bf16[512,256]{1,0:T(8,128)(2,1)}, bf16[128,256]{1,0:T(8,128)(2,1)}) custom-call(bf16[2,512,256]{2,1,0:T(8,128)(2,1)} %features_ref.5, f32[512,256]{1,0:T(8,128)} %get-tuple-element.21.total_ref, bf16[1152,256]{1,0:T(8,128)(2,1)} %bitcast.7.received_ref, bf16[512,1792]{1,0:T(8,128)(2,1)} %get-tuple-element.23.halo_onehot_ref, ...), custom_call_target="tpu_custom_call" | custom-call | flops 1000000000 | bytes 1000000 | tf_op jit(solution)/shard_map/encode/pallas_call | solution.py:341
  28.8 6.2 %all-to-all-start.1 = ((bf16[16,8,256]{2,1,0:T(8,128)(2,1)}), bf16[16,8,256]{2,1,0:T(8,128)(2,1)S(1)}, u32[]{:S(2)}, u32[]{:S(2)}) async-start(bf16[16,8,256]{2,1,0:T(8,128)(2,1)} %bitcast.20), calls=%async_computation.1 | async-start | bytes 131072 | tf_op jit(solution)/shard_map/all_to_all | solution.py:353
  35.0 0.0 copy-start
  35.0 0.0 copy-start.1
  35.0 0.0 copy-start.2
  35.0 7.8 %second_local.1.total_ref = f32[15360,256]{1,0:T(8,128)} custom-call(bf16[512,256]{1,0:T(8,128)(2,1)} %get-tuple-element.26.normed_ref, s32[512,128]{1,0:T(8,128)} %get-tuple-element.27.codes_ref, bf16[27,256,256]{2,1,0:T(8,128)(2,1)} %bitcast.17, bf16[27,256,256]{2,1,0:T(8,128)(2,1)} %copy-done.3), custom_call_target="tpu_custom_call" | custom-call | flops 5435817984 | bytes 1000000 | tf_op jit(solution)/shard_map/second_local/pallas_call | solution.py:341
  42.8 0.0 all-to-all-done.1
  42.9 0.0 copy-done
  42.9 0.0 copy-done.1
  42.9 0.0 copy-done.2
  42.9 3.7 %decode.1 = (bf16[2,512,256]{2,1,0:T(8,128)(2,1)}, bf16[512,256]{1,0:T(8,128)(2,1)S(1)}) custom-call(bf16[512,256]{1,0:T(8,128)(2,1)S(1)} %copy-done.1, f32[15360,256]{1,0:T(8,128)} %second_local.1.total_ref, bf16[128,256]{1,0:T(8,128)(2,1)S(1)} %bitcast.13, bf16[512,1792]{1,0:T(8,128)(2,1)S(1)} %copy-done, f32[2,256]{1,0:T(2,128)S(1)} %copy-done.2, ...), custom_call_target="tpu_custom_call" | custom-call | flops 1000000000 | bytes 1000000 | tf_op jit(solution)/shard_map/decode/pallas_call | solution.py:341
  46.6 0.1 collective-permute-start.2
  46.6 1.5 %collective-permute-done.2 = bf16[512,256]{1,0:T(8,128)(2,1)S(1)} collective-permute-done((bf16[512,256]{1,0:T(8,128)(2,1)S(1)}, bf16[512,256]{1,0:T(8,128)(2,1)S(1)}, u32[]{:S(2)}, u32[]{:S(2)}) %collective-permute-start.2) | collective-permute-done | bytes 262176 | tf_op jit(solution)/shard_map/ppermute | solution.py:387
  48.2 0.7 %bitcast_dynamic-update-slice_fusion = bf16[1,2,512,256]{3,2,1,0:T(8,128)(2,1)} fusion(bf16[1,2,512,256]{3,2,1,0:T(8,128)(2,1)} %bitcast.23, s32[]{:T(128)S(6)} %select_n.3, bf16[512,256]{1,0:T(8,128)(2,1)S(1)} %collective-permute-done.2), kind=kLoop, calls=%fused_computation | loop fusion | bytes 524292 | tf_op jit(solution)/shard_map/dynamic_update_slice | solution.py:388
  (1 shorter events, 0.0 us)
Async XLA Ops:
  0.0 9.3 %collective-permute-start.1 = (bf16[27,256,256]{2,1,0:T(8,128)(2,1)}, bf16[27,256,256]{2,1,0:T(8,128)(2,1)S(1)}, u32[]{:S(2)}, u32[]{:S(2)}) collective-permute-start(bf16[27,256,256]{2,1,0:T(8,128)(2,1)} %bitcast.14), channel_id=1, source_target_pairs={{0,16},{16,0},{1,17},{17,1},{2,18},{18,2},{3,19},{19,3},{4,20},{20... | collective-permute-start | bytes 10616840 | tf_op jit(solution)/shard_map/ppermute | solution.py:324
  2.5 6.0 %collective-permute-start = (bf16[72,256]{1,0:T(8,128)(2,1)}, bf16[72,256]{1,0:T(8,128)(2,1)S(1)}, u32[]{:S(2)}, u32[]{:S(2)}) collective-permute-start(bf16[72,256]{1,0:T(8,128)(2,1)} %get-tuple-element.19), channel_id=1, source_target_pairs={{0,8},{1,9},{2,10},{3,11},{4,12},{5,13},{6,14},{7,15},{8,0},{9,1},... | collective-permute-start | bytes 110600 | tf_op jit(solution)/shard_map/ppermute | solution.py:360
  9.3 4.9 %copy-start.3 = (bf16[27,256,256]{2,1,0:T(8,128)(2,1)}, bf16[27,256,256]{2,1,0:T(8,128)(2,1)S(1)}, u32[]{:S(2)}) copy-start(bf16[27,256,256]{2,1,0:T(8,128)(2,1)S(1)} %collective-permute-done.1.other_ref) | copy-start | bytes 10616836
  9.3 14.7 %all-to-all-start = ((bf16[8,144,256]{2,1,0:T(8,128)(2,1)}), bf16[8,144,256]{2,1,0:T(8,128)(2,1)}, u32[]{:S(2)}, u32[]{:S(2)}) async-start(bf16[8,144,256]{2,1,0:T(8,128)(2,1)} %bitcast.19), calls=%async_computation | async-start | bytes 1179648 | tf_op jit(solution)/shard_map/all_to_all | solution.py:353
  28.8 14.0 %all-to-all-start.1 = ((bf16[16,8,256]{2,1,0:T(8,128)(2,1)}), bf16[16,8,256]{2,1,0:T(8,128)(2,1)S(1)}, u32[]{:S(2)}, u32[]{:S(2)}) async-start(bf16[16,8,256]{2,1,0:T(8,128)(2,1)} %bitcast.20), calls=%async_computation.1 | async-start | bytes 131072 | tf_op jit(solution)/shard_map/all_to_all | solution.py:353
  35.0 7.9 %copy-start = (bf16[512,1792]{1,0:T(8,128)(2,1)S(1)}, bf16[512,1792]{1,0:T(8,128)(2,1)}, u32[]{:S(2)}) copy-start(bf16[512,1792]{1,0:T(8,128)(2,1)} %get-tuple-element.23.halo_onehot_ref) | copy-start | bytes 5505028
  35.0 7.9 %copy-start.1 = (bf16[512,256]{1,0:T(8,128)(2,1)S(1)}, bf16[512,256]{1,0:T(8,128)(2,1)}, u32[]{:S(2)}) copy-start(bf16[512,256]{1,0:T(8,128)(2,1)} %get-tuple-element.25.latent_ref) | copy-start | bytes 786436
  35.0 7.9 %copy-start.2 = (f32[2,256]{1,0:T(2,128)S(1)}, f32[2,256]{1,0:T(2,128)}, u32[]{:S(2)}) copy-start(f32[2,256]{1,0:T(2,128)} %bias_ref.3) | copy-start | bytes 6148
  46.6 1.6 %collective-permute-start.2 = (bf16[512,256]{1,0:T(8,128)(2,1)S(1)}, bf16[512,256]{1,0:T(8,128)(2,1)S(1)}, u32[]{:S(2)}, u32[]{:S(2)}) collective-permute-start(bf16[512,256]{1,0:T(8,128)(2,1)S(1)} %get-tuple-element.30), channel_id=1, source_target_pairs={{0,16},{16,0},{1,17},{17,1},{2,18},{18,2},{3,19},{19,3},{4,20},{20... | collective-permute-start | bytes 786440 | tf_op jit(solution)/shard_map/ppermute | solution.py:387

commit v7 on v6

--- a/solution.py
+++ b/solution.py
@@ -12,6 +12,7 @@
 I32 = jnp.int32
 TILE = 8
 BLOCK = 128
+CHUNK = 9
 VMEM_BYTES = 60 * 2**20
 DECODE_BYTES = 50 * 2**20
 PADDED_ROWS = 15 * 1024
@@ -55,6 +56,11 @@
         self.used += 1
         copy.start()
         return copy
+
+    def start_chunks(self, chosen, source, other, target, step):
+        count = target.shape[0]
+        spans = [pl.ds(first, min(step, count - first)) for first in range(0, count, step)]
+        return [self.start_either(chosen, (source.at[s], target.at[s]), (other.at[s], target.at[s])) for s in spans]
 
     def start_either(self, chosen, copy, other):
         sem = self.sems.at[self.used]
@@ -193,14 +199,17 @@
     return found
 
 
-def spread_halo(halo, held_ref, spread_ref):
+def spread_halo(halo, loads, held_ref, spread_ref):
     slots, channels = halo.shape
     offsets = held_ref.shape[0]
     whole = spread_ref.shape[0]
     if whole > offsets * slots:
         spread_ref[offsets * slots : whole, :] = jnp.zeros((whole - offsets * slots, channels), BF16)
-    for k in range(offsets):
-        spread_ref[k * slots : (k + 1) * slots, :] = dot(halo, held_ref[k]).astype(BF16)
+    step = -(-offsets // len(loads))
+    for at, load in enumerate(loads):
+        load.wait()
+        for k in range(at * step, min((at + 1) * step, offsets)):
+            spread_ref[k * slots : (k + 1) * slots, :] = dot(halo, held_ref[k]).astype(BF16)
 
 
 def halo_term(halo_onehot_v, span, spread_ref):
@@ -242,8 +251,7 @@
     found = pick_rows(places_v[:, 0:1], received_v)
     theirs = jnp.where(iota((send_v.shape[0], found.shape[1]), 1) == lax.axis_index("space"), found[slots:], 0.0)
     asked = lookup(jnp.sum(theirs, axis=1, keepdims=True).astype(I32), border_v[...])
-    weights_load.wait()
-    spread_halo(found[:slots].astype(BF16), held_ref, spread_ref)
+    spread_halo(found[:slots].astype(BF16), [weights_load], held_ref, spread_ref)
     for load in late:
         load.wait()
     term = halo_term(halo_onehot_v, pl.ds(0, block_ref.shape[0]), spread_ref)
@@ -285,7 +293,7 @@
     first = lax.axis_index("phase") == 0
     copies = Copies(sems)
     received_load = copies.start(received_ref, received_v)
-    weights_load = copies.start_either(first, (other_ref, held_ref), (own_ref, held_ref))
+    weights_loads = copies.start_chunks(first, other_ref, own_ref, held_ref, CHUNK)
     late = [
         copies.start(halo_onehot_ref, halo_onehot_v),
         copies.start(total_ref.at[pl.ds(0, total_v.shape[0])], total_v),
@@ -295,8 +303,7 @@
     received_load.wait()
     peer, slot = slot_numbers(received_v.shape[0] // TILE * cap, cap, cap)
     halo = pick_rows(peer * TILE + slot, received_v).astype(BF16)
-    weights_load.wait()
-    spread_halo(halo, held_ref, spread_ref)
+    spread_halo(halo, weights_loads, held_ref, spread_ref)
     for load in late:
         load.wait()
     stores = [copies.start_either(first, (latent_v, kept_ref.at[0]), (latent_v, passed_ref))]
@@ -343,7 +350,7 @@
             in_specs=[anywhere] * len(args),
             out_specs=[anywhere] * len(out_shapes),
             out_shape=out_shapes,
-            scratch_shapes=[pltpu.VMEM(s.shape, s.dtype) for s in scratch] + [pltpu.SemaphoreType.DMA((max(12, half + 4),))],
+            scratch_shapes=[pltpu.VMEM(s.shape, s.dtype) for s in scratch] + [pltpu.SemaphoreType.DMA((max(24, half + 4),))],
             compiler_params=pltpu.CompilerParams(vmem_limit_bytes=limit),
             cost_estimate=pl.CostEstimate(flops=flops, bytes_accessed=10**6, transcendentals=0),
             name=name,

time: 49.2 us -> 49.3 us (level)
  no operation moved by 1% of the time
where the time goes in v7:
time: 49.3 us; the launch traced here: 49 us
  Pallas kernels  26.6 us (54%)
  starting transfers between devices  15.3 us (31%)
  waiting for transfers between devices  5.45 us (11%)
  local copies, waits for them, and re-layouts  1.51 us (3%)
    pallas_call x5, Pallas kernels, call(): pl.pallas_call(kernel, in_specs=[anywhere] * len(args), out_specs=[anywhe...  26.6 us
    all_to_all x2, starting transfers between devices, exchange(): lax.all_to_all(value, 'space', 0, 0, tiled=True, axis_index_groups=groups)  11.1 us
    ppermute x1, starting transfers between devices, body(): lax.ppermute(shown, 'space', [(place, (place + half) % peers) for place i...  3.65 us
    ppermute x1, waiting for transfers between devices, body(): lax.ppermute(shown, 'space', [(place, (place + half) % peers) for place i...  2.36 us
    all_to_all x2, waiting for transfers between devices, exchange(): lax.all_to_all(value, 'space', 0, 0, tiled=True, axis_index_groups=groups)  1.57 us
    ppermute x1, waiting for transfers between devices, body(): got = lax.ppermute(passed, 'phase', swap)  1.52 us
  transfers between devices with their start and end apart: 5, of which 3 were waited for; matrix products, arithmetic and copies ran while one was open for 2% of the time, Pallas kernels for 37%

profile of v7, /device:TPU:0, one launch (start us, length us, event | category | flops | bytes accessed | tf_op | source)
XLA Modules:
  0.0 49.0 jit_solution(14291024603136832366)
XLA Ops:
  0.0 0.5 collective-permute-start.1
  0.5 2.2 %publish.1 = (bf16[72,256]{1,0:T(8,128)(2,1)}, bf16[8,2,72,256]{3,2,1,0:T(8,128)(2,1)}) custom-call(bf16[2,512,256]{2,1,0:T(8,128)(2,1)} %features_ref.5, s32[1,64]{1,0:T(1,128)} %border_ref.3, s32[4,16]{1,0:T(4,128)} %bitcast.21), custom_call_target="tpu_custom_call" | custom-call | flops 100000000 | bytes 1000000 | tf_op jit(solution)/shard_map/publish/pallas_call | solution.py:348
  2.6 3.7 %collective-permute-start = (bf16[72,256]{1,0:T(8,128)(2,1)}, bf16[72,256]{1,0:T(8,128)(2,1)S(1)}, u32[]{:S(2)}, u32[]{:S(2)}) collective-permute-start(bf16[72,256]{1,0:T(8,128)(2,1)} %get-tuple-element.19), channel_id=1, source_target_pairs={{0,8},{1,9},{2,10},{3,11},{4,12},{5,13},{6,14},{7,15},{8,0},{9,1},... | collective-permute-start | bytes 110600 | tf_op jit(solution)/shard_map/ppermute | solution.py:367
  6.3 2.4 %collective-permute-done = bf16[72,256]{1,0:T(8,128)(2,1)S(1)} collective-permute-done((bf16[72,256]{1,0:T(8,128)(2,1)}, bf16[72,256]{1,0:T(8,128)(2,1)S(1)}, u32[]{:S(2)}, u32[]{:S(2)}) %collective-permute-start) | collective-permute-done | bytes 36896 | tf_op jit(solution)/shard_map/ppermute | solution.py:367
  8.7 0.8 %broadcast_dynamic-update-slice_fusion = bf16[8,2,72,256]{3,2,1,0:T(8,128)(2,1)} fusion(bf16[8,2,72,256]{3,2,1,0:T(8,128)(2,1)} %get-tuple-element.18, bf16[72,256]{1,0:T(8,128)(2,1)S(1)} %collective-permute-done), kind=kLoop, calls=%fused_computation.1 | loop fusion | bytes 331776 | tf_op jit(solution)/shard_map/dynamic_update_slice | solution.py:368
  9.4 0.0 collective-permute-done.1.other_ref
  9.4 4.9 %all-to-all-start = ((bf16[8,144,256]{2,1,0:T(8,128)(2,1)}), bf16[8,144,256]{2,1,0:T(8,128)(2,1)}, u32[]{:S(2)}, u32[]{:S(2)}) async-start(bf16[8,144,256]{2,1,0:T(8,128)(2,1)} %bitcast.19), calls=%async_computation | async-start | bytes 1179648 | tf_op jit(solution)/shard_map/all_to_all | solution.py:360
  14.3 0.0 copy-done.3
  14.3 8.2 %first_local.1 = (f32[512,256]{1,0:T(8,128)}, bf16[512,1792]{1,0:T(8,128)(2,1)}, s32[192,128]{1,0:T(8,128)}, s32[512,128]{1,0:T(8,128)}) custom-call(bf16[2,512,256]{2,1,0:T(8,128)(2,1)} %features_ref.5, s32[27,512]{1,0:T(8,128)} %bitcast.24, s32[4,16]{1,0:T(4,128)} %bitcast.22, bf16[27,256,256]{2,1,0:T(8,128)(2,1)} %bitcast.15, bf16[27,256,256]{2,1,0:T(8,128)(2,1)} %copy-done.3), custom_call_target="tpu_custom_call" | custom-call | flops 5435817984 | bytes 1000000 | tf_op jit(solution)/shard_map/first_local/pallas_call | solution.py:348
  22.5 1.6 %all-to-all-done = bf16[8,144,256]{2,1,0:T(8,128)(2,1)} async-done(((bf16[8,144,256]{2,1,0:T(8,128)(2,1)}), bf16[8,144,256]{2,1,0:T(8,128)(2,1)}, u32[]{:S(2)}, u32[]{:S(2)}) %all-to-all-start) | async-done | bytes 589856 | tf_op jit(solution)/shard_map/all_to_all | solution.py:360
  24.1 4.9 %encode.1 = (bf16[512,256]{1,0:T(8,128)(2,1)}, bf16[512,256]{1,0:T(8,128)(2,1)}, bf16[128,256]{1,0:T(8,128)(2,1)}) custom-call(bf16[2,512,256]{2,1,0:T(8,128)(2,1)} %features_ref.5, f32[512,256]{1,0:T(8,128)} %get-tuple-element.21.total_ref, bf16[1152,256]{1,0:T(8,128)(2,1)} %bitcast.7.received_ref, bf16[512,1792]{1,0:T(8,128)(2,1)} %get-tuple-element.23.halo_onehot_ref, ...), custom_call_target="tpu_custom_call" | custom-call | flops 1000000000 | bytes 1000000 | tf_op jit(solution)/shard_map/encode/pallas_call | solution.py:348
  29.0 6.3 %all-to-all-start.1 = ((bf16[16,8,256]{2,1,0:T(8,128)(2,1)}), bf16[16,8,256]{2,1,0:T(8,128)(2,1)S(1)}, u32[]{:S(2)}, u32[]{:S(2)}) async-start(bf16[16,8,256]{2,1,0:T(8,128)(2,1)} %bitcast.20), calls=%async_computation.1 | async-start | bytes 131072 | tf_op jit(solution)/shard_map/all_to_all | solution.py:360
  35.3 0.0 copy-start
  35.3 0.0 copy-start.1
  35.3 0.0 copy-start.2
  35.3 7.9 %second_local.1.total_ref = f32[15360,256]{1,0:T(8,128)} custom-call(bf16[512,256]{1,0:T(8,128)(2,1)} %get-tuple-element.26.normed_ref, s32[512,128]{1,0:T(8,128)} %get-tuple-element.27.codes_ref, bf16[27,256,256]{2,1,0:T(8,128)(2,1)} %bitcast.17, bf16[27,256,256]{2,1,0:T(8,128)(2,1)} %copy-done.3), custom_call_target="tpu_custom_call" | custom-call | flops 5435817984 | bytes 1000000 | tf_op jit(solution)/shard_map/second_local/pallas_call | solution.py:348
  43.3 0.0 all-to-all-done.1
  43.3 0.0 copy-done
  43.3 0.0 copy-done.1
  43.3 0.0 copy-done.2
  43.3 3.3 %decode.1 = (bf16[2,512,256]{2,1,0:T(8,128)(2,1)}, bf16[512,256]{1,0:T(8,128)(2,1)S(1)}) custom-call(bf16[512,256]{1,0:T(8,128)(2,1)S(1)} %copy-done.1, f32[15360,256]{1,0:T(8,128)} %second_local.1.total_ref, bf16[128,256]{1,0:T(8,128)(2,1)S(1)} %bitcast.13, bf16[512,1792]{1,0:T(8,128)(2,1)S(1)} %copy-done, f32[2,256]{1,0:T(2,128)S(1)} %copy-done.2, ...), custom_call_target="tpu_custom_call" | custom-call | flops 1000000000 | bytes 1000000 | tf_op jit(solution)/shard_map/decode/pallas_call | solution.py:348
  46.7 0.1 collective-permute-start.2
  46.7 1.5 %collective-permute-done.2 = bf16[512,256]{1,0:T(8,128)(2,1)S(1)} collective-permute-done((bf16[512,256]{1,0:T(8,128)(2,1)S(1)}, bf16[512,256]{1,0:T(8,128)(2,1)S(1)}, u32[]{:S(2)}, u32[]{:S(2)}) %collective-permute-start.2) | collective-permute-done | bytes 262176 | tf_op jit(solution)/shard_map/ppermute | solution.py:394
  48.3 0.7 %bitcast_dynamic-update-slice_fusion = bf16[1,2,512,256]{3,2,1,0:T(8,128)(2,1)} fusion(bf16[1,2,512,256]{3,2,1,0:T(8,128)(2,1)} %bitcast.23, s32[]{:T(128)S(6)} %select_n.3, bf16[512,256]{1,0:T(8,128)(2,1)S(1)} %collective-permute-done.2), kind=kLoop, calls=%fused_computation | loop fusion | bytes 524292 | tf_op jit(solution)/shard_map/dynamic_update_slice | solution.py:395
  (1 shorter events, 0.0 us)
Async XLA Ops:
  0.0 9.4 %collective-permute-start.1 = (bf16[27,256,256]{2,1,0:T(8,128)(2,1)}, bf16[27,256,256]{2,1,0:T(8,128)(2,1)S(1)}, u32[]{:S(2)}, u32[]{:S(2)}) collective-permute-start(bf16[27,256,256]{2,1,0:T(8,128)(2,1)} %bitcast.14), channel_id=1, source_target_pairs={{0,16},{16,0},{1,17},{17,1},{2,18},{18,2},{3,19},{19,3},{4,20},{20... | collective-permute-start | bytes 10616840 | tf_op jit(solution)/shard_map/ppermute | solution.py:331
  2.6 6.0 %collective-permute-start = (bf16[72,256]{1,0:T(8,128)(2,1)}, bf16[72,256]{1,0:T(8,128)(2,1)S(1)}, u32[]{:S(2)}, u32[]{:S(2)}) collective-permute-start(bf16[72,256]{1,0:T(8,128)(2,1)} %get-tuple-element.19), channel_id=1, source_target_pairs={{0,8},{1,9},{2,10},{3,11},{4,12},{5,13},{6,14},{7,15},{8,0},{9,1},... | collective-permute-start | bytes 110600 | tf_op jit(solution)/shard_map/ppermute | solution.py:367
  9.4 4.9 %copy-start.3 = (bf16[27,256,256]{2,1,0:T(8,128)(2,1)}, bf16[27,256,256]{2,1,0:T(8,128)(2,1)S(1)}, u32[]{:S(2)}) copy-start(bf16[27,256,256]{2,1,0:T(8,128)(2,1)S(1)} %collective-permute-done.1.other_ref) | copy-start | bytes 10616836
  9.4 14.7 %all-to-all-start = ((bf16[8,144,256]{2,1,0:T(8,128)(2,1)}), bf16[8,144,256]{2,1,0:T(8,128)(2,1)}, u32[]{:S(2)}, u32[]{:S(2)}) async-start(bf16[8,144,256]{2,1,0:T(8,128)(2,1)} %bitcast.19), calls=%async_computation | async-start | bytes 1179648 | tf_op jit(solution)/shard_map/all_to_all | solution.py:360
  29.0 14.3 %all-to-all-start.1 = ((bf16[16,8,256]{2,1,0:T(8,128)(2,1)}), bf16[16,8,256]{2,1,0:T(8,128)(2,1)S(1)}, u32[]{:S(2)}, u32[]{:S(2)}) async-start(bf16[16,8,256]{2,1,0:T(8,128)(2,1)} %bitcast.20), calls=%async_computation.1 | async-start | bytes 131072 | tf_op jit(solution)/shard_map/all_to_all | solution.py:360
  35.3 8.0 %copy-start = (bf16[512,1792]{1,0:T(8,128)(2,1)S(1)}, bf16[512,1792]{1,0:T(8,128)(2,1)}, u32[]{:S(2)}) copy-start(bf16[512,1792]{1,0:T(8,128)(2,1)} %get-tuple-element.23.halo_onehot_ref) | copy-start | bytes 5505028
  35.3 8.0 %copy-start.1 = (bf16[512,256]{1,0:T(8,128)(2,1)S(1)}, bf16[512,256]{1,0:T(8,128)(2,1)}, u32[]{:S(2)}) copy-start(bf16[512,256]{1,0:T(8,128)(2,1)} %get-tuple-element.25.latent_ref) | copy-start | bytes 786436
  35.3 8.0 %copy-start.2 = (f32[2,256]{1,0:T(2,128)S(1)}, f32[2,256]{1,0:T(2,128)}, u32[]{:S(2)}) copy-start(f32[2,256]{1,0:T(2,128)} %bias_ref.3) | copy-start | bytes 6148
  46.7 1.6 %collective-permute-start.2 = (bf16[512,256]{1,0:T(8,128)(2,1)S(1)}, bf16[512,256]{1,0:T(8,128)(2,1)S(1)}, u32[]{:S(2)}, u32[]{:S(2)}) collective-permute-start(bf16[512,256]{1,0:T(8,128)(2,1)S(1)} %get-tuple-element.30), channel_id=1, source_target_pairs={{0,16},{16,0},{1,17},{17,1},{2,18},{18,2},{3,19},{19,3},{4,20},{20... | collective-permute-start | bytes 786440 | tf_op jit(solution)/shard_map/ppermute | solution.py:394

commit v8 on v6

--- a/solution.py
+++ b/solution.py
@@ -253,7 +253,10 @@
     normed = normalise(latent.astype(F32))
     normed_v[...] = normed
     stores.append(copies.start(normed_v, normed_ref))
-    send_v[...] = dot(onehot(asked, normed.shape[0]), normed).astype(BF16)
+    out = dot(onehot(asked, normed.shape[0]), normed)
+    width = send_v.shape[1]
+    part = lax.rem(iota((send_v.shape[0], 1), 0), TILE)
+    send_v[...] = jnp.where(part < TILE // 2, out[:, :width], out[:, width:]).astype(BF16)
     stores.append(copies.start(send_v, send_ref))
     for store in stores:
         store.wait()
@@ -294,7 +297,8 @@
     ]
     received_load.wait()
     peer, slot = slot_numbers(received_v.shape[0] // TILE * cap, cap, cap)
-    halo = pick_rows(peer * TILE + slot, received_v).astype(BF16)
+    halves = [pick_rows(peer * TILE + slot + cap * side, received_v).astype(BF16) for side in range(2)]
+    halo = jnp.concatenate(halves, axis=1)
     weights_load.wait()
     spread_halo(halo, held_ref, spread_ref)
     for load in late:
@@ -329,7 +333,7 @@
     total_like = array((rows, channels), F32)
     published_like = array((published, channels), BF16)
     shown_like = array((borders + TILE, channels), BF16)
-    sent_like = array((peers * TILE, channels), BF16)
+    sent_like = array((peers * TILE, channels // 2), BF16)
     onehot_like = array((rows, groups * pack * slots), BF16)
     places_like = array((slots + peers * TILE, 128), I32)
     columns_like = array((rows, -(-offsets // 128) * 128), I32)

time: 49.2 us -> 49.1 us (level)
  no operation moved by 1% of the time
where the time goes in v8:
time: 49.1 us; the launch traced here: 48.9 us
  Pallas kernels  26.5 us (54%)
  starting transfers between devices  15.2 us (31%)
  waiting for transfers between devices  5.57 us (11%)
  local copies, waits for them, and re-layouts  1.51 us (3%)
    pallas_call x5, Pallas kernels, call(): pl.pallas_call(kernel, in_specs=[anywhere] * len(args), out_specs=[anywhe...  26.5 us
    all_to_all x2, starting transfers between devices, exchange(): lax.all_to_all(value, 'space', 0, 0, tiled=True, axis_index_groups=groups)  11 us
    ppermute x1, starting transfers between devices, body(): lax.ppermute(shown, 'space', [(place, (place + half) % peers) for place i...  3.65 us
    ppermute x1, waiting for transfers between devices, body(): lax.ppermute(shown, 'space', [(place, (place + half) % peers) for place i...  2.36 us
    all_to_all x2, waiting for transfers between devices, exchange(): lax.all_to_all(value, 'space', 0, 0, tiled=True, axis_index_groups=groups)  1.69 us
    ppermute x1, waiting for transfers between devices, body(): got = lax.ppermute(passed, 'phase', swap)  1.52 us
  transfers between devices with their start and end apart: 5, of which 3 were waited for; matrix products, arithmetic and copies ran while one was open for 2% of the time, Pallas kernels for 37%

profile of v8, /device:TPU:0, one launch (start us, length us, event | category | flops | bytes accessed | tf_op | source)
XLA Modules:
  0.0 48.9 jit_solution(8554628343140188813)
XLA Ops:
  0.0 0.5 collective-permute-start.1
  0.5 2.1 %publish.1 = (bf16[72,256]{1,0:T(8,128)(2,1)}, bf16[8,2,72,256]{3,2,1,0:T(8,128)(2,1)}) custom-call(bf16[2,512,256]{2,1,0:T(8,128)(2,1)} %features_ref.5, s32[1,64]{1,0:T(1,128)} %border_ref.3, s32[4,16]{1,0:T(4,128)} %bitcast.21), custom_call_target="tpu_custom_call" | custom-call | flops 100000000 | bytes 1000000 | tf_op jit(solution)/shard_map/publish/pallas_call | solution.py:345
  2.5 3.7 %collective-permute-start = (bf16[72,256]{1,0:T(8,128)(2,1)}, bf16[72,256]{1,0:T(8,128)(2,1)S(1)}, u32[]{:S(2)}, u32[]{:S(2)}) collective-permute-start(bf16[72,256]{1,0:T(8,128)(2,1)} %get-tuple-element.19), channel_id=1, source_target_pairs={{0,8},{1,9},{2,10},{3,11},{4,12},{5,13},{6,14},{7,15},{8,0},{9,1},... | collective-permute-start | bytes 110600 | tf_op jit(solution)/shard_map/ppermute | solution.py:364
  6.2 2.4 %collective-permute-done = bf16[72,256]{1,0:T(8,128)(2,1)S(1)} collective-permute-done((bf16[72,256]{1,0:T(8,128)(2,1)}, bf16[72,256]{1,0:T(8,128)(2,1)S(1)}, u32[]{:S(2)}, u32[]{:S(2)}) %collective-permute-start) | collective-permute-done | bytes 36896 | tf_op jit(solution)/shard_map/ppermute | solution.py:364
  8.5 0.8 %broadcast_dynamic-update-slice_fusion = bf16[8,2,72,256]{3,2,1,0:T(8,128)(2,1)} fusion(bf16[8,2,72,256]{3,2,1,0:T(8,128)(2,1)} %get-tuple-element.18, bf16[72,256]{1,0:T(8,128)(2,1)S(1)} %collective-permute-done), kind=kLoop, calls=%fused_computation.1 | loop fusion | bytes 331776 | tf_op jit(solution)/shard_map/dynamic_update_slice | solution.py:365
  9.3 0.0 collective-permute-done.1.other_ref
  9.3 4.9 %all-to-all-start = ((bf16[8,144,256]{2,1,0:T(8,128)(2,1)}), bf16[8,144,256]{2,1,0:T(8,128)(2,1)}, u32[]{:S(2)}, u32[]{:S(2)}) async-start(bf16[8,144,256]{2,1,0:T(8,128)(2,1)} %bitcast.19), calls=%async_computation | async-start | bytes 1179648 | tf_op jit(solution)/shard_map/all_to_all | solution.py:357
  14.2 0.0 copy-done.3
  14.2 8.1 %first_local.1 = (f32[512,256]{1,0:T(8,128)}, bf16[512,1792]{1,0:T(8,128)(2,1)}, s32[192,128]{1,0:T(8,128)}, s32[512,128]{1,0:T(8,128)}) custom-call(bf16[2,512,256]{2,1,0:T(8,128)(2,1)} %features_ref.5, s32[27,512]{1,0:T(8,128)} %bitcast.24, s32[4,16]{1,0:T(4,128)} %bitcast.22, bf16[27,256,256]{2,1,0:T(8,128)(2,1)} %bitcast.15, bf16[27,256,256]{2,1,0:T(8,128)(2,1)} %copy-done.3), custom_call_target="tpu_custom_call" | custom-call | flops 5435817984 | bytes 1000000 | tf_op jit(solution)/shard_map/first_local/pallas_call | solution.py:345
  22.3 1.7 %all-to-all-done = bf16[8,144,256]{2,1,0:T(8,128)(2,1)} async-done(((bf16[8,144,256]{2,1,0:T(8,128)(2,1)}), bf16[8,144,256]{2,1,0:T(8,128)(2,1)}, u32[]{:S(2)}, u32[]{:S(2)}) %all-to-all-start) | async-done | bytes 589856 | tf_op jit(solution)/shard_map/all_to_all | solution.py:357
  24.0 4.8 %encode.1 = (bf16[512,256]{1,0:T(8,128)(2,1)}, bf16[512,256]{1,0:T(8,128)(2,1)}, bf16[128,128]{1,0:T(8,128)(2,1)}) custom-call(bf16[2,512,256]{2,1,0:T(8,128)(2,1)} %features_ref.5, f32[512,256]{1,0:T(8,128)} %get-tuple-element.21.total_ref, bf16[1152,256]{1,0:T(8,128)(2,1)} %bitcast.7.received_ref, bf16[512,1792]{1,0:T(8,128)(2,1)} %get-tuple-element.23.halo_onehot_ref, ...), custom_call_target="tpu_custom_call" | custom-call | flops 1000000000 | bytes 1000000 | tf_op jit(solution)/shard_map/encode/pallas_call | solution.py:345
  28.8 6.2 %all-to-all-start.1 = ((bf16[16,8,128]{2,1,0:T(8,128)(2,1)}), bf16[16,8,128]{2,1,0:T(8,128)(2,1)S(1)}, u32[]{:S(2)}, u32[]{:S(2)}) async-start(bf16[16,8,128]{2,1,0:T(8,128)(2,1)} %bitcast.20), calls=%async_computation.1 | async-start | bytes 65536 | tf_op jit(solution)/shard_map/all_to_all | solution.py:357
  35.0 0.0 copy-start
  35.0 0.0 copy-start.1
  35.0 0.0 copy-start.2
  35.0 7.8 %second_local.1.total_ref = f32[15360,256]{1,0:T(8,128)} custom-call(bf16[512,256]{1,0:T(8,128)(2,1)} %get-tuple-element.26.normed_ref, s32[512,128]{1,0:T(8,128)} %get-tuple-element.27.codes_ref, bf16[27,256,256]{2,1,0:T(8,128)(2,1)} %bitcast.17, bf16[27,256,256]{2,1,0:T(8,128)(2,1)} %copy-done.3), custom_call_target="tpu_custom_call" | custom-call | flops 5435817984 | bytes 1000000 | tf_op jit(solution)/shard_map/second_local/pallas_call | solution.py:345
  42.8 0.0 all-to-all-done.1
  42.8 0.0 copy-done
  42.9 0.0 copy-done.1
  42.9 0.0 copy-done.2
  42.9 3.7 %decode.1 = (bf16[2,512,256]{2,1,0:T(8,128)(2,1)}, bf16[512,256]{1,0:T(8,128)(2,1)S(1)}) custom-call(bf16[512,256]{1,0:T(8,128)(2,1)S(1)} %copy-done.1, f32[15360,256]{1,0:T(8,128)} %second_local.1.total_ref, bf16[128,128]{1,0:T(8,128)(2,1)S(1)} %bitcast.13, bf16[512,1792]{1,0:T(8,128)(2,1)S(1)} %copy-done, f32[2,256]{1,0:T(2,128)S(1)} %copy-done.2, ...), custom_call_target="tpu_custom_call" | custom-call | flops 1000000000 | bytes 1000000 | tf_op jit(solution)/shard_map/decode/pallas_call | solution.py:345
  46.5 0.1 collective-permute-start.2
  46.6 1.5 %collective-permute-done.2 = bf16[512,256]{1,0:T(8,128)(2,1)S(1)} collective-permute-done((bf16[512,256]{1,0:T(8,128)(2,1)S(1)}, bf16[512,256]{1,0:T(8,128)(2,1)S(1)}, u32[]{:S(2)}, u32[]{:S(2)}) %collective-permute-start.2) | collective-permute-done | bytes 262176 | tf_op jit(solution)/shard_map/ppermute | solution.py:391
  48.2 0.7 %bitcast_dynamic-update-slice_fusion = bf16[1,2,512,256]{3,2,1,0:T(8,128)(2,1)} fusion(bf16[1,2,512,256]{3,2,1,0:T(8,128)(2,1)} %bitcast.23, s32[]{:T(128)S(6)} %select_n.3, bf16[512,256]{1,0:T(8,128)(2,1)S(1)} %collective-permute-done.2), kind=kLoop, calls=%fused_computation | loop fusion | bytes 524292 | tf_op jit(solution)/shard_map/dynamic_update_slice | solution.py:392
  (1 shorter events, 0.0 us)
Async XLA Ops:
  0.0 9.3 %collective-permute-start.1 = (bf16[27,256,256]{2,1,0:T(8,128)(2,1)}, bf16[27,256,256]{2,1,0:T(8,128)(2,1)S(1)}, u32[]{:S(2)}, u32[]{:S(2)}) collective-permute-start(bf16[27,256,256]{2,1,0:T(8,128)(2,1)} %bitcast.14), channel_id=1, source_target_pairs={{0,16},{16,0},{1,17},{17,1},{2,18},{18,2},{3,19},{19,3},{4,20},{20... | collective-permute-start | bytes 10616840 | tf_op jit(solution)/shard_map/ppermute | solution.py:328
  2.5 6.0 %collective-permute-start = (bf16[72,256]{1,0:T(8,128)(2,1)}, bf16[72,256]{1,0:T(8,128)(2,1)S(1)}, u32[]{:S(2)}, u32[]{:S(2)}) collective-permute-start(bf16[72,256]{1,0:T(8,128)(2,1)} %get-tuple-element.19), channel_id=1, source_target_pairs={{0,8},{1,9},{2,10},{3,11},{4,12},{5,13},{6,14},{7,15},{8,0},{9,1},... | collective-permute-start | bytes 110600 | tf_op jit(solution)/shard_map/ppermute | solution.py:364
  9.3 4.9 %copy-start.3 = (bf16[27,256,256]{2,1,0:T(8,128)(2,1)}, bf16[27,256,256]{2,1,0:T(8,128)(2,1)S(1)}, u32[]{:S(2)}) copy-start(bf16[27,256,256]{2,1,0:T(8,128)(2,1)S(1)} %collective-permute-done.1.other_ref) | copy-start | bytes 10616836
  9.3 14.7 %all-to-all-start = ((bf16[8,144,256]{2,1,0:T(8,128)(2,1)}), bf16[8,144,256]{2,1,0:T(8,128)(2,1)}, u32[]{:S(2)}, u32[]{:S(2)}) async-start(bf16[8,144,256]{2,1,0:T(8,128)(2,1)} %bitcast.19), calls=%async_computation | async-start | bytes 1179648 | tf_op jit(solution)/shard_map/all_to_all | solution.py:357
  28.8 14.0 %all-to-all-start.1 = ((bf16[16,8,128]{2,1,0:T(8,128)(2,1)}), bf16[16,8,128]{2,1,0:T(8,128)(2,1)S(1)}, u32[]{:S(2)}, u32[]{:S(2)}) async-start(bf16[16,8,128]{2,1,0:T(8,128)(2,1)} %bitcast.20), calls=%async_computation.1 | async-start | bytes 65536 | tf_op jit(solution)/shard_map/all_to_all | solution.py:357
  35.0 7.9 %copy-start = (bf16[512,1792]{1,0:T(8,128)(2,1)S(1)}, bf16[512,1792]{1,0:T(8,128)(2,1)}, u32[]{:S(2)}) copy-start(bf16[512,1792]{1,0:T(8,128)(2,1)} %get-tuple-element.23.halo_onehot_ref) | copy-start | bytes 5505028
  35.0 7.9 %copy-start.1 = (bf16[512,256]{1,0:T(8,128)(2,1)S(1)}, bf16[512,256]{1,0:T(8,128)(2,1)}, u32[]{:S(2)}) copy-start(bf16[512,256]{1,0:T(8,128)(2,1)} %get-tuple-element.25.latent_ref) | copy-start | bytes 786436
  35.0 7.9 %copy-start.2 = (f32[2,256]{1,0:T(2,128)S(1)}, f32[2,256]{1,0:T(2,128)}, u32[]{:S(2)}) copy-start(f32[2,256]{1,0:T(2,128)} %bias_ref.3) | copy-start | bytes 6148
  46.5 1.6 %collective-permute-start.2 = (bf16[512,256]{1,0:T(8,128)(2,1)S(1)}, bf16[512,256]{1,0:T(8,128)(2,1)S(1)}, u32[]{:S(2)}, u32[]{:S(2)}) collective-permute-start(bf16[512,256]{1,0:T(8,128)(2,1)S(1)} %get-tuple-element.30), channel_id=1, source_target_pairs={{0,16},{16,0},{1,17},{17,1},{2,18},{18,2},{3,19},{19,3},{4,20},{20... | collective-permute-start | bytes 786440 | tf_op jit(solution)/shard_map/ppermute | solution.py:391

commit v9 on v8

--- a/solution.py
+++ b/solution.py
@@ -249,15 +249,17 @@
     term = halo_term(halo_onehot_v, pl.ds(0, block_ref.shape[0]), spread_ref)
     latent = residual(block_ref[...].astype(F32), total_v[...] + term + bias_v[0:1, :])
     latent_v[...] = latent
-    stores = [copies.start(latent_v, latent_ref)]
     normed = normalise(latent.astype(F32))
     normed_v[...] = normed
-    stores.append(copies.start(normed_v, normed_ref))
     out = dot(onehot(asked, normed.shape[0]), normed)
     width = send_v.shape[1]
     part = lax.rem(iota((send_v.shape[0], 1), 0), TILE)
     send_v[...] = jnp.where(part < TILE // 2, out[:, :width], out[:, width:]).astype(BF16)
-    stores.append(copies.start(send_v, send_ref))
+    stores = [
+        copies.start(send_v, send_ref),
+        copies.start(normed_v, normed_ref),
+        copies.start(latent_v, latent_ref),
+    ]
     for store in stores:
         store.wait()
 

time: 49.1 us -> 49.4 us (level)
  no operation moved by 1% of the time
where the time goes in v9:
time: 49.4 us; the launch traced here: 49.1 us
  Pallas kernels  26.7 us (54%)
  starting transfers between devices  15.2 us (31%)
  waiting for transfers between devices  5.57 us (11%)
  local copies, waits for them, and re-layouts  1.51 us (3%)
    pallas_call x5, Pallas kernels, call(): pl.pallas_call(kernel, in_specs=[anywhere] * len(args), out_specs=[anywhe...  26.7 us
    all_to_all x2, starting transfers between devices, exchange(): lax.all_to_all(value, 'space', 0, 0, tiled=True, axis_index_groups=groups)  11 us
    ppermute x1, starting transfers between devices, body(): lax.ppermute(shown, 'space', [(place, (place + half) % peers) for place i...  3.65 us
    ppermute x1, waiting for transfers between devices, body(): lax.ppermute(shown, 'space', [(place, (place + half) % peers) for place i...  2.36 us
    all_to_all x2, waiting for transfers between devices, exchange(): lax.all_to_all(value, 'space', 0, 0, tiled=True, axis_index_groups=groups)  1.69 us
    ppermute x1, waiting for transfers between devices, body(): got = lax.ppermute(passed, 'phase', swap)  1.52 us
  transfers between devices with their start and end apart: 5, of which 3 were waited for; matrix products, arithmetic and copies ran while one was open for 2% of the time, Pallas kernels for 37%

profile of v9, /device:TPU:0, one launch (start us, length us, event | category | flops | bytes accessed | tf_op | source)
XLA Modules:
  0.0 49.1 jit_solution(15150427510489570899)
XLA Ops:
  0.0 0.5 collective-permute-start.1
  0.5 2.1 %publish.1 = (bf16[72,256]{1,0:T(8,128)(2,1)}, bf16[8,2,72,256]{3,2,1,0:T(8,128)(2,1)}) custom-call(bf16[2,512,256]{2,1,0:T(8,128)(2,1)} %features_ref.5, s32[1,64]{1,0:T(1,128)} %border_ref.3, s32[4,16]{1,0:T(4,128)} %bitcast.21), custom_call_target="tpu_custom_call" | custom-call | flops 100000000 | bytes 1000000 | tf_op jit(solution)/shard_map/publish/pallas_call | solution.py:347
  2.5 3.7 %collective-permute-start = (bf16[72,256]{1,0:T(8,128)(2,1)}, bf16[72,256]{1,0:T(8,128)(2,1)S(1)}, u32[]{:S(2)}, u32[]{:S(2)}) collective-permute-start(bf16[72,256]{1,0:T(8,128)(2,1)} %get-tuple-element.19), channel_id=1, source_target_pairs={{0,8},{1,9},{2,10},{3,11},{4,12},{5,13},{6,14},{7,15},{8,0},{9,1},... | collective-permute-start | bytes 110600 | tf_op jit(solution)/shard_map/ppermute | solution.py:366
  6.2 2.4 %collective-permute-done = bf16[72,256]{1,0:T(8,128)(2,1)S(1)} collective-permute-done((bf16[72,256]{1,0:T(8,128)(2,1)}, bf16[72,256]{1,0:T(8,128)(2,1)S(1)}, u32[]{:S(2)}, u32[]{:S(2)}) %collective-permute-start) | collective-permute-done | bytes 36896 | tf_op jit(solution)/shard_map/ppermute | solution.py:366
  8.5 0.8 %broadcast_dynamic-update-slice_fusion = bf16[8,2,72,256]{3,2,1,0:T(8,128)(2,1)} fusion(bf16[8,2,72,256]{3,2,1,0:T(8,128)(2,1)} %get-tuple-element.18, bf16[72,256]{1,0:T(8,128)(2,1)S(1)} %collective-permute-done), kind=kLoop, calls=%fused_computation.1 | loop fusion | bytes 331776 | tf_op jit(solution)/shard_map/dynamic_update_slice | solution.py:367
  9.3 0.0 collective-permute-done.1.other_ref
  9.3 4.9 %all-to-all-start = ((bf16[8,144,256]{2,1,0:T(8,128)(2,1)}), bf16[8,144,256]{2,1,0:T(8,128)(2,1)}, u32[]{:S(2)}, u32[]{:S(2)}) async-start(bf16[8,144,256]{2,1,0:T(8,128)(2,1)} %bitcast.19), calls=%async_computation | async-start | bytes 1179648 | tf_op jit(solution)/shard_map/all_to_all | solution.py:359
  14.2 0.0 copy-done.3
  14.2 8.1 %first_local.1 = (f32[512,256]{1,0:T(8,128)}, bf16[512,1792]{1,0:T(8,128)(2,1)}, s32[192,128]{1,0:T(8,128)}, s32[512,128]{1,0:T(8,128)}) custom-call(bf16[2,512,256]{2,1,0:T(8,128)(2,1)} %features_ref.5, s32[27,512]{1,0:T(8,128)} %bitcast.24, s32[4,16]{1,0:T(4,128)} %bitcast.22, bf16[27,256,256]{2,1,0:T(8,128)(2,1)} %bitcast.15, bf16[27,256,256]{2,1,0:T(8,128)(2,1)} %copy-done.3), custom_call_target="tpu_custom_call" | custom-call | flops 5435817984 | bytes 1000000 | tf_op jit(solution)/shard_map/first_local/pallas_call | solution.py:347
  22.3 1.7 %all-to-all-done = bf16[8,144,256]{2,1,0:T(8,128)(2,1)} async-done(((bf16[8,144,256]{2,1,0:T(8,128)(2,1)}), bf16[8,144,256]{2,1,0:T(8,128)(2,1)}, u32[]{:S(2)}, u32[]{:S(2)}) %all-to-all-start) | async-done | bytes 589856 | tf_op jit(solution)/shard_map/all_to_all | solution.py:359
  24.0 5.0 %encode.1 = (bf16[512,256]{1,0:T(8,128)(2,1)}, bf16[512,256]{1,0:T(8,128)(2,1)}, bf16[128,128]{1,0:T(8,128)(2,1)}) custom-call(bf16[2,512,256]{2,1,0:T(8,128)(2,1)} %features_ref.5, f32[512,256]{1,0:T(8,128)} %get-tuple-element.21.total_ref, bf16[1152,256]{1,0:T(8,128)(2,1)} %bitcast.7.received_ref, bf16[512,1792]{1,0:T(8,128)(2,1)} %get-tuple-element.23.halo_onehot_ref, ...), custom_call_target="tpu_custom_call" | custom-call | flops 1000000000 | bytes 1000000 | tf_op jit(solution)/shard_map/encode/pallas_call | solution.py:347
  29.0 6.2 %all-to-all-start.1 = ((bf16[16,8,128]{2,1,0:T(8,128)(2,1)}), bf16[16,8,128]{2,1,0:T(8,128)(2,1)S(1)}, u32[]{:S(2)}, u32[]{:S(2)}) async-start(bf16[16,8,128]{2,1,0:T(8,128)(2,1)} %bitcast.20), calls=%async_computation.1 | async-start | bytes 65536 | tf_op jit(solution)/shard_map/all_to_all | solution.py:359
  35.2 0.0 copy-start
  35.2 0.0 copy-start.1
  35.2 0.0 copy-start.2
  35.2 7.8 %second_local.1.total_ref = f32[15360,256]{1,0:T(8,128)} custom-call(bf16[512,256]{1,0:T(8,128)(2,1)} %get-tuple-element.26.normed_ref, s32[512,128]{1,0:T(8,128)} %get-tuple-element.27.codes_ref, bf16[27,256,256]{2,1,0:T(8,128)(2,1)} %bitcast.17, bf16[27,256,256]{2,1,0:T(8,128)(2,1)} %copy-done.3), custom_call_target="tpu_custom_call" | custom-call | flops 5435817984 | bytes 1000000 | tf_op jit(solution)/shard_map/second_local/pallas_call | solution.py:347
  43.0 0.0 all-to-all-done.1
  43.0 0.0 copy-done
  43.1 0.0 copy-done.1
  43.1 0.0 copy-done.2
  43.1 3.7 %decode.1 = (bf16[2,512,256]{2,1,0:T(8,128)(2,1)}, bf16[512,256]{1,0:T(8,128)(2,1)S(1)}) custom-call(bf16[512,256]{1,0:T(8,128)(2,1)S(1)} %copy-done.1, f32[15360,256]{1,0:T(8,128)} %second_local.1.total_ref, bf16[128,128]{1,0:T(8,128)(2,1)S(1)} %bitcast.13, bf16[512,1792]{1,0:T(8,128)(2,1)S(1)} %copy-done, f32[2,256]{1,0:T(2,128)S(1)} %copy-done.2, ...), custom_call_target="tpu_custom_call" | custom-call | flops 1000000000 | bytes 1000000 | tf_op jit(solution)/shard_map/decode/pallas_call | solution.py:347
  46.8 0.1 collective-permute-start.2
  46.8 1.5 %collective-permute-done.2 = bf16[512,256]{1,0:T(8,128)(2,1)S(1)} collective-permute-done((bf16[512,256]{1,0:T(8,128)(2,1)S(1)}, bf16[512,256]{1,0:T(8,128)(2,1)S(1)}, u32[]{:S(2)}, u32[]{:S(2)}) %collective-permute-start.2) | collective-permute-done | bytes 262176 | tf_op jit(solution)/shard_map/ppermute | solution.py:393
  48.4 0.7 %bitcast_dynamic-update-slice_fusion = bf16[1,2,512,256]{3,2,1,0:T(8,128)(2,1)} fusion(bf16[1,2,512,256]{3,2,1,0:T(8,128)(2,1)} %bitcast.23, s32[]{:T(128)S(6)} %select_n.3, bf16[512,256]{1,0:T(8,128)(2,1)S(1)} %collective-permute-done.2), kind=kLoop, calls=%fused_computation | loop fusion | bytes 524292 | tf_op jit(solution)/shard_map/dynamic_update_slice | solution.py:394
  (1 shorter events, 0.0 us)
Async XLA Ops:
  0.0 9.3 %collective-permute-start.1 = (bf16[27,256,256]{2,1,0:T(8,128)(2,1)}, bf16[27,256,256]{2,1,0:T(8,128)(2,1)S(1)}, u32[]{:S(2)}, u32[]{:S(2)}) collective-permute-start(bf16[27,256,256]{2,1,0:T(8,128)(2,1)} %bitcast.14), channel_id=1, source_target_pairs={{0,16},{16,0},{1,17},{17,1},{2,18},{18,2},{3,19},{19,3},{4,20},{20... | collective-permute-start | bytes 10616840 | tf_op jit(solution)/shard_map/ppermute | solution.py:330
  2.5 6.0 %collective-permute-start = (bf16[72,256]{1,0:T(8,128)(2,1)}, bf16[72,256]{1,0:T(8,128)(2,1)S(1)}, u32[]{:S(2)}, u32[]{:S(2)}) collective-permute-start(bf16[72,256]{1,0:T(8,128)(2,1)} %get-tuple-element.19), channel_id=1, source_target_pairs={{0,8},{1,9},{2,10},{3,11},{4,12},{5,13},{6,14},{7,15},{8,0},{9,1},... | collective-permute-start | bytes 110600 | tf_op jit(solution)/shard_map/ppermute | solution.py:366
  9.3 4.9 %copy-start.3 = (bf16[27,256,256]{2,1,0:T(8,128)(2,1)}, bf16[27,256,256]{2,1,0:T(8,128)(2,1)S(1)}, u32[]{:S(2)}) copy-start(bf16[27,256,256]{2,1,0:T(8,128)(2,1)S(1)} %collective-permute-done.1.other_ref) | copy-start | bytes 10616836
  9.3 14.7 %all-to-all-start = ((bf16[8,144,256]{2,1,0:T(8,128)(2,1)}), bf16[8,144,256]{2,1,0:T(8,128)(2,1)}, u32[]{:S(2)}, u32[]{:S(2)}) async-start(bf16[8,144,256]{2,1,0:T(8,128)(2,1)} %bitcast.19), calls=%async_computation | async-start | bytes 1179648 | tf_op jit(solution)/shard_map/all_to_all | solution.py:359
  29.0 14.0 %all-to-all-start.1 = ((bf16[16,8,128]{2,1,0:T(8,128)(2,1)}), bf16[16,8,128]{2,1,0:T(8,128)(2,1)S(1)}, u32[]{:S(2)}, u32[]{:S(2)}) async-start(bf16[16,8,128]{2,1,0:T(8,128)(2,1)} %bitcast.20), calls=%async_computation.1 | async-start | bytes 65536 | tf_op jit(solution)/shard_map/all_to_all | solution.py:359
  35.2 7.9 %copy-start = (bf16[512,1792]{1,0:T(8,128)(2,1)S(1)}, bf16[512,1792]{1,0:T(8,128)(2,1)}, u32[]{:S(2)}) copy-start(bf16[512,1792]{1,0:T(8,128)(2,1)} %get-tuple-element.23.halo_onehot_ref) | copy-start | bytes 5505028
  35.2 7.9 %copy-start.1 = (bf16[512,256]{1,0:T(8,128)(2,1)S(1)}, bf16[512,256]{1,0:T(8,128)(2,1)}, u32[]{:S(2)}) copy-start(bf16[512,256]{1,0:T(8,128)(2,1)} %get-tuple-element.25.latent_ref) | copy-start | bytes 786436
  35.2 7.9 %copy-start.2 = (f32[2,256]{1,0:T(2,128)S(1)}, f32[2,256]{1,0:T(2,128)}, u32[]{:S(2)}) copy-start(f32[2,256]{1,0:T(2,128)} %bias_ref.3) | copy-start | bytes 6148
  46.8 1.6 %collective-permute-start.2 = (bf16[512,256]{1,0:T(8,128)(2,1)S(1)}, bf16[512,256]{1,0:T(8,128)(2,1)S(1)}, u32[]{:S(2)}, u32[]{:S(2)}) collective-permute-start(bf16[512,256]{1,0:T(8,128)(2,1)S(1)} %get-tuple-element.30), channel_id=1, source_target_pairs={{0,16},{16,0},{1,17},{17,1},{2,18},{18,2},{3,19},{19,3},{4,20},{20... | collective-permute-start | bytes 786440 | tf_op jit(solution)/shard_map/ppermute | solution.py:393
